TPU v7x, 256 devices: a whole 4x4x8 slice. The times are simulated.
256 devices in a mesh: dp: 32 (over z, x_lo, core), fsdp: 8 (over y, x_hi).
Axes of the slice: x: 4 (x_hi: 2, x_lo: 2; x = x_hi * 2 + x_lo), y: 4, z: 8, core: 2. Of those that a mesh axis runs over, the one named last changes fastest.
Arguments:
- inputs: bfloat16 [1024, 256, 512], P(('dp', 'fsdp')), may hold values from -0.25 to 0.25
- out_grad: bfloat16 [1024, 256, 512], P(('dp', 'fsdp')), may hold values from -6 to 6
- coeff_fixed: int32 [1024, 16], P(('dp', 'fsdp')), may hold values from 0 to 4096
- atom_counts: int32 [1024], P(('dp', 'fsdp')), may hold values from 64 to 256, as said below
- experts: bfloat16 [16, 512, 512], P(None, ('dp', 'fsdp')), may hold values from -0.125 to 0.125
Outputs:
- in_grad: bfloat16 [1024, 256, 512], P(('dp', 'fsdp'))
- expert_grad: float32 [16, 512, 512], P(None, ('dp', 'fsdp'))
Inputs may be any that keep to these rules, and one draw needn't show every extreme that they name: `atom_counts`: some system has exactly 256 atoms and some exactly 64.
All inputs are finite; a program needn't handle non-finite values.
Results may differ from a plain program's by a relative error of at most 0.0049.
Values may be sent and summed in bfloat16 or wider, within the bound.
No kernel may reach another device: no remote copies, remote signals or barrier semaphores. Data moves between devices by JAX's collectives and lax.ppermute only.
A program may use at most 128 MiB of HBM per device.

v0:
```python
import jax
import jax.numpy as jnp
from jax import lax
from jax.sharding import PartitionSpec as P

HIGH = lax.Precision.HIGHEST


def shards(inputs, out_grad, coeff_fixed, atom_counts, experts):
    n_sys, n_slots, width = inputs.shape
    n_exp = experts.shape[0]
    coeffs = coeff_fixed.astype(jnp.float32) / 4096.0
    valid = lax.broadcasted_iota(jnp.int32, (n_sys, n_slots), 1) < atom_counts[:, None]
    masked = jnp.where(valid[:, :, None], out_grad, jnp.zeros_like(out_grad))
    whole = lax.all_gather(experts, ("dp", "fsdp"), axis=1, tiled=True)
    flat = whole.reshape(n_exp, width * width).astype(jnp.float32)
    merged = jnp.dot(coeffs, flat, precision=HIGH).reshape(n_sys, width, width)
    merged_low = merged.astype(jnp.bfloat16)
    per_system = jnp.einsum("smi,smj->sij", inputs, masked, preferred_element_type=jnp.float32)
    term = jnp.einsum("se,sij->eij", coeffs, per_system, precision=HIGH)
    expert_grad = lax.psum_scatter(term, ("dp", "fsdp"), scatter_dimension=1, tiled=True)
    in_grad = jnp.einsum(
        "smj,sij->smi", masked, merged_low, preferred_element_type=jnp.float32
    ).astype(jnp.bfloat16)
    return (in_grad, expert_grad)


def solution(mesh):
    placed = (
        P(("dp", "fsdp"), None, None),
        P(("dp", "fsdp"), None, None),
        P(("dp", "fsdp"), None),
        P(("dp", "fsdp")),
        P(None, ("dp", "fsdp"), None),
    )
    return jax.shard_map(
        shards,
        mesh=mesh,
        in_specs=placed,
        out_specs=(P(("dp", "fsdp"), None, None), P(None, ("dp", "fsdp"), None)),
        check_vma=False,
    )
```

profile of v0, /device:TPU:9, one launch (start us, length us, event | category | flops | bytes accessed | tf_op | source)
XLA Modules:
  0.0 2026.1 jit_solution(14154587248023291205)
XLA Ops:
  7.2 0.0 copy-start
  7.2 0.0 all-gather.2.cloned.1.call-start
  7.2 1.5 copy.16
  8.7 0.0 all-gather.2.cloned.1.call-update
  8.7 0.0 reduce-scatter.2.cloned.1.call-start
  8.8 0.7 iota_compare_fusion
  9.5 0.0 copy-done
  9.5 4.1 convolution_bitcast_fusion
  13.6 0.0 copy-start.2
  13.6 5.5 copy.21
  19.1 0.0 copy-done.2
  19.1 17.5 fusion.13
  36.6 0.0 reduce-scatter.2.cloned.1.call-update
  36.6 0.0 copy-start.1
  36.6 665.0 %all-gather.2.cloned.1.call-done = bf16[16,512,512]{2,0,1:T(8,128)(2,1)} async-done(((bf16[16,2,512]{2,0,1:T(8,128)(2,1)}), bf16[16,512,512]{2,0,1:T(8,128)(2,1)}) %all-gather.2.cloned.1.call-update) | async-done | bytes 8388624 | tf_op jit(solution)/shard_map/all_gather | solution.py:15
  701.6 5.9 fusion.5
  707.5 0.0 copy-done.1
  707.5 2.0 fusion.8
  709.5 1308.3 %reduce-scatter.2.cloned.1.call-done = f32[16,2,512]{2,0,1:T(8,128)} async-done(((f32[16,512,512]{2,0,1:T(8,128)}), f32[16,2,512]{2,0,1:T(8,128)}) %reduce-scatter.2.cloned.1.call-update) | async-done | bytes 65552 | tf_op jit(solution)/shard_map/reduce_scatter | solution.py:21
  2017.7 1.5 copy.22
Async XLA Ops:
  7.2 2.3 copy-start
  7.2 694.4 %all-gather.2.cloned.1.call-start = ((), (), s32[]{:S(2)}) async-start(), calls=%async_computation.1 | async-start | bytes 8421376 | tf_op jit(solution)/shard_map/all_gather | solution.py:15
  8.7 2009.0 %reduce-scatter.2.cloned.1.call-start = ((), (), s32[]{:S(2)}) async-start(), calls=%async_computation.2 | async-start | bytes 16842752 | tf_op jit(solution)/shard_map/reduce_scatter | solution.py:21
  13.6 5.5 copy-start.2
  36.6 670.9 %copy-start.1 = (bf16[4,256,512]{2,1,0:T(8,128)(2,1)S(1)}, bf16[4,256,512]{2,1,0:T(8,128)(2,1)}, u32[]{:S(2)}) copy-start(bf16[4,256,512]{2,1,0:T(8,128)(2,1)} %param.6) | copy-start | bytes 3145732
Sparse Core Ops, SparseCore 0:
  10.5 691.1 all-gather.1
  704.1 1313.5 reduce-scatter.1
where the time goes:
time: 2040 us; the launch traced here: 2030 us
  waiting for transfers between devices  1970 us (97%)
  matrix products  29.5 us (1%)
    reduce_scatter x1, waiting for transfers between devices, shards(): lax.psum_scatter(term, ('dp', 'fsdp'), scatter_dimension=1, tiled=True)  1310 us
    all_gather x1, waiting for transfers between devices, shards(): whole = lax.all_gather(experts, ('dp', 'fsdp'), axis=1, tiled=True)  665 us
  transfers between devices with their start and end apart: 2, of which 2 were waited for; matrix products, arithmetic and copies ran while one was open for 2% of the time, Pallas kernels for 0%

commit v1 on v0

v1 whole, which is shorter than its diff:
```python
import jax
import jax.numpy as jnp
from jax import lax
from jax.experimental import pallas as pl
from jax.experimental.pallas import tpu as pltpu
from jax.sharding import Mesh, PartitionSpec as P

AXES = (("z", 8), ("xl", 2), ("core", 2), ("y", 4), ("xh", 2))
NAMES = tuple(name for name, _ in AXES)
PLANE = ("xl", "core", "y", "xh")
NZ = 8
NG = 32
ROWS = 2
PER = NZ * ROWS
D = 512
E = 16
K = 4
M = 256
F32 = jnp.float32
BF16 = jnp.bfloat16
LIMIT = pltpu.CompilerParams(vmem_limit_bytes=32 * 1024 * 1024)


def order():
    to = lax.broadcasted_iota(jnp.int32, (D, D), 0)
    at = lax.broadcasted_iota(jnp.int32, (D, D), 1)
    g, z, r = to // PER, (to // ROWS) % NZ, to % ROWS
    return jnp.where(z * (NG * ROWS) + g * ROWS + r == at, 1.0, 0.0).astype(BF16)


def matmul(a, b, dims):
    return lax.dot_general(a, b, (dims, ((), ())), preferred_element_type=F32)


def masked_of(grad, count):
    slot = lax.broadcasted_iota(jnp.int32, (M, D), 0)
    return jnp.where(slot < count, grad.astype(F32), 0.0).astype(BF16)


def outer_kernel(counts, x, grad, out, pick):
    k = pl.program_id(0)

    @pl.when(k == 0)
    def _():
        pick[...] = order()

    turned = matmul(pick[...], x[0], ((1,), (1,))).astype(BF16)
    masked = masked_of(grad[0], counts[k])
    product = matmul(turned, masked, ((1,), (0,)))
    out[...] = product.astype(BF16).reshape(NG, 1, PER, D)


def outer(counts, x, grad):
    return pl.pallas_call(
        outer_kernel,
        grid_spec=pltpu.PrefetchScalarGridSpec(
            num_scalar_prefetch=1,
            grid=(K,),
            in_specs=[
                pl.BlockSpec((1, M, D), lambda k, c: (k, 0, 0)),
                pl.BlockSpec((1, M, D), lambda k, c: (k, 0, 0)),
            ],
            out_specs=pl.BlockSpec((NG, 1, PER, D), lambda k, c: (0, k, 0, 0)),
            scratch_shapes=[pltpu.VMEM((D, D), BF16)],
        ),
        out_shape=jax.ShapeDtypeStruct((NG, K, PER, D), BF16),
        compiler_params=LIMIT,
        cost_estimate=pl.CostEstimate(flops=2 * K * D * D * (M + M), bytes_accessed=4 << 20, transcendentals=0),
        name="outer",
    )(counts, x, grad)


def spread(fixed):
    n = fixed.shape[0]
    width = NZ * E * ROWS
    lane = lax.broadcasted_iota(jnp.int32, (E, width), 1)
    row = lax.broadcasted_iota(jnp.int32, (E, width), 0)
    widen = jnp.where((lane // ROWS) % E == row, 1.0, 0.0).astype(BF16)
    q = lax.broadcasted_iota(jnp.int32, (n * PER, width), 0) % PER
    col = lax.broadcasted_iota(jnp.int32, (n * PER, width), 1)
    same = (q // ROWS == col // (E * ROWS)) & (q % ROWS == col % ROWS)
    high = (fixed // 64).astype(F32) * (1.0 / 64.0)
    low = (fixed % 64).astype(F32) * (1.0 / 4096.0)
    parts = []
    for part in (high, low):
        wide = matmul(part.astype(BF16), widen, ((1,), (0,)))
        tall = jnp.broadcast_to(wide[:, None, :], (n, PER, width)).reshape(n * PER, width)
        parts.append(jnp.where(same, tall, 0.0).astype(BF16))
    return parts


STEP = 32


def merge_kernel(fixed, experts, out):
    high, low = spread(fixed[...])
    e = experts[...]
    total = matmul(high, e, ((1,), (0,))) + matmul(low, e, ((1,), (0,)))
    out[...] = total.astype(BF16)


def merge(fixed, experts):
    systems = NG * K
    width = NZ * E * ROWS
    return pl.pallas_call(
        merge_kernel,
        grid=(systems // STEP,),
        in_specs=[
            pl.BlockSpec((STEP, E), lambda s: (s, 0)),
            pl.BlockSpec((width, D), lambda s: (0, 0)),
        ],
        out_specs=pl.BlockSpec((STEP * PER, D), lambda s: (s, 0)),
        out_shape=jax.ShapeDtypeStruct((systems * PER, D), BF16),
        compiler_params=LIMIT,
        cost_estimate=pl.CostEstimate(flops=4 * systems * PER * width * D, bytes_accessed=3 << 20, transcendentals=0),
        name="merge",
    )(fixed, experts)


def mix_kernel(fixed, terms, out):
    high, low = spread(fixed[...])
    t = terms[...]
    total = matmul(high, t, ((0,), (0,))) + matmul(low, t, ((0,), (0,)))

    @pl.when(pl.program_id(0) == 0)
    def _():
        out[...] = total

    @pl.when(pl.program_id(0) > 0)
    def _():
        out[...] += total


def mix(fixed, terms):
    systems = NG * K
    width = NZ * E * ROWS
    return pl.pallas_call(
        mix_kernel,
        grid=(systems // STEP,),
        in_specs=[
            pl.BlockSpec((STEP, E), lambda s: (s, 0)),
            pl.BlockSpec((STEP * PER, D), lambda s: (s, 0)),
        ],
        out_specs=pl.BlockSpec((width, D), lambda s: (0, 0)),
        out_shape=jax.ShapeDtypeStruct((width, D), F32),
        compiler_params=LIMIT,
        cost_estimate=pl.CostEstimate(flops=4 * systems * PER * width * D, bytes_accessed=3 << 20, transcendentals=0),
        name="mix",
    )(fixed, terms)


def back_kernel(counts, grad, merged, out, pick):
    k = pl.program_id(0)

    @pl.when(k == 0)
    def _():
        pick[...] = order()

    masked = masked_of(grad[0], counts[k])
    weights = merged[...].reshape(D, D)
    moved = matmul(masked, weights, ((1,), (1,))).astype(BF16)
    out[0] = matmul(moved, pick[...], ((1,), (0,))).astype(BF16)


def back(counts, grad, merged):
    return pl.pallas_call(
        back_kernel,
        grid_spec=pltpu.PrefetchScalarGridSpec(
            num_scalar_prefetch=1,
            grid=(K,),
            in_specs=[
                pl.BlockSpec((1, M, D), lambda k, c: (k, 0, 0)),
                pl.BlockSpec((NG, 1, PER, D), lambda k, c: (0, k, 0, 0)),
            ],
            out_specs=pl.BlockSpec((1, M, D), lambda k, c: (k, 0, 0)),
            scratch_shapes=[pltpu.VMEM((D, D), BF16)],
        ),
        out_shape=jax.ShapeDtypeStruct((K, M, D), BF16),
        compiler_params=LIMIT,
        cost_estimate=pl.CostEstimate(flops=4 * K * M * D * D, bytes_accessed=4 << 20, transcendentals=0),
        name="back",
    )(counts, grad, merged)


def swap(array, axes):
    return lax.all_to_all(array, axes, 0, 0, tiled=True)


def shards(inputs, out_grad, coeff_fixed, atom_counts, experts):
    fixed = swap(jnp.broadcast_to(coeff_fixed[None], (NG, K, E)), PLANE).reshape(NG * K, E)
    own = experts.reshape(1, E * ROWS, D)
    rows = swap(jnp.broadcast_to(own, (NZ, E * ROWS, D)), ("z",)).reshape(NZ * E * ROWS, D)
    terms = swap(outer(atom_counts, inputs, out_grad), PLANE)
    merged = swap(merge(fixed, rows).reshape(NG, K, PER, D), PLANE)
    summed = mix(fixed, terms.reshape(NG * K * PER, D))
    arrived = swap(summed.reshape(NZ, E * ROWS, D), ("z",))
    in_grad = back(atom_counts, out_grad, merged)
    return in_grad, arrived.sum(axis=0).reshape(E, ROWS, D)


def solution(mesh):
    split = Mesh(mesh.devices.reshape([size for _, size in AXES]), NAMES)
    placed = (
        P(NAMES, None, None),
        P(NAMES, None, None),
        P(NAMES, None),
        P(NAMES),
        P(None, NAMES, None),
    )
    return jax.shard_map(
        shards,
        mesh=split,
        in_specs=placed,
        out_specs=(P(NAMES, None, None), P(None, NAMES, None)),
        check_vma=False,
    )
```

time: 2040 us -> 131 us (0.06)
  waiting for transfers between devices: 1970 us -> 71.4 us
  starting transfers between devices: 0.08 us -> 32.2 us
  matrix products: 29.5 us -> 0 us
    reduce_scatter x1 -> x0, waiting for transfers between devices: 1310 us -> none  [shards(): lax.psum_scatter(term, ('dp', 'fsdp'), scatter_dimension=1, tiled=True)]
    all_gather x1 -> x0, waiting for transfers between devices: 665 us -> none  [shards(): whole = lax.all_gather(experts, ('dp', 'fsdp'), axis=1, tiled=True)]
    all_to_all x0 -> x5, waiting for transfers between devices: none -> 71.4 us  [swap(): return lax.all_to_all(array, axes, 0, 0, tiled=True)]
    all_to_all x0 -> x5, starting transfers between devices: none -> 32.2 us  [swap(): return lax.all_to_all(array, axes, 0, 0, tiled=True)]
    dot_general x4 -> x0, matrix products: 29.5 us -> none  [the longest x1 17.5 us: shards(): term = jnp.einsum('se,sij->eij', coeffs, per_system, precision=HIGH)]
  transfers between devices with their start and end apart: 2 -> 5, of which waited for: 2 -> 5; matrix products, arithmetic and copies ran while one was open for 2% -> 1% of each run, Pallas kernels for 0% -> 10%
where the time goes in v1:
time: 131 us
  waiting for transfers between devices  71.4 us (55%)
  starting transfers between devices  32.2 us (25%)
  Pallas kernels  13.7 us (10%)
  local copies, waits for them, and re-layouts  11.6 us (9%)
    all_to_all x5, waiting for transfers between devices, swap(): return lax.all_to_all(array, axes, 0, 0, tiled=True)  71.4 us
    all_to_all x5, starting transfers between devices, swap(): return lax.all_to_all(array, axes, 0, 0, tiled=True)  32.2 us
    unnamed x18, local copies, waits for them, and re-layouts  8.15 us
    pallas_call x1, Pallas kernels, outer(): pl.pallas_call(outer_kernel, grid_spec=pltpu.PrefetchScalarGridSpec(num_s...  4.6 us
    pallas_call x1, Pallas kernels, back(): pl.pallas_call(back_kernel, grid_spec=pltpu.PrefetchScalarGridSpec(num_sc...  3.91 us
    pallas_call x1, Pallas kernels, mix(): pl.pallas_call(mix_kernel, grid=(systems // STEP,), in_specs=[pl.BlockSpe...  2.9 us
  transfers between devices with their start and end apart: 5, of which 5 were waited for; matrix products, arithmetic and copies ran while one was open for 1% of the time, Pallas kernels for 10%

profile of v1, /device:TPU:9, one launch (start us, length us, event | category | flops | bytes accessed | tf_op | source)
XLA Modules:
  0.0 130.7 jit_solution(10280657208785897397)
XLA Ops:
  0.6 1.3 %broadcast_in_dim.6 = s32[32,4,16]{2,1,0:T(4,128)} broadcast(s32[4,16]{1,0:T(4,128)} %param.7), dimensions={1,2} | broadcast | bytes 8448 | tf_op jit(solution)/shard_map/broadcast_in_dim | solution.py:190
  1.9 7.8 %all-to-all-start = ((s32[32,4,16]{2,1,0:T(4,128)}), s32[32,4,16]{2,1,0:T(4,128)S(1)}, u32[]{:S(2)}, u32[]{:S(2)}) async-start(s32[32,4,16]{2,1,0:T(4,128)} %broadcast_in_dim.6), calls=%async_computation | async-start | bytes 131072 | tf_op jit(solution)/shard_map/all_to_all | solution.py:186
  9.8 0.8 broadcast_in_dim.14
  10.6 5.4 %all-to-all-done = s32[32,4,16]{2,1,0:T(4,128)S(1)} async-done(((s32[32,4,16]{2,1,0:T(4,128)}), s32[32,4,16]{2,1,0:T(4,128)S(1)}, u32[]{:S(2)}, u32[]{:S(2)}) %all-to-all-start) | async-done | bytes 8224 | tf_op jit(solution)/shard_map/all_to_all | solution.py:186
  16.0 0.7 broadcast_in_dim.15
  16.7 8.2 %all-to-all-start.1 = ((bf16[8,32,512]{2,1,0:T(8,128)(2,1)}), bf16[8,32,512]{2,1,0:T(8,128)(2,1)S(1)}, u32[]{:S(2)}, u32[]{:S(2)}) async-start(bf16[8,32,512]{2,1,0:T(8,128)(2,1)} %broadcast_in_dim.15), calls=%async_computation.1 | async-start | bytes 524288 | tf_op jit(solution)/shard_map/all_to_all | solution.py:186
  24.9 0.0 copy-start
  24.9 1.2 copy-done
  26.1 0.0 copy-start.5
  26.1 1.2 copy-done.5
  27.3 0.0 copy-start.7
  27.4 0.7 copy-done.7
  28.0 4.6 %outer.1 = bf16[32,4,16,512]{3,2,1,0:T(8,128)(2,1)} custom-call(s32[4]{0:T(128)S(1)} %copy-done.7, bf16[4,256,512]{2,1,0:T(8,128)(2,1)S(1)} %copy-done.5, bf16[4,256,512]{2,1,0:T(8,128)(2,1)S(1)} %copy-done), custom_call_target="tpu_custom_call" | custom-call | flops 1073741824 | bytes 4194304 | tf_op jit(solution)/shard_map/outer/pallas_call | solution.py:54
  32.6 3.3 %all-to-all-done.1 = bf16[8,32,512]{2,1,0:T(8,128)(2,1)S(1)} async-done(((bf16[8,32,512]{2,1,0:T(8,128)(2,1)}), bf16[8,32,512]{2,1,0:T(8,128)(2,1)S(1)}, u32[]{:S(2)}, u32[]{:S(2)}) %all-to-all-start.1) | async-done | bytes 262176 | tf_op jit(solution)/shard_map/all_to_all | solution.py:186
  35.9 6.6 %all-to-all-start.3 = ((bf16[32,4,16,512]{3,2,1,0:T(8,128)(2,1)}), bf16[32,4,16,512]{3,2,1,0:T(8,128)(2,1)S(1)}, u32[]{:S(2)}, u32[]{:S(2)}) async-start(bf16[32,4,16,512]{3,2,1,0:T(8,128)(2,1)} %outer.1), calls=%async_computation.3 | async-start | bytes 4194304 | tf_op jit(solution)/shard_map/all_to_all | solution.py:186
  42.5 2.3 %merge.1 = bf16[2048,512]{1,0:T(8,128)(2,1)S(1)} custom-call(s32[128,16]{1,0:T(8,128)S(1)} %bitcast.9, bf16[256,512]{1,0:T(8,128)(2,1)S(1)} %bitcast.8), custom_call_target="tpu_custom_call" | custom-call | flops 1073741824 | bytes 3145728 | tf_op jit(solution)/shard_map/merge/pallas_call | solution.py:105
  44.8 0.0 copy-start.4
  44.8 1.3 %copy-done.4 = bf16[2048,512]{1,0:T(8,128)(2,1)} copy-done((bf16[2048,512]{1,0:T(8,128)(2,1)}, bf16[2048,512]{1,0:T(8,128)(2,1)S(1)}, u32[]{:S(2)}) %copy-start.4) | copy-done | bytes 2097176
  46.1 25.2 %all-to-all-done.3 = bf16[32,4,16,512]{3,2,1,0:T(8,128)(2,1)S(1)} async-done(((bf16[32,4,16,512]{3,2,1,0:T(8,128)(2,1)}), bf16[32,4,16,512]{3,2,1,0:T(8,128)(2,1)S(1)}, u32[]{:S(2)}, u32[]{:S(2)}) %all-to-all-start.3) | async-done | bytes 2097184 | tf_op jit(solution)/shard_map/all_to_all | solution.py:186
  71.4 0.0 copy-start.2
  71.4 1.3 %copy-done.2 = bf16[32,4,16,512]{3,2,1,0:T(8,128)(2,1)} copy-done((bf16[32,4,16,512]{3,2,1,0:T(8,128)(2,1)}, bf16[32,4,16,512]{3,2,1,0:T(8,128)(2,1)S(1)}, u32[]{:S(2)}) %copy-start.2) | copy-done | bytes 2097176
  72.7 5.4 %all-to-all-start.2 = ((bf16[32,4,16,512]{3,2,1,0:T(8,128)(2,1)}), bf16[32,4,16,512]{3,2,1,0:T(8,128)(2,1)S(1)}, u32[]{:S(2)}, u32[]{:S(2)}) async-start(bf16[32,4,16,512]{3,2,1,0:T(8,128)(2,1)} %bitcast.6), calls=%async_computation.2 | async-start | bytes 4194304 | tf_op jit(solution)/shard_map/all_to_all | solution.py:186
  78.0 0.0 copy-start.3
  78.1 1.6 %copy-done.3 = bf16[32,4,16,512]{3,2,1,0:T(8,128)(2,1)S(1)} copy-done((bf16[32,4,16,512]{3,2,1,0:T(8,128)(2,1)S(1)}, bf16[32,4,16,512]{3,2,1,0:T(8,128)(2,1)}, u32[]{:S(2)}) %copy-start.3) | copy-done | bytes 2097176
  79.6 0.0 copy-start.1
  79.6 0.0 copy-start.8
  79.6 2.9 %mix.1 = f32[256,512]{1,0:T(8,128)S(1)} custom-call(s32[128,16]{1,0:T(8,128)S(1)} %bitcast.10, bf16[2048,512]{1,0:T(8,128)(2,1)S(1)} %bitcast.5), custom_call_target="tpu_custom_call" | custom-call | flops 1073741824 | bytes 3145728 | tf_op jit(solution)/shard_map/mix/pallas_call | solution.py:137
  82.6 0.0 copy-start.6
  82.6 0.8 copy-done.6
  83.4 23.5 %all-to-all-done.2.merged = bf16[32,4,16,512]{3,2,1,0:T(8,128)(2,1)S(1)} async-done(((bf16[32,4,16,512]{3,2,1,0:T(8,128)(2,1)}), bf16[32,4,16,512]{3,2,1,0:T(8,128)(2,1)S(1)}, u32[]{:S(2)}, u32[]{:S(2)}) %all-to-all-start.2) | async-done | bytes 2097184 | tf_op jit(solution)/shard_map/all_to_all | solution.py:186
  106.9 4.1 %all-to-all-start.4 = ((f32[8,32,512]{2,1,0:T(8,128)}), f32[8,32,512]{2,1,0:T(8,128)}, u32[]{:S(2)}, u32[]{:S(2)}) async-start(f32[8,32,512]{2,1,0:T(8,128)} %bitcast.7), calls=%async_computation.4 | async-start | bytes 1048576 | tf_op jit(solution)/shard_map/all_to_all | solution.py:186
  111.0 0.0 copy-done.1
  111.0 0.0 copy-done.8
  111.0 3.9 %back.1 = bf16[4,256,512]{2,1,0:T(8,128)(2,1)} custom-call(s32[4]{0:T(128)S(1)} %copy-done.8, bf16[4,256,512]{2,1,0:T(8,128)(2,1)S(1)} %copy-done.1, bf16[32,4,16,512]{3,2,1,0:T(8,128)(2,1)S(1)} %all-to-all-done.2.merged), custom_call_target="tpu_custom_call" | custom-call | flops 1073741824 | bytes 4194304 | tf_op jit(solution)/shard_map/back/pallas_call | solution.py:166
  115.0 14.0 %all-to-all-done.4 = f32[8,32,512]{2,1,0:T(8,128)} async-done(((f32[8,32,512]{2,1,0:T(8,128)}), f32[8,32,512]{2,1,0:T(8,128)}, u32[]{:S(2)}, u32[]{:S(2)}) %all-to-all-start.4) | async-done | bytes 524320 | tf_op jit(solution)/shard_map/all_to_all | solution.py:186
  129.0 1.1 reduce_sum.9
  130.1 0.7 reshape.30
Async XLA Ops:
  1.9 14.0 %all-to-all-start = ((s32[32,4,16]{2,1,0:T(4,128)}), s32[32,4,16]{2,1,0:T(4,128)S(1)}, u32[]{:S(2)}, u32[]{:S(2)}) async-start(s32[32,4,16]{2,1,0:T(4,128)} %broadcast_in_dim.6), calls=%async_computation | async-start | bytes 131072 | tf_op jit(solution)/shard_map/all_to_all | solution.py:186
  16.7 19.2 %all-to-all-start.1 = ((bf16[8,32,512]{2,1,0:T(8,128)(2,1)}), bf16[8,32,512]{2,1,0:T(8,128)(2,1)S(1)}, u32[]{:S(2)}, u32[]{:S(2)}) async-start(bf16[8,32,512]{2,1,0:T(8,128)(2,1)} %broadcast_in_dim.15), calls=%async_computation.1 | async-start | bytes 524288 | tf_op jit(solution)/shard_map/all_to_all | solution.py:186
  24.9 1.2 copy-start
  26.1 1.2 copy-start.5
  27.3 0.7 copy-start.7
  35.9 35.5 %all-to-all-start.3 = ((bf16[32,4,16,512]{3,2,1,0:T(8,128)(2,1)}), bf16[32,4,16,512]{3,2,1,0:T(8,128)(2,1)S(1)}, u32[]{:S(2)}, u32[]{:S(2)}) async-start(bf16[32,4,16,512]{3,2,1,0:T(8,128)(2,1)} %outer.1), calls=%async_computation.3 | async-start | bytes 4194304 | tf_op jit(solution)/shard_map/all_to_all | solution.py:186
  44.8 1.3 %copy-start.4 = (bf16[2048,512]{1,0:T(8,128)(2,1)}, bf16[2048,512]{1,0:T(8,128)(2,1)S(1)}, u32[]{:S(2)}) copy-start(bf16[2048,512]{1,0:T(8,128)(2,1)S(1)} %merge.1) | copy-start | bytes 6291460
  71.4 1.3 %copy-start.2 = (bf16[32,4,16,512]{3,2,1,0:T(8,128)(2,1)}, bf16[32,4,16,512]{3,2,1,0:T(8,128)(2,1)S(1)}, u32[]{:S(2)}) copy-start(bf16[32,4,16,512]{3,2,1,0:T(8,128)(2,1)S(1)} %all-to-all-done.3) | copy-start | bytes 6291460
  72.7 34.2 %all-to-all-start.2 = ((bf16[32,4,16,512]{3,2,1,0:T(8,128)(2,1)}), bf16[32,4,16,512]{3,2,1,0:T(8,128)(2,1)S(1)}, u32[]{:S(2)}, u32[]{:S(2)}) async-start(bf16[32,4,16,512]{3,2,1,0:T(8,128)(2,1)} %bitcast.6), calls=%async_computation.2 | async-start | bytes 4194304 | tf_op jit(solution)/shard_map/all_to_all | solution.py:186
  78.0 1.6 %copy-start.3 = (bf16[32,4,16,512]{3,2,1,0:T(8,128)(2,1)S(1)}, bf16[32,4,16,512]{3,2,1,0:T(8,128)(2,1)}, u32[]{:S(2)}) copy-start(bf16[32,4,16,512]{3,2,1,0:T(8,128)(2,1)} %copy-done.2) | copy-start | bytes 6291460
  79.6 31.4 %copy-start.1 = (bf16[4,256,512]{2,1,0:T(8,128)(2,1)S(1)}, bf16[4,256,512]{2,1,0:T(8,128)(2,1)}, u32[]{:S(2)}) copy-start(bf16[4,256,512]{2,1,0:T(8,128)(2,1)} %grad.3) | copy-start | bytes 3145732
  79.6 31.4 %copy-start.8 = (s32[4]{0:T(128)S(1)}, s32[4]{0:T(128)}, u32[]{:S(2)}) copy-start(s32[4]{0:T(128)} %counts.3) | copy-start | bytes 52
  82.6 0.8 copy-start.6
  106.9 22.1 %all-to-all-start.4 = ((f32[8,32,512]{2,1,0:T(8,128)}), f32[8,32,512]{2,1,0:T(8,128)}, u32[]{:S(2)}, u32[]{:S(2)}) async-start(f32[8,32,512]{2,1,0:T(8,128)} %bitcast.7), calls=%async_computation.4 | async-start | bytes 1048576 | tf_op jit(solution)/shard_map/all_to_all | solution.py:186

commit v2 on v1

v2 whole, which is shorter than its diff:
```python
import jax
import jax.numpy as jnp
from jax import lax
from jax.experimental import pallas as pl
from jax.experimental.pallas import tpu as pltpu
from jax.sharding import Mesh, PartitionSpec as P

AXES = (("z", 8), ("xl", 2), ("core", 2), ("y", 4), ("xh", 2))
NAMES = tuple(name for name, _ in AXES)
PLANE = ("xl", "core", "y", "xh")
NZ = 8
NG = 32
ROWS = 2
PER = NZ * ROWS
D = 512
E = 16
K = 4
M = 256
F32 = jnp.float32
BF16 = jnp.bfloat16
LIMIT = pltpu.CompilerParams(vmem_limit_bytes=56 * 1024 * 1024)


def row_of(shape, dim):
    return lax.broadcasted_iota(jnp.int32, shape, dim)


def order():
    to = row_of((D, 1), 0)
    source = (((to >> 1) & (NZ - 1)) << 6) + ((to >> 4) << 1) + (to & 1)
    return jnp.where(source == row_of((1, D), 1), 1.0, 0.0).astype(BF16)


def matmul(a, b, dims):
    return lax.dot_general(a, b, (dims, ((), ())), preferred_element_type=F32)


def masked_of(grad, count):
    return jnp.where(row_of((M, 1), 0) < count, grad, jnp.zeros_like(grad))


def outer_kernel(counts, x, grad, out, pick):
    k = pl.program_id(0)

    @pl.when(k == 0)
    def _():
        pick[...] = order()

    turned = matmul(pick[...], x[0], ((1,), (1,))).astype(BF16)
    masked = masked_of(grad[0], counts[k])
    product = matmul(turned, masked, ((1,), (0,)))
    out[...] = product.astype(BF16).reshape(NG, 1, PER, D)


def outer(counts, x, grad):
    return pl.pallas_call(
        outer_kernel,
        grid_spec=pltpu.PrefetchScalarGridSpec(
            num_scalar_prefetch=1,
            grid=(K,),
            in_specs=[
                pl.BlockSpec((1, M, D), lambda k, c: (k, 0, 0)),
                pl.BlockSpec((1, M, D), lambda k, c: (k, 0, 0)),
            ],
            out_specs=pl.BlockSpec((NG, 1, PER, D), lambda k, c: (0, k, 0, 0)),
            scratch_shapes=[pltpu.VMEM((D, D), BF16)],
        ),
        out_shape=jax.ShapeDtypeStruct((NG, K, PER, D), BF16),
        compiler_params=LIMIT,
        cost_estimate=pl.CostEstimate(flops=2 * K * D * D * (M + M), bytes_accessed=4 << 20, transcendentals=0),
        name="outer",
    )(counts, x, grad)


WIDTH = NZ * E * ROWS
STEP = 32


def spread(fixed, z, away):
    n = fixed.shape[0]
    widen = jnp.where(((row_of((E, WIDTH), 1) >> 1) & (E - 1)) == row_of((E, WIDTH), 0), 1.0, 0.0).astype(BF16)
    row = row_of((n * PER, 1), 0) & (PER - 1)
    col = row_of((1, WIDTH), 1)
    line = (z + away * (col >> 5) + NZ) & (NZ - 1)
    same = row == (line << 1) + (col & 1)
    high = (fixed >> 6).astype(F32) * (1.0 / 64.0)
    low = (fixed & 63).astype(F32) * (1.0 / 4096.0)
    parts = []
    for part in (high, low):
        wide = matmul(part.astype(BF16), widen, ((1,), (0,)))
        tall = jnp.broadcast_to(wide[:, None, :], (n, PER, WIDTH)).reshape(n * PER, WIDTH)
        parts.append(jnp.where(same, tall, 0.0).astype(BF16))
    return parts


def merge_kernel(z, fixed, *refs):
    *blocks, out, whole = refs

    @pl.when(pl.program_id(0) == 0)
    def _():
        for n, block in enumerate(blocks):
            whole[n * E * ROWS : (n + 1) * E * ROWS] = block[...]

    high, low = spread(fixed[...], z[0], -1)
    e = whole[...]
    total = matmul(high, e, ((1,), (0,))) + matmul(low, e, ((1,), (0,)))
    out[...] = total.astype(BF16)


def merge(z, fixed, blocks):
    systems = NG * K
    return pl.pallas_call(
        merge_kernel,
        grid_spec=pltpu.PrefetchScalarGridSpec(
            num_scalar_prefetch=1,
            grid=(systems // STEP,),
            in_specs=[pl.BlockSpec((STEP, E), lambda s, z: (s, 0))]
            + [pl.BlockSpec((E * ROWS, D), lambda s, z: (0, 0))] * NZ,
            out_specs=pl.BlockSpec((STEP * PER, D), lambda s, z: (s, 0)),
            scratch_shapes=[pltpu.VMEM((WIDTH, D), BF16)],
        ),
        out_shape=jax.ShapeDtypeStruct((systems * PER, D), BF16),
        compiler_params=LIMIT,
        cost_estimate=pl.CostEstimate(flops=4 * systems * PER * WIDTH * D, bytes_accessed=3 << 20, transcendentals=0),
        name="merge",
    )(z, fixed, *blocks)


def mix_kernel(z, fixed, terms, *refs):
    *outs, total = refs
    step = pl.program_id(0)
    high, low = spread(fixed[...], z[0], 1)
    t = terms[...]
    part = matmul(high, t, ((0,), (0,))) + matmul(low, t, ((0,), (0,)))

    @pl.when(step == 0)
    def _():
        total[...] = part

    @pl.when(step > 0)
    def _():
        total[...] += part

    @pl.when(step == pl.num_programs(0) - 1)
    def _():
        for n, out in enumerate(outs):
            out[...] = total[n * E * ROWS : (n + 1) * E * ROWS]


def mix(z, fixed, terms):
    systems = NG * K
    return pl.pallas_call(
        mix_kernel,
        grid_spec=pltpu.PrefetchScalarGridSpec(
            num_scalar_prefetch=1,
            grid=(systems // STEP,),
            in_specs=[
                pl.BlockSpec((STEP, E), lambda s, z: (s, 0)),
                pl.BlockSpec((STEP * PER, D), lambda s, z: (s, 0)),
            ],
            out_specs=[pl.BlockSpec((E * ROWS, D), lambda s, z: (0, 0))] * NZ,
            scratch_shapes=[pltpu.VMEM((WIDTH, D), F32)],
        ),
        out_shape=[jax.ShapeDtypeStruct((E * ROWS, D), F32)] * NZ,
        compiler_params=LIMIT,
        cost_estimate=pl.CostEstimate(flops=4 * systems * PER * WIDTH * D, bytes_accessed=3 << 20, transcendentals=0),
        name="mix",
    )(z, fixed, terms)


def back_kernel(counts, grad, merged, *refs):
    *sums, out, expert_grad, pick = refs
    k = pl.program_id(0)

    @pl.when(k == 0)
    def _():
        pick[...] = order()

    masked = masked_of(grad[0], counts[k])
    weights = merged[...].reshape(D, D)
    moved = matmul(masked, weights, ((1,), (1,))).astype(BF16)
    out[0] = matmul(moved, pick[...], ((1,), (0,))).astype(BF16)

    @pl.when(k == K - 1)
    def _():
        total = sums[0][...]
        for part in sums[1:]:
            total += part[...]
        for e in range(E):
            expert_grad[e] = total[ROWS * e : ROWS * (e + 1)]


def back(counts, grad, merged, sums):
    return pl.pallas_call(
        back_kernel,
        grid_spec=pltpu.PrefetchScalarGridSpec(
            num_scalar_prefetch=1,
            grid=(K,),
            in_specs=[
                pl.BlockSpec((1, M, D), lambda k, c: (k, 0, 0)),
                pl.BlockSpec((NG, 1, PER, D), lambda k, c: (0, k, 0, 0)),
            ]
            + [pl.BlockSpec((E * ROWS, D), lambda k, c: (0, 0))] * NZ,
            out_specs=[
                pl.BlockSpec((1, M, D), lambda k, c: (k, 0, 0)),
                pl.BlockSpec((E, ROWS, D), lambda k, c: (0, 0, 0)),
            ],
            scratch_shapes=[pltpu.VMEM((D, D), BF16)],
        ),
        out_shape=[
            jax.ShapeDtypeStruct((K, M, D), BF16),
            jax.ShapeDtypeStruct((E, ROWS, D), F32),
        ],
        compiler_params=LIMIT,
        cost_estimate=pl.CostEstimate(flops=4 * K * M * D * D, bytes_accessed=5 << 20, transcendentals=0),
        name="back",
    )(counts, grad, merged, *sums)


def swap(array, axes):
    return lax.all_to_all(array, axes, 0, 0, tiled=True)


def along_z(array, by):
    return lax.ppermute(array, "z", [(i, (i + by) % NZ) for i in range(NZ)])


def shards(inputs, out_grad, coeff_fixed, atom_counts, experts):
    z = lax.axis_index("z").astype(jnp.int32).reshape(1)
    fixed = swap(jnp.broadcast_to(coeff_fixed[None], (NG, K, E)), PLANE).reshape(NG * K, E)
    own = experts.reshape(E * ROWS, D)
    rows = [own] + [along_z(own, n) for n in range(1, NZ)]
    terms = swap(outer(atom_counts, inputs, out_grad), PLANE)
    merged = swap(merge(z, fixed, rows).reshape(NG, K, PER, D), PLANE)
    mixed = mix(z, fixed, terms.reshape(NG * K * PER, D))
    sums = [mixed[0]] + [along_z(mixed[n], n) for n in range(1, NZ)]
    return tuple(back(atom_counts, out_grad, merged, sums))


def solution(mesh):
    split = Mesh(mesh.devices.reshape([size for _, size in AXES]), NAMES)
    placed = (
        P(NAMES, None, None),
        P(NAMES, None, None),
        P(NAMES, None),
        P(NAMES),
        P(None, NAMES, None),
    )
    return jax.shard_map(
        shards,
        mesh=split,
        in_specs=placed,
        out_specs=(P(NAMES, None, None), P(None, NAMES, None)),
        check_vma=False,
    )
```

time: 131 us -> 97.2 us (0.74); the launches traced: 131 us -> 95.6 us
  waiting for transfers between devices: 71.4 us -> 16 us
  starting transfers between devices: 32.2 us -> 52.9 us
  Pallas kernels: 13.7 us -> 21.2 us
  local copies, waits for them, and re-layouts: 11.6 us -> 4.6 us
    all_to_all x5 -> x3, waiting for transfers between devices: 71.4 us -> 13 us  [swap(): return lax.all_to_all(array, axes, 0, 0, tiled=True)]
    ppermute x0 -> x14, starting transfers between devices: none -> 31.7 us  [along_z(): return lax.ppermute(array, 'z', [(i, (i + by) % NZ) for i in range(NZ)])]
    all_to_all x5 -> x3, starting transfers between devices: 32.2 us -> 21.2 us  [swap(): return lax.all_to_all(array, axes, 0, 0, tiled=True)]
    unnamed x18 -> x36, local copies, waits for them, and re-layouts: 8.15 us -> 3.26 us
    pallas_call x2, Pallas kernels: 5.15 us -> 9.28 us  [the longest x1 4.97 us: mix(): pl.pallas_call(mix_kernel, grid_spec=pltpu.PrefetchScalarGridSpec(num_sca...]
    ppermute x0 -> x14, waiting for transfers between devices: none -> 3.05 us  [along_z(): return lax.ppermute(array, 'z', [(i, (i + by) % NZ) for i in range(NZ)])]
    pallas_call x1, Pallas kernels: 3.91 us -> 5.8 us  [back(): pl.pallas_call(back_kernel, grid_spec=pltpu.PrefetchScalarGridSpec(num_sc...]
    pallas_call x1, Pallas kernels: 4.6 us -> 6.12 us  [outer(): pl.pallas_call(outer_kernel, grid_spec=pltpu.PrefetchScalarGridSpec(num_s...]
  transfers between devices with their start and end apart: 5 -> 17, of which waited for: 5 -> 6; matrix products, arithmetic and copies ran while one was open for 1% -> 0% of each run, Pallas kernels for 10% -> 16%
where the time goes in v2:
time: 97.2 us; the launch traced here: 95.6 us
  starting transfers between devices  52.9 us (54%)
  Pallas kernels  21.2 us (22%)
  waiting for transfers between devices  16 us (16%)
  local copies, waits for them, and re-layouts  4.6 us (5%)
    ppermute x14, starting transfers between devices, along_z(): return lax.ppermute(array, 'z', [(i, (i + by) % NZ) for i in range(NZ)])  31.7 us
    all_to_all x3, starting transfers between devices, swap(): return lax.all_to_all(array, axes, 0, 0, tiled=True)  21.2 us
    all_to_all x3, waiting for transfers between devices, swap(): return lax.all_to_all(array, axes, 0, 0, tiled=True)  13 us
    pallas_call x1, Pallas kernels, outer(): pl.pallas_call(outer_kernel, grid_spec=pltpu.PrefetchScalarGridSpec(num_s...  6.12 us
    pallas_call x1, Pallas kernels, back(): pl.pallas_call(back_kernel, grid_spec=pltpu.PrefetchScalarGridSpec(num_sc...  5.8 us
    pallas_call x1, Pallas kernels, mix(): pl.pallas_call(mix_kernel, grid_spec=pltpu.PrefetchScalarGridSpec(num_sca...  4.97 us
    pallas_call x1, Pallas kernels, merge(): pl.pallas_call(merge_kernel, grid_spec=pltpu.PrefetchScalarGridSpec(num_s...  4.3 us
    unnamed x36, local copies, waits for them, and re-layouts  3.26 us
  transfers between devices with their start and end apart: 17, of which 6 were waited for; matrix products, arithmetic and copies ran while one was open for 0% of the time, Pallas kernels for 16%

profile of v2, /device:TPU:9, one launch (start us, length us, event | category | flops | bytes accessed | tf_op | source)
XLA Modules:
  0.0 95.6 jit_solution(4760884426137484950)
XLA Ops:
  0.6 1.3 %broadcast_in_dim.2 = s32[32,4,16]{2,1,0:T(4,128)} broadcast(s32[4,16]{1,0:T(4,128)} %param.7), dimensions={1,2} | broadcast | bytes 8448 | tf_op jit(solution)/shard_map/broadcast_in_dim | solution.py:230
  1.9 7.8 %all-to-all-start = ((s32[32,4,16]{2,1,0:T(4,128)}), s32[32,4,16]{2,1,0:T(4,128)S(1)}, u32[]{:S(2)}, u32[]{:S(2)}) async-start(s32[32,4,16]{2,1,0:T(4,128)} %broadcast_in_dim.2), calls=%async_computation | async-start | bytes 131072 | tf_op jit(solution)/shard_map/all_to_all | solution.py:221
  9.8 6.1 %outer.1 = bf16[32,4,16,512]{3,2,1,0:T(8,128)(2,1)} custom-call(s32[4]{0:T(128)} %counts.3, bf16[4,256,512]{2,1,0:T(8,128)(2,1)} %x.1, bf16[4,256,512]{2,1,0:T(8,128)(2,1)} %grad.3), custom_call_target="tpu_custom_call" | custom-call | flops 1073741824 | bytes 4194304 | tf_op jit(solution)/shard_map/outer/pallas_call | solution.py:56
  15.9 0.1 all-to-all-done
  16.0 0.6 copy-done.1
  16.6 7.3 %all-to-all-start.2 = ((bf16[32,4,16,512]{3,2,1,0:T(8,128)(2,1)}), bf16[32,4,16,512]{3,2,1,0:T(8,128)(2,1)S(1)}, u32[]{:S(2)}, u32[]{:S(2)}) async-start(bf16[32,4,16,512]{3,2,1,0:T(8,128)(2,1)} %outer.1), calls=%async_computation.2 | async-start | bytes 4194304 | tf_op jit(solution)/shard_map/all_to_all | solution.py:221
  24.0 0.0 copy-start.3
  24.0 5.7 %collective-permute-start.6 = (bf16[32,512]{1,0:T(8,128)(2,1)S(1)}, bf16[32,512]{1,0:T(8,128)(2,1)S(1)}, u32[]{:S(2)}, u32[]{:S(2)}) collective-permute-start(bf16[32,512]{1,0:T(8,128)(2,1)S(1)} %reshape.22.refs_0_), channel_id=1, source_target_pairs={{0,224},{32,0},{64,32},{96,64},{128,96},{160,128},{192,160},{224,1... | collective-permute-start | bytes 98312 | tf_op jit(solution)/shard_map/ppermute | solution.py:225
  29.6 1.2 %collective-permute-start.5 = (bf16[32,512]{1,0:T(8,128)(2,1)S(1)}, bf16[32,512]{1,0:T(8,128)(2,1)S(1)}, u32[]{:S(2)}, u32[]{:S(2)}) collective-permute-start(bf16[32,512]{1,0:T(8,128)(2,1)S(1)} %reshape.22.refs_0_), channel_id=1, source_target_pairs={{0,192},{32,224},{64,0},{96,32},{128,64},{160,96},{192,128},{224,1... | collective-permute-start | bytes 98312 | tf_op jit(solution)/shard_map/ppermute | solution.py:225
  30.8 0.4 collective-permute-start.4
  31.3 4.5 %collective-permute-start.3 = (bf16[32,512]{1,0:T(8,128)(2,1)S(1)}, bf16[32,512]{1,0:T(8,128)(2,1)S(1)}, u32[]{:S(2)}, u32[]{:S(2)}) collective-permute-start(bf16[32,512]{1,0:T(8,128)(2,1)S(1)} %reshape.22.refs_0_), channel_id=1, source_target_pairs={{0,128},{32,160},{64,192},{96,224},{128,0},{160,32},{192,64},{224,... | collective-permute-start | bytes 98312 | tf_op jit(solution)/shard_map/ppermute | solution.py:225
  35.7 0.0 collective-permute-start.2
  35.7 0.0 collective-permute-done.6.refs_7_
  35.7 2.2 %collective-permute-start.1 = (bf16[32,512]{1,0:T(8,128)(2,1)S(1)}, bf16[32,512]{1,0:T(8,128)(2,1)S(1)}, u32[]{:S(2)}, u32[]{:S(2)}) collective-permute-start(bf16[32,512]{1,0:T(8,128)(2,1)S(1)} %reshape.22.refs_0_), channel_id=1, source_target_pairs={{0,64},{32,96},{64,128},{96,160},{128,192},{160,224},{192,0},{224,... | collective-permute-start | bytes 98312 | tf_op jit(solution)/shard_map/ppermute | solution.py:225
  37.9 0.0 collective-permute-done.5.refs_6_
  37.9 1.4 %collective-permute-start = (bf16[32,512]{1,0:T(8,128)(2,1)S(1)}, bf16[32,512]{1,0:T(8,128)(2,1)S(1)}, u32[]{:S(2)}, u32[]{:S(2)}) collective-permute-start(bf16[32,512]{1,0:T(8,128)(2,1)S(1)} %reshape.22.refs_0_), channel_id=1, source_target_pairs={{0,32},{32,64},{64,96},{96,128},{128,160},{160,192},{192,224},{224... | collective-permute-start | bytes 98312 | tf_op jit(solution)/shard_map/ppermute | solution.py:225
  39.3 0.0 collective-permute-done.4.refs_5_
  39.3 0.0 collective-permute-done.3.refs_4_
  39.3 2.2 %collective-permute-done.2.refs_3_ = bf16[32,512]{1,0:T(8,128)(2,1)S(1)} collective-permute-done((bf16[32,512]{1,0:T(8,128)(2,1)S(1)}, bf16[32,512]{1,0:T(8,128)(2,1)S(1)}, u32[]{:S(2)}, u32[]{:S(2)}) %collective-permute-start.2) | collective-permute-done | bytes 32800 | tf_op jit(solution)/shard_map/ppermute | solution.py:225
  41.5 0.7 collective-permute-done.1.refs_2_
  42.2 0.2 collective-permute-done.refs_1_
  42.4 0.4 copy-done.16
  42.8 0.1 copy-done.17
  42.9 4.3 %merge.1 = bf16[2048,512]{1,0:T(8,128)(2,1)} custom-call(s32[1]{0:T(128)} %bitcast.z, s32[128,16]{1,0:T(8,128)} %bitcast.6, bf16[32,512]{1,0:T(8,128)(2,1)} %copy-done.3, bf16[32,512]{1,0:T(8,128)(2,1)} %copy-done.17, bf16[32,512]{1,0:T(8,128)(2,1)} %copy-done.16, bf16[32,512]{1,0:T(8,128)(2,1)} %copy-done.15, bf16[32,512]{1,0:T(8,128)(2,1)} %copy-done.14, ...), custom_call_target="tpu_custom_call" | custom-call | flops 1073741824 | bytes 3145728 | tf_op jit(solution)/shard_map/merge/pallas_call | solution.py:112
  47.2 5.5 %all-to-all-done.2 = bf16[32,4,16,512]{3,2,1,0:T(8,128)(2,1)S(1)} async-done(((bf16[32,4,16,512]{3,2,1,0:T(8,128)(2,1)}), bf16[32,4,16,512]{3,2,1,0:T(8,128)(2,1)S(1)}, u32[]{:S(2)}, u32[]{:S(2)}) %all-to-all-start.2) | async-done | bytes 2097184 | tf_op jit(solution)/shard_map/all_to_all | solution.py:221
  52.7 1.4 %copy-done = bf16[32,4,16,512]{3,2,1,0:T(8,128)(2,1)} copy-done((bf16[32,4,16,512]{3,2,1,0:T(8,128)(2,1)}, bf16[32,4,16,512]{3,2,1,0:T(8,128)(2,1)S(1)}, u32[]{:S(2)}) %copy-start) | copy-done | bytes 2097176
  54.1 6.0 %all-to-all-start.1 = ((bf16[32,4,16,512]{3,2,1,0:T(8,128)(2,1)}), bf16[32,4,16,512]{3,2,1,0:T(8,128)(2,1)}, u32[]{:S(2)}, u32[]{:S(2)}) async-start(bf16[32,4,16,512]{3,2,1,0:T(8,128)(2,1)} %bitcast.5), calls=%async_computation.1 | async-start | bytes 4194304 | tf_op jit(solution)/shard_map/all_to_all | solution.py:221
  60.1 5.0 %mix.1 = (f32[32,512]{1,0:T(8,128)}, f32[32,512]{1,0:T(8,128)}, f32[32,512]{1,0:T(8,128)}, f32[32,512]{1,0:T(8,128)}, f32[32,512]{1,0:T(8,128)}, /*index=5*/f32[...) custom-call(s32[1]{0:T(128)} %bitcast.z, s32[128,16]{1,0:T(8,128)} %bitcast.7, bf16[2048,512]{1,0:T(8,128)(2,1)} %bitcast.4), custom_call_target="tpu_custom_call" | custom-call | flops 1073741824 | bytes 3145728 | tf_op jit(solution)/shard_map/mix/pallas_call | solution.py:152
  65.1 1.7 %collective-permute-start.7 = (f32[32,512]{1,0:T(8,128)}, f32[32,512]{1,0:T(8,128)S(1)}, u32[]{:S(2)}, u32[]{:S(2)}) collective-permute-start(f32[32,512]{1,0:T(8,128)} %get-tuple-element.11), channel_id=1, source_target_pairs={{0,32},{32,64},{64,96},{96,128},{128,160},{160,192},{192,224},{224... | collective-permute-start | bytes 196616 | tf_op jit(solution)/shard_map/ppermute | solution.py:225
  66.8 3.0 %collective-permute-start.8 = (f32[32,512]{1,0:T(8,128)}, f32[32,512]{1,0:T(8,128)S(1)}, u32[]{:S(2)}, u32[]{:S(2)}) collective-permute-start(f32[32,512]{1,0:T(8,128)} %get-tuple-element.12), channel_id=1, source_target_pairs={{0,64},{32,96},{64,128},{96,160},{128,192},{160,224},{192,0},{224,... | collective-permute-start | bytes 196616 | tf_op jit(solution)/shard_map/ppermute | solution.py:225
  69.8 3.8 %collective-permute-start.9 = (f32[32,512]{1,0:T(8,128)}, f32[32,512]{1,0:T(8,128)S(1)}, u32[]{:S(2)}, u32[]{:S(2)}) collective-permute-start(f32[32,512]{1,0:T(8,128)} %get-tuple-element.13), channel_id=1, source_target_pairs={{0,96},{32,128},{64,160},{96,192},{128,224},{160,0},{192,32},{224,... | collective-permute-start | bytes 196616 | tf_op jit(solution)/shard_map/ppermute | solution.py:225
  73.5 0.5 collective-permute-start.10
  74.0 4.5 %collective-permute-start.11 = (f32[32,512]{1,0:T(8,128)}, f32[32,512]{1,0:T(8,128)S(1)}, u32[]{:S(2)}, u32[]{:S(2)}) collective-permute-start(f32[32,512]{1,0:T(8,128)} %get-tuple-element.15), channel_id=1, source_target_pairs={{0,160},{32,192},{64,224},{96,0},{128,32},{160,64},{192,96},{224,1... | collective-permute-start | bytes 196616 | tf_op jit(solution)/shard_map/ppermute | solution.py:225
  78.4 0.0 collective-permute-done.7.refs_1_
  78.4 2.4 %collective-permute-start.12 = (f32[32,512]{1,0:T(8,128)}, f32[32,512]{1,0:T(8,128)S(1)}, u32[]{:S(2)}, u32[]{:S(2)}) collective-permute-start(f32[32,512]{1,0:T(8,128)} %get-tuple-element.16), channel_id=1, source_target_pairs={{0,192},{32,224},{64,0},{96,32},{128,64},{160,96},{192,128},{224,1... | collective-permute-start | bytes 196616 | tf_op jit(solution)/shard_map/ppermute | solution.py:225
  80.8 0.0 collective-permute-done.8.refs_2_
  80.8 0.7 collective-permute-start.13
  81.6 7.4 %all-to-all-done.1.merged = bf16[32,4,16,512]{3,2,1,0:T(8,128)(2,1)} async-done(((bf16[32,4,16,512]{3,2,1,0:T(8,128)(2,1)}), bf16[32,4,16,512]{3,2,1,0:T(8,128)(2,1)}, u32[]{:S(2)}, u32[]{:S(2)}) %all-to-all-start.1) | async-done | bytes 2097184 | tf_op jit(solution)/shard_map/all_to_all | solution.py:221
  89.0 0.0 collective-permute-done.9.refs_3_
  89.0 0.0 collective-permute-done.10.refs_4_
  89.0 0.0 collective-permute-done.12.refs_6_
  89.1 0.0 collective-permute-done.13.refs_7_
  89.1 0.5 copy-done.6
  89.6 0.0 copy-done.7
  89.7 0.0 copy-done.8
  89.7 0.0 copy-done.9
  89.7 0.0 copy-done.10
  89.7 5.8 %back.1 = (bf16[4,256,512]{2,1,0:T(8,128)(2,1)}, f32[16,2,512]{2,1,0:T(2,128)}) custom-call(s32[4]{0:T(128)} %counts.3, bf16[4,256,512]{2,1,0:T(8,128)(2,1)} %grad.3, bf16[32,4,16,512]{3,2,1,0:T(8,128)(2,1)} %all-to-all-done.1.merged, f32[32,512]{1,0:T(8,128)} %get-tuple-element.10.refs_0_, f32[32,512]{1,0:T(8,128)} %copy-done.4, f32[32,512]{1,0:T(8,128)} %copy-done.5, ...), custom_call_target="tpu_custom_call" | custom-call | flops 1073741824 | bytes 5242880 | tf_op jit(solution)/shard_map/back/pallas_call | solution.py:194
  (28 shorter events, 0.1 us)
Async XLA Ops:
  1.9 14.0 %all-to-all-start = ((s32[32,4,16]{2,1,0:T(4,128)}), s32[32,4,16]{2,1,0:T(4,128)S(1)}, u32[]{:S(2)}, u32[]{:S(2)}) async-start(s32[32,4,16]{2,1,0:T(4,128)} %broadcast_in_dim.2), calls=%async_computation | async-start | bytes 131072 | tf_op jit(solution)/shard_map/all_to_all | solution.py:221
  15.9 8.0 %copy-start.2 = (bf16[16,2,512]{2,1,0:T(2,128)(2,1)S(1)}, bf16[16,2,512]{2,1,0:T(2,128)(2,1)}, u32[]{:S(2)}) copy-start(bf16[16,2,512]{2,1,0:T(2,128)(2,1)} %param.9) | copy-start | bytes 98308
  16.0 0.6 copy-start.1
  16.6 36.1 %all-to-all-start.2 = ((bf16[32,4,16,512]{3,2,1,0:T(8,128)(2,1)}), bf16[32,4,16,512]{3,2,1,0:T(8,128)(2,1)S(1)}, u32[]{:S(2)}, u32[]{:S(2)}) async-start(bf16[32,4,16,512]{3,2,1,0:T(8,128)(2,1)} %outer.1), calls=%async_computation.2 | async-start | bytes 4194304 | tf_op jit(solution)/shard_map/all_to_all | solution.py:221
  24.0 18.4 %copy-start.3 = (bf16[32,512]{1,0:T(8,128)(2,1)}, bf16[32,512]{1,0:T(8,128)(2,1)S(1)}, u32[]{:S(2)}) copy-start(bf16[32,512]{1,0:T(8,128)(2,1)S(1)} %reshape.22.refs_0_) | copy-start | bytes 98308
  24.0 11.8 %collective-permute-start.6 = (bf16[32,512]{1,0:T(8,128)(2,1)S(1)}, bf16[32,512]{1,0:T(8,128)(2,1)S(1)}, u32[]{:S(2)}, u32[]{:S(2)}) collective-permute-start(bf16[32,512]{1,0:T(8,128)(2,1)S(1)} %reshape.22.refs_0_), channel_id=1, source_target_pairs={{0,224},{32,0},{64,32},{96,64},{128,96},{160,128},{192,160},{224,1... | collective-permute-start | bytes 98312 | tf_op jit(solution)/shard_map/ppermute | solution.py:225
  29.6 8.3 %collective-permute-start.5 = (bf16[32,512]{1,0:T(8,128)(2,1)S(1)}, bf16[32,512]{1,0:T(8,128)(2,1)S(1)}, u32[]{:S(2)}, u32[]{:S(2)}) collective-permute-start(bf16[32,512]{1,0:T(8,128)(2,1)S(1)} %reshape.22.refs_0_), channel_id=1, source_target_pairs={{0,192},{32,224},{64,0},{96,32},{128,64},{160,96},{192,128},{224,1... | collective-permute-start | bytes 98312 | tf_op jit(solution)/shard_map/ppermute | solution.py:225
  30.8 8.5 %collective-permute-start.4 = (bf16[32,512]{1,0:T(8,128)(2,1)S(1)}, bf16[32,512]{1,0:T(8,128)(2,1)S(1)}, u32[]{:S(2)}, u32[]{:S(2)}) collective-permute-start(bf16[32,512]{1,0:T(8,128)(2,1)S(1)} %reshape.22.refs_0_), channel_id=1, source_target_pairs={{0,160},{32,192},{64,224},{96,0},{128,32},{160,64},{192,96},{224,1... | collective-permute-start | bytes 98312 | tf_op jit(solution)/shard_map/ppermute | solution.py:225
  31.3 8.0 %collective-permute-start.3 = (bf16[32,512]{1,0:T(8,128)(2,1)S(1)}, bf16[32,512]{1,0:T(8,128)(2,1)S(1)}, u32[]{:S(2)}, u32[]{:S(2)}) collective-permute-start(bf16[32,512]{1,0:T(8,128)(2,1)S(1)} %reshape.22.refs_0_), channel_id=1, source_target_pairs={{0,128},{32,160},{64,192},{96,224},{128,0},{160,32},{192,64},{224,... | collective-permute-start | bytes 98312 | tf_op jit(solution)/shard_map/ppermute | solution.py:225
  35.7 5.8 %collective-permute-start.2 = (bf16[32,512]{1,0:T(8,128)(2,1)S(1)}, bf16[32,512]{1,0:T(8,128)(2,1)S(1)}, u32[]{:S(2)}, u32[]{:S(2)}) collective-permute-start(bf16[32,512]{1,0:T(8,128)(2,1)S(1)} %reshape.22.refs_0_), channel_id=1, source_target_pairs={{0,96},{32,128},{64,160},{96,192},{128,224},{160,0},{192,32},{224,... | collective-permute-start | bytes 98312 | tf_op jit(solution)/shard_map/ppermute | solution.py:225
  35.7 6.6 %copy-start.11 = (bf16[32,512]{1,0:T(8,128)(2,1)}, bf16[32,512]{1,0:T(8,128)(2,1)S(1)}, u32[]{:S(2)}) copy-start(bf16[32,512]{1,0:T(8,128)(2,1)S(1)} %collective-permute-done.6.refs_7_) | copy-start | bytes 98308
  35.7 6.4 %collective-permute-start.1 = (bf16[32,512]{1,0:T(8,128)(2,1)S(1)}, bf16[32,512]{1,0:T(8,128)(2,1)S(1)}, u32[]{:S(2)}, u32[]{:S(2)}) collective-permute-start(bf16[32,512]{1,0:T(8,128)(2,1)S(1)} %reshape.22.refs_0_), channel_id=1, source_target_pairs={{0,64},{32,96},{64,128},{96,160},{128,192},{160,224},{192,0},{224,... | collective-permute-start | bytes 98312 | tf_op jit(solution)/shard_map/ppermute | solution.py:225
  37.9 4.4 %copy-start.12 = (bf16[32,512]{1,0:T(8,128)(2,1)}, bf16[32,512]{1,0:T(8,128)(2,1)S(1)}, u32[]{:S(2)}) copy-start(bf16[32,512]{1,0:T(8,128)(2,1)S(1)} %collective-permute-done.5.refs_6_) | copy-start | bytes 98308
  37.9 4.4 %collective-permute-start = (bf16[32,512]{1,0:T(8,128)(2,1)S(1)}, bf16[32,512]{1,0:T(8,128)(2,1)S(1)}, u32[]{:S(2)}, u32[]{:S(2)}) collective-permute-start(bf16[32,512]{1,0:T(8,128)(2,1)S(1)} %reshape.22.refs_0_), channel_id=1, source_target_pairs={{0,32},{32,64},{64,96},{96,128},{128,160},{160,192},{192,224},{224... | collective-permute-start | bytes 98312 | tf_op jit(solution)/shard_map/ppermute | solution.py:225
  39.3 3.1 %copy-start.13 = (bf16[32,512]{1,0:T(8,128)(2,1)}, bf16[32,512]{1,0:T(8,128)(2,1)S(1)}, u32[]{:S(2)}) copy-start(bf16[32,512]{1,0:T(8,128)(2,1)S(1)} %collective-permute-done.4.refs_5_) | copy-start | bytes 98308
  39.3 3.1 %copy-start.14 = (bf16[32,512]{1,0:T(8,128)(2,1)}, bf16[32,512]{1,0:T(8,128)(2,1)S(1)}, u32[]{:S(2)}) copy-start(bf16[32,512]{1,0:T(8,128)(2,1)S(1)} %collective-permute-done.3.refs_4_) | copy-start | bytes 98308
  41.5 0.9 copy-start.15
  42.2 0.6 copy-start.16
  42.3 0.6 copy-start.17
  52.7 1.4 %copy-start = (bf16[32,4,16,512]{3,2,1,0:T(8,128)(2,1)}, bf16[32,4,16,512]{3,2,1,0:T(8,128)(2,1)S(1)}, u32[]{:S(2)}) copy-start(bf16[32,4,16,512]{3,2,1,0:T(8,128)(2,1)S(1)} %all-to-all-done.2) | copy-start | bytes 6291460
  54.1 34.9 %all-to-all-start.1 = ((bf16[32,4,16,512]{3,2,1,0:T(8,128)(2,1)}), bf16[32,4,16,512]{3,2,1,0:T(8,128)(2,1)}, u32[]{:S(2)}, u32[]{:S(2)}) async-start(bf16[32,4,16,512]{3,2,1,0:T(8,128)(2,1)} %bitcast.5), calls=%async_computation.1 | async-start | bytes 4194304 | tf_op jit(solution)/shard_map/all_to_all | solution.py:221
  65.1 13.3 %collective-permute-start.7 = (f32[32,512]{1,0:T(8,128)}, f32[32,512]{1,0:T(8,128)S(1)}, u32[]{:S(2)}, u32[]{:S(2)}) collective-permute-start(f32[32,512]{1,0:T(8,128)} %get-tuple-element.11), channel_id=1, source_target_pairs={{0,32},{32,64},{64,96},{96,128},{128,160},{160,192},{192,224},{224... | collective-permute-start | bytes 196616 | tf_op jit(solution)/shard_map/ppermute | solution.py:225
  66.8 14.1 %collective-permute-start.8 = (f32[32,512]{1,0:T(8,128)}, f32[32,512]{1,0:T(8,128)S(1)}, u32[]{:S(2)}, u32[]{:S(2)}) collective-permute-start(f32[32,512]{1,0:T(8,128)} %get-tuple-element.12), channel_id=1, source_target_pairs={{0,64},{32,96},{64,128},{96,160},{128,192},{160,224},{192,0},{224,... | collective-permute-start | bytes 196616 | tf_op jit(solution)/shard_map/ppermute | solution.py:225
  69.8 19.2 %collective-permute-start.9 = (f32[32,512]{1,0:T(8,128)}, f32[32,512]{1,0:T(8,128)S(1)}, u32[]{:S(2)}, u32[]{:S(2)}) collective-permute-start(f32[32,512]{1,0:T(8,128)} %get-tuple-element.13), channel_id=1, source_target_pairs={{0,96},{32,128},{64,160},{96,192},{128,224},{160,0},{192,32},{224,... | collective-permute-start | bytes 196616 | tf_op jit(solution)/shard_map/ppermute | solution.py:225
  73.5 15.5 %collective-permute-start.10 = (f32[32,512]{1,0:T(8,128)}, f32[32,512]{1,0:T(8,128)S(1)}, u32[]{:S(2)}, u32[]{:S(2)}) collective-permute-start(f32[32,512]{1,0:T(8,128)} %get-tuple-element.14), channel_id=1, source_target_pairs={{0,128},{32,160},{64,192},{96,224},{128,0},{160,32},{192,64},{224,... | collective-permute-start | bytes 196616 | tf_op jit(solution)/shard_map/ppermute | solution.py:225
  74.0 15.1 %collective-permute-start.11 = (f32[32,512]{1,0:T(8,128)}, f32[32,512]{1,0:T(8,128)S(1)}, u32[]{:S(2)}, u32[]{:S(2)}) collective-permute-start(f32[32,512]{1,0:T(8,128)} %get-tuple-element.15), channel_id=1, source_target_pairs={{0,160},{32,192},{64,224},{96,0},{128,32},{160,64},{192,96},{224,1... | collective-permute-start | bytes 196616 | tf_op jit(solution)/shard_map/ppermute | solution.py:225
  78.4 10.6 %copy-start.4 = (f32[32,512]{1,0:T(8,128)}, f32[32,512]{1,0:T(8,128)S(1)}, u32[]{:S(2)}) copy-start(f32[32,512]{1,0:T(8,128)S(1)} %collective-permute-done.7.refs_1_) | copy-start | bytes 196612
  78.4 10.6 %collective-permute-start.12 = (f32[32,512]{1,0:T(8,128)}, f32[32,512]{1,0:T(8,128)S(1)}, u32[]{:S(2)}, u32[]{:S(2)}) collective-permute-start(f32[32,512]{1,0:T(8,128)} %get-tuple-element.16), channel_id=1, source_target_pairs={{0,192},{32,224},{64,0},{96,32},{128,64},{160,96},{192,128},{224,1... | collective-permute-start | bytes 196616 | tf_op jit(solution)/shard_map/ppermute | solution.py:225
  80.8 8.3 %copy-start.5 = (f32[32,512]{1,0:T(8,128)}, f32[32,512]{1,0:T(8,128)S(1)}, u32[]{:S(2)}) copy-start(f32[32,512]{1,0:T(8,128)S(1)} %collective-permute-done.8.refs_2_) | copy-start | bytes 196612
  80.8 8.2 %collective-permute-start.13 = (f32[32,512]{1,0:T(8,128)}, f32[32,512]{1,0:T(8,128)S(1)}, u32[]{:S(2)}, u32[]{:S(2)}) collective-permute-start(f32[32,512]{1,0:T(8,128)} %get-tuple-element.17), channel_id=1, source_target_pairs={{0,224},{32,0},{64,32},{96,64},{128,96},{160,128},{192,160},{224,1... | collective-permute-start | bytes 196616 | tf_op jit(solution)/shard_map/ppermute | solution.py:225
  89.0 0.6 copy-start.6
  89.0 0.7 copy-start.7
  89.0 0.7 copy-start.8
  89.1 0.7 copy-start.9
  89.1 0.7 copy-start.10

commit v3 on v2

v3 whole, which is shorter than its diff:
```python
import jax
import jax.numpy as jnp
from jax import lax
from jax.experimental import pallas as pl
from jax.experimental.pallas import tpu as pltpu
from jax.sharding import Mesh, PartitionSpec as P

AXES = (("z", 8), ("xl", 2), ("core", 2), ("y", 4), ("xh", 2))
NAMES = tuple(name for name, _ in AXES)
PLANE = ("xl", "y", "xh")
NZ = 8
NP = 16
NC = 2
ROWS = 2
PER = NZ * ROWS
PART = 16 * ROWS
D = 512
E = 16
K = 4
M = 256
MERGE_MIB = 62
MIX_MIB = 40
BACK_MIB = 24
F32 = jnp.float32
BF16 = jnp.bfloat16


def vmem(mib):
    return pltpu.CompilerParams(vmem_limit_bytes=mib * 1024 * 1024)


def row_of(shape, dim):
    return lax.broadcasted_iota(jnp.int32, shape, dim)


def order():
    to = row_of((D, 1), 0)
    line, core, r = (to >> 1) & (NZ - 1), (to >> 4) & 1, to & 1
    source = (line << 6) + ((to >> 8) << 5) + (core << 4) + (((to >> 5) & 7) << 1) + r
    return jnp.where(source == row_of((1, D), 1), 1.0, 0.0).astype(BF16)


def matmul(a, b, dims):
    return lax.dot_general(a, b, (dims, ((), ())), preferred_element_type=F32)


def masked_of(grad, count):
    return jnp.where(row_of((M, 1), 0) < count, grad, jnp.zeros_like(grad))


def outer_kernel(counts, x, grad, out, pick):
    k = pl.program_id(0)

    @pl.when(k == 0)
    def _():
        pick[...] = order()

    turned = matmul(pick[...], x[0], ((1,), (1,))).astype(BF16)
    masked = masked_of(grad[0], counts[k])
    product = matmul(turned, masked, ((1,), (0,)))
    out[...] = product.astype(BF16).reshape(NP, 1, NC, PER, D)


def outer(counts, x, grad):
    return pl.pallas_call(
        outer_kernel,
        grid_spec=pltpu.PrefetchScalarGridSpec(
            num_scalar_prefetch=1,
            grid=(K,),
            in_specs=[
                pl.BlockSpec((1, M, D), lambda k, c: (k, 0, 0)),
                pl.BlockSpec((1, M, D), lambda k, c: (k, 0, 0)),
            ],
            out_specs=pl.BlockSpec((NP, 1, NC, PER, D), lambda k, c: (0, k, 0, 0, 0)),
            scratch_shapes=[pltpu.VMEM((D, D), BF16)],
        ),
        out_shape=jax.ShapeDtypeStruct((NP, K, NC, PER, D), BF16),
        compiler_params=vmem(56),
        cost_estimate=pl.CostEstimate(flops=2 * K * D * D * (M + M), bytes_accessed=4 << 20, transcendentals=0),
        name="outer",
    )(counts, x, grad)


WIDTH = NZ * E * ROWS
CHIPS = 4
STEP = CHIPS * K


def spread(fixed, z, away):
    n = fixed.shape[0]
    widen = jnp.where(((row_of((E, WIDTH), 1) >> 1) & (E - 1)) == row_of((E, WIDTH), 0), 1.0, 0.0).astype(BF16)
    row = row_of((n * PER, 1), 0) & (PER - 1)
    col = row_of((1, WIDTH), 1)
    line = (z + away * (col >> 5) + NZ) & (NZ - 1)
    same = row == (line << 1) + (col & 1)
    high = (fixed >> 6).astype(F32) * (1.0 / 64.0)
    low = (fixed & 63).astype(F32) * (1.0 / 4096.0)
    parts = []
    for part in (high, low):
        wide = matmul(part.astype(BF16), widen, ((1,), (0,)))
        tall = jnp.broadcast_to(wide[:, None, :], (n, PER, WIDTH)).reshape(n * PER, WIDTH)
        parts.append(jnp.where(same, tall, 0.0).astype(BF16))
    return parts


def merge_kernel(at, fixed, *refs):
    *blocks, out, whole = refs
    core = at[1]

    @pl.when(pl.program_id(0) == 0)
    def _():
        for n, block in enumerate(blocks):
            whole[core, n * PART : (n + 1) * PART] = block[0]
            whole[1 - core, n * PART : (n + 1) * PART] = block[1]

    high, low = spread(fixed[...], at[0], -1)
    for c in range(NC):
        e = whole[c]
        total = matmul(high, e, ((1,), (0,))) + matmul(low, e, ((1,), (0,)))
        out[:, :, c] = total.astype(BF16).reshape(CHIPS, K, PER, D)


def merge(at, fixed, blocks):
    return pl.pallas_call(
        merge_kernel,
        grid_spec=pltpu.PrefetchScalarGridSpec(
            num_scalar_prefetch=1,
            grid=(NP // CHIPS,),
            in_specs=[pl.BlockSpec((STEP, E), lambda s, at: (s, 0))]
            + [pl.BlockSpec((NC, PART, D), lambda s, at: (0, 0, 0))] * NZ,
            out_specs=pl.BlockSpec((CHIPS, K, NC, PER, D), lambda s, at: (s, 0, 0, 0, 0)),
            scratch_shapes=[pltpu.VMEM((NC, WIDTH, D), BF16)],
        ),
        out_shape=jax.ShapeDtypeStruct((NP, K, NC, PER, D), BF16),
        compiler_params=vmem(MERGE_MIB),
        cost_estimate=pl.CostEstimate(flops=8 * NP * K * PER * WIDTH * D, bytes_accessed=3 << 20, transcendentals=0),
        name="merge",
    )(at, fixed, *blocks)


def mix_kernel(at, fixed, terms, mine, other, total):
    step = pl.program_id(0)
    high, low = spread(fixed[...], at[0], 1)
    for c in range(NC):
        t = terms[:, :, c].reshape(STEP * PER, D)
        part = matmul(high, t, ((0,), (0,))) + matmul(low, t, ((0,), (0,)))
        total[c] = jnp.where(step == 0, part, total[c] + part)

    @pl.when(step == pl.num_programs(0) - 1)
    def _():
        mine[...] = total[at[1]]
        other[...] = total[1 - at[1]]


def mix(at, fixed, terms):
    return pl.pallas_call(
        mix_kernel,
        grid_spec=pltpu.PrefetchScalarGridSpec(
            num_scalar_prefetch=1,
            grid=(NP // CHIPS,),
            in_specs=[
                pl.BlockSpec((STEP, E), lambda s, at: (s, 0)),
                pl.BlockSpec((CHIPS, K, NC, PER, D), lambda s, at: (s, 0, 0, 0, 0)),
            ],
            out_specs=[pl.BlockSpec((WIDTH, D), lambda s, at: (0, 0))] * 2,
            scratch_shapes=[pltpu.VMEM((NC, WIDTH, D), F32)],
        ),
        out_shape=[jax.ShapeDtypeStruct((WIDTH, D), F32)] * 2,
        compiler_params=vmem(MIX_MIB),
        cost_estimate=pl.CostEstimate(flops=8 * NP * K * PER * WIDTH * D, bytes_accessed=3 << 20, transcendentals=0),
        name="mix",
    )(at, fixed, terms)


def both_kernel(a, b, *outs):
    for n, out in enumerate(outs):
        out[...] = a[n * PART : (n + 1) * PART] + b[n * PART : (n + 1) * PART]


def both(a, b):
    return pl.pallas_call(
        both_kernel,
        out_shape=[jax.ShapeDtypeStruct((PART, D), F32)] * NZ,
        compiler_params=vmem(8),
        cost_estimate=pl.CostEstimate(flops=WIDTH * D, bytes_accessed=12 * WIDTH * D, transcendentals=0),
        name="both",
    )(a, b)


def back_kernel(counts, grad, merged, *refs):
    *sums, out, expert_grad, pick = refs
    k = pl.program_id(0)

    @pl.when(k == 0)
    def _():
        pick[...] = order()

    masked = masked_of(grad[0], counts[k])
    weights = merged[...].reshape(D, D)
    moved = matmul(masked, weights, ((1,), (1,))).astype(BF16)
    out[0] = matmul(moved, pick[...], ((1,), (0,))).astype(BF16)

    @pl.when(k == K - 1)
    def _():
        total = sums[0][...]
        for part in sums[1:]:
            total += part[...]
        for e in range(E):
            expert_grad[e] = total[ROWS * e : ROWS * (e + 1)]


def back(counts, grad, merged, sums):
    return pl.pallas_call(
        back_kernel,
        grid_spec=pltpu.PrefetchScalarGridSpec(
            num_scalar_prefetch=1,
            grid=(K,),
            in_specs=[
                pl.BlockSpec((1, M, D), lambda k, c: (k, 0, 0)),
                pl.BlockSpec((NP, 1, NC, PER, D), lambda k, c: (0, k, 0, 0, 0)),
            ]
            + [pl.BlockSpec((PART, D), lambda k, c: (0, 0))] * NZ,
            out_specs=[
                pl.BlockSpec((1, M, D), lambda k, c: (k, 0, 0)),
                pl.BlockSpec((E, ROWS, D), lambda k, c: (0, 0, 0)),
            ],
            scratch_shapes=[pltpu.VMEM((D, D), BF16)],
        ),
        out_shape=[
            jax.ShapeDtypeStruct((K, M, D), BF16),
            jax.ShapeDtypeStruct((E, ROWS, D), F32),
        ],
        compiler_params=vmem(BACK_MIB),
        cost_estimate=pl.CostEstimate(flops=4 * K * M * D * D, bytes_accessed=5 << 20, transcendentals=0),
        name="back",
    )(counts, grad, merged, *sums)


def swap(array, axes):
    return lax.all_to_all(array, axes, 0, 0, tiled=True)


def along_z(array, by):
    return lax.ppermute(array, "z", [(i, (i + by) % NZ) for i in range(NZ)])


def across(array):
    return lax.ppermute(array, "core", [(0, 1), (1, 0)])


def shards(inputs, out_grad, coeff_fixed, atom_counts, experts):
    at = jnp.stack([lax.axis_index("z"), lax.axis_index("core")]).astype(jnp.int32)
    fixed = swap(jnp.broadcast_to(coeff_fixed[None], (NP, K, E)), PLANE).reshape(NP * K, E)
    own = experts.reshape(PART, D)
    pair = jnp.stack([own, across(own)])
    rows = [pair] + [along_z(pair, n) for n in range(1, NZ)]
    terms = swap(outer(atom_counts, inputs, out_grad), PLANE)
    merged = swap(merge(at, fixed, rows), PLANE)
    mine, other = mix(at, fixed, terms)
    mixed = both(mine, across(other))
    sums = [mixed[0]] + [along_z(mixed[n], n) for n in range(1, NZ)]
    return tuple(back(atom_counts, out_grad, merged, sums))


def solution(mesh):
    split = Mesh(mesh.devices.reshape([size for _, size in AXES]), NAMES)
    placed = (
        P(NAMES, None, None),
        P(NAMES, None, None),
        P(NAMES, None),
        P(NAMES),
        P(None, NAMES, None),
    )
    return jax.shard_map(
        shards,
        mesh=split,
        in_specs=placed,
        out_specs=(P(NAMES, None, None), P(None, NAMES, None)),
        check_vma=False,
    )
```

time: 97.2 us -> 99.8 us (1.027)
  the two profiles are of different devices: /device:TPU:9 before, /device:TPU:64 now
where the time goes in v3:
time: 99.8 us; the launch traced here: 99 us
  starting transfers between devices  48.6 us (49%)
  waiting for transfers between devices  25.3 us (25%)
  Pallas kernels  21.6 us (22%)
  local copies, waits for them, and re-layouts  1.97 us (2%)
    ppermute x14, starting transfers between devices, along_z(): return lax.ppermute(array, 'z', [(i, (i + by) % NZ) for i in range(NZ)])  28.4 us
    all_to_all x3, starting transfers between devices, swap(): return lax.all_to_all(array, axes, 0, 0, tiled=True)  20 us
    all_to_all x3, waiting for transfers between devices, swap(): return lax.all_to_all(array, axes, 0, 0, tiled=True)  16 us
    ppermute x14, waiting for transfers between devices, along_z(): return lax.ppermute(array, 'z', [(i, (i + by) % NZ) for i in range(NZ)])  6.31 us
    pallas_call x1, Pallas kernels, outer(): pl.pallas_call(outer_kernel, grid_spec=pltpu.PrefetchScalarGridSpec(num_s...  6.2 us
    pallas_call x1, Pallas kernels, merge(): pl.pallas_call(merge_kernel, grid_spec=pltpu.PrefetchScalarGridSpec(num_s...  5.19 us
    pallas_call x1, Pallas kernels, back(): pl.pallas_call(back_kernel, grid_spec=pltpu.PrefetchScalarGridSpec(num_sc...  4.99 us
    pallas_call x1, Pallas kernels, mix(): pl.pallas_call(mix_kernel, grid_spec=pltpu.PrefetchScalarGridSpec(num_sca...  4.56 us
  transfers between devices with their start and end apart: 19, of which 7 were waited for; matrix products, arithmetic and copies ran while one was open for 1% of the time, Pallas kernels for 17%

profile of v3, /device:TPU:64, one launch (start us, length us, event | category | flops | bytes accessed | tf_op | source)
XLA Modules:
  0.0 99.0 jit_solution(1616531054917211451)
XLA Ops:
  0.6 1.3 %broadcast_in_dim.2 = s32[16,4,16]{2,1,0:T(4,128)} broadcast(s32[4,16]{1,0:T(4,128)} %param.7), dimensions={1,2} | broadcast | bytes 4352 | tf_op jit(solution)/shard_map/broadcast_in_dim | solution.py:253
  1.9 7.0 %all-to-all-start = ((s32[16,4,16]{2,1,0:T(4,128)}), s32[16,4,16]{2,1,0:T(4,128)S(1)}, u32[]{:S(2)}, u32[]{:S(2)}) async-start(s32[16,4,16]{2,1,0:T(4,128)} %broadcast_in_dim.2), calls=%async_computation | async-start | bytes 65536 | tf_op jit(solution)/shard_map/all_to_all | solution.py:240
  9.0 6.2 %outer.1 = bf16[16,4,2,16,512]{4,3,2,1,0:T(8,128)(2,1)} custom-call(s32[4]{0:T(128)} %counts.3, bf16[4,256,512]{2,1,0:T(8,128)(2,1)} %x.1, bf16[4,256,512]{2,1,0:T(8,128)(2,1)} %grad.3), custom_call_target="tpu_custom_call" | custom-call | flops 1073741824 | bytes 4194304 | tf_op jit(solution)/shard_map/outer/pallas_call | solution.py:65
  15.2 1.5 %all-to-all-done = s32[16,4,16]{2,1,0:T(4,128)S(1)} async-done(((s32[16,4,16]{2,1,0:T(4,128)}), s32[16,4,16]{2,1,0:T(4,128)S(1)}, u32[]{:S(2)}, u32[]{:S(2)}) %all-to-all-start) | async-done | bytes 4128 | tf_op jit(solution)/shard_map/all_to_all | solution.py:240
  16.7 5.8 %all-to-all-start.2 = ((bf16[16,4,2,16,512]{4,3,2,1,0:T(8,128)(2,1)}), bf16[16,4,2,16,512]{4,3,2,1,0:T(8,128)(2,1)}, u32[]{:S(2)}, u32[]{:S(2)}) async-start(bf16[16,4,2,16,512]{4,3,2,1,0:T(8,128)(2,1)} %outer.1), calls=%async_computation.2 | async-start | bytes 4194304 | tf_op jit(solution)/shard_map/all_to_all | solution.py:240
  22.5 0.1 collective-permute-start
  22.6 1.2 %collective-permute-done = bf16[32,512]{1,0:T(8,128)(2,1)S(1)} collective-permute-done((bf16[32,512]{1,0:T(8,128)(2,1)S(1)}, bf16[32,512]{1,0:T(8,128)(2,1)S(1)}, u32[]{:S(2)}, u32[]{:S(2)}) %collective-permute-start) | collective-permute-done | bytes 32800 | tf_op jit(solution)/shard_map/ppermute | solution.py:248
  23.8 0.0 copy-start.6
  23.8 0.2 collective-permute-start.7
  24.0 5.4 %collective-permute-start.6 = (bf16[2,32,512]{2,1,0:T(8,128)(2,1)S(1)}, bf16[2,32,512]{2,1,0:T(8,128)(2,1)S(1)}, u32[]{:S(2)}, u32[]{:S(2)}) collective-permute-start(bf16[2,32,512]{2,1,0:T(8,128)(2,1)S(1)} %pad_maximum_fusion.refs_0_), channel_id=1, source_target_pairs={{0,192},{32,224},{64,0},{96,32},{128,64},{160,96},{192,128},{224,1... | collective-permute-start | bytes 196616 | tf_op jit(solution)/shard_map/ppermute | solution.py:244
  29.4 1.9 %collective-permute-start.5 = (bf16[2,32,512]{2,1,0:T(8,128)(2,1)S(1)}, bf16[2,32,512]{2,1,0:T(8,128)(2,1)S(1)}, u32[]{:S(2)}, u32[]{:S(2)}) collective-permute-start(bf16[2,32,512]{2,1,0:T(8,128)(2,1)S(1)} %pad_maximum_fusion.refs_0_), channel_id=1, source_target_pairs={{0,160},{32,192},{64,224},{96,0},{128,32},{160,64},{192,96},{224,1... | collective-permute-start | bytes 196616 | tf_op jit(solution)/shard_map/ppermute | solution.py:244
  31.3 0.0 collective-permute-start.4
  31.3 4.6 %collective-permute-start.3 = (bf16[2,32,512]{2,1,0:T(8,128)(2,1)S(1)}, bf16[2,32,512]{2,1,0:T(8,128)(2,1)S(1)}, u32[]{:S(2)}, u32[]{:S(2)}) collective-permute-start(bf16[2,32,512]{2,1,0:T(8,128)(2,1)S(1)} %pad_maximum_fusion.refs_0_), channel_id=1, source_target_pairs={{0,96},{32,128},{64,160},{96,192},{128,224},{160,0},{192,32},{224,... | collective-permute-start | bytes 196616 | tf_op jit(solution)/shard_map/ppermute | solution.py:244
  35.9 0.0 collective-permute-done.7.refs_7_
  35.9 2.4 %collective-permute-start.2 = (bf16[2,32,512]{2,1,0:T(8,128)(2,1)S(1)}, bf16[2,32,512]{2,1,0:T(8,128)(2,1)S(1)}, u32[]{:S(2)}, u32[]{:S(2)}) collective-permute-start(bf16[2,32,512]{2,1,0:T(8,128)(2,1)S(1)} %pad_maximum_fusion.refs_0_), channel_id=1, source_target_pairs={{0,64},{32,96},{64,128},{96,160},{128,192},{160,224},{192,0},{224,... | collective-permute-start | bytes 196616 | tf_op jit(solution)/shard_map/ppermute | solution.py:244
  38.3 0.0 collective-permute-done.6.refs_6_
  38.3 2.2 %collective-permute-start.1 = (bf16[2,32,512]{2,1,0:T(8,128)(2,1)S(1)}, bf16[2,32,512]{2,1,0:T(8,128)(2,1)S(1)}, u32[]{:S(2)}, u32[]{:S(2)}) collective-permute-start(bf16[2,32,512]{2,1,0:T(8,128)(2,1)S(1)} %pad_maximum_fusion.refs_0_), channel_id=1, source_target_pairs={{0,32},{32,64},{64,96},{96,128},{128,160},{160,192},{192,224},{224... | collective-permute-start | bytes 196616 | tf_op jit(solution)/shard_map/ppermute | solution.py:244
  40.5 0.7 pad_add_fusion.at
  41.2 0.0 collective-permute-done.5.refs_5_
  41.2 1.9 %collective-permute-done.4.refs_4_ = bf16[2,32,512]{2,1,0:T(8,128)(2,1)S(1)} collective-permute-done((bf16[2,32,512]{2,1,0:T(8,128)(2,1)S(1)}, bf16[2,32,512]{2,1,0:T(8,128)(2,1)S(1)}, u32[]{:S(2)}, u32[]{:S(2)}) %collective-permute-start.4) | collective-permute-done | bytes 65568 | tf_op jit(solution)/shard_map/ppermute | solution.py:244
  43.1 0.0 collective-permute-done.3.refs_3_
  43.1 3.6 %collective-permute-done.2.refs_2_ = bf16[2,32,512]{2,1,0:T(8,128)(2,1)S(1)} collective-permute-done((bf16[2,32,512]{2,1,0:T(8,128)(2,1)S(1)}, bf16[2,32,512]{2,1,0:T(8,128)(2,1)S(1)}, u32[]{:S(2)}, u32[]{:S(2)}) %collective-permute-start.2) | collective-permute-done | bytes 65568 | tf_op jit(solution)/shard_map/ppermute | solution.py:244
  46.7 0.8 collective-permute-done.1.refs_1_
  47.5 0.6 copy-done.13
  48.1 5.2 %merge.1 = bf16[16,4,2,16,512]{4,3,2,1,0:T(8,128)(2,1)} custom-call(s32[2]{0:T(128)} %pad_add_fusion.at, s32[64,16]{1,0:T(8,128)} %bitcast.4, bf16[2,32,512]{2,1,0:T(8,128)(2,1)} %copy-done.6, bf16[2,32,512]{2,1,0:T(8,128)(2,1)} %copy-done.13, bf16[2,32,512]{2,1,0:T(8,128)(2,1)} %copy-done.12, bf16[2,32,512]{2,1,0:T(8,128)(2,1)} %copy-done.11, ...), custom_call_target="tpu_custom_call" | custom-call | flops 1073741824 | bytes 3145728 | tf_op jit(solution)/shard_map/merge/pallas_call | solution.py:124
  53.3 0.0 all-to-all-done.2.terms
  53.3 7.2 %all-to-all-start.1 = ((bf16[16,4,2,16,512]{4,3,2,1,0:T(8,128)(2,1)}), bf16[16,4,2,16,512]{4,3,2,1,0:T(8,128)(2,1)S(1)}, u32[]{:S(2)}, u32[]{:S(2)}) async-start(bf16[16,4,2,16,512]{4,3,2,1,0:T(8,128)(2,1)} %merge.1), calls=%async_computation.1 | async-start | bytes 4194304 | tf_op jit(solution)/shard_map/all_to_all | solution.py:240
  60.5 0.0 copy-start
  60.5 0.0 copy-start.3
  60.5 4.6 %mix.1 = (f32[256,512]{1,0:T(8,128)S(1)}, f32[256,512]{1,0:T(8,128)S(1)}) custom-call(s32[2]{0:T(128)S(1)} %copy-done.4, s32[64,16]{1,0:T(8,128)S(1)} %bitcast.5, bf16[16,4,2,16,512]{4,3,2,1,0:T(8,128)(2,1)} %all-to-all-done.2.terms), custom_call_target="tpu_custom_call" | custom-call | flops 1073741824 | bytes 3145728 | tf_op jit(solution)/shard_map/mix/pallas_call | solution.py:156
  65.1 0.1 collective-permute-start.8
  65.2 1.9 %collective-permute-done.8.b = f32[256,512]{1,0:T(8,128)S(1)} collective-permute-done((f32[256,512]{1,0:T(8,128)S(1)}, f32[256,512]{1,0:T(8,128)S(1)}, u32[]{:S(2)}, u32[]{:S(2)}) %collective-permute-start.8) | collective-permute-done | bytes 524320 | tf_op jit(solution)/shard_map/ppermute | solution.py:248
  67.1 0.7 both.1
  67.8 0.4 collective-permute-start.9
  68.2 2.1 %collective-permute-start.10 = (f32[32,512]{1,0:T(8,128)S(1)}, f32[32,512]{1,0:T(8,128)S(1)}, u32[]{:S(2)}, u32[]{:S(2)}) collective-permute-start(f32[32,512]{1,0:T(8,128)S(1)} %get-tuple-element.16), channel_id=1, source_target_pairs={{0,64},{32,96},{64,128},{96,160},{128,192},{160,224},{192,0},{224,... | collective-permute-start | bytes 196616 | tf_op jit(solution)/shard_map/ppermute | solution.py:244
  70.4 2.6 %collective-permute-start.11 = (f32[32,512]{1,0:T(8,128)}, f32[32,512]{1,0:T(8,128)}, u32[]{:S(2)}, u32[]{:S(2)}) collective-permute-start(f32[32,512]{1,0:T(8,128)} %get-tuple-element.17), channel_id=1, source_target_pairs={{0,96},{32,128},{64,160},{96,192},{128,224},{160,0},{192,32},{224,... | collective-permute-start | bytes 196616 | tf_op jit(solution)/shard_map/ppermute | solution.py:244
  72.9 3.5 %collective-permute-start.12 = (f32[32,512]{1,0:T(8,128)}, f32[32,512]{1,0:T(8,128)}, u32[]{:S(2)}, u32[]{:S(2)}) collective-permute-start(f32[32,512]{1,0:T(8,128)} %get-tuple-element.18), channel_id=1, source_target_pairs={{0,128},{32,160},{64,192},{96,224},{128,0},{160,32},{192,64},{224,... | collective-permute-start | bytes 196616 | tf_op jit(solution)/shard_map/ppermute | solution.py:244
  76.5 2.0 %collective-permute-start.13 = (f32[32,512]{1,0:T(8,128)}, f32[32,512]{1,0:T(8,128)}, u32[]{:S(2)}, u32[]{:S(2)}) collective-permute-start(f32[32,512]{1,0:T(8,128)} %get-tuple-element.19), channel_id=1, source_target_pairs={{0,160},{32,192},{64,224},{96,0},{128,32},{160,64},{192,96},{224,1... | collective-permute-start | bytes 196616 | tf_op jit(solution)/shard_map/ppermute | solution.py:244
  78.5 0.0 collective-permute-done.9.refs_1_
  78.5 0.4 collective-permute-start.14
  78.9 0.0 collective-permute-done.10.refs_2_
  78.9 0.6 collective-permute-start.15
  79.5 14.4 %all-to-all-done.1.merged = bf16[16,4,2,16,512]{4,3,2,1,0:T(8,128)(2,1)S(1)} async-done(((bf16[16,4,2,16,512]{4,3,2,1,0:T(8,128)(2,1)}), bf16[16,4,2,16,512]{4,3,2,1,0:T(8,128)(2,1)S(1)}, u32[]{:S(2)}, u32[]{:S(2)}) %all-to-all-start.1) | async-done | bytes 2097184 | tf_op jit(solution)/shard_map/all_to_all | solution.py:240
  94.0 0.0 collective-permute-done.11.refs_3_
  94.0 0.0 collective-permute-done.12.refs_4_
  94.0 0.0 collective-permute-done.13.refs_5_
  94.0 0.0 collective-permute-done.14.refs_6_
  94.0 5.0 %back.1 = (bf16[4,256,512]{2,1,0:T(8,128)(2,1)}, f32[16,2,512]{2,1,0:T(2,128)}) custom-call(s32[4]{0:T(128)S(1)} %copy-done.3, bf16[4,256,512]{2,1,0:T(8,128)(2,1)S(1)} %copy-done, bf16[16,4,2,16,512]{4,3,2,1,0:T(8,128)(2,1)S(1)} %all-to-all-done.1.merged, f32[32,512]{1,0:T(8,128)S(1)} %get-tuple-element.14.refs_0_, ...), custom_call_target="tpu_custom_call" | custom-call | flops 1073741824 | bytes 5242880 | tf_op jit(solution)/shard_map/back/pallas_call | solution.py:213
  (28 shorter events, 0.1 us)
Async XLA Ops:
  1.9 14.8 %all-to-all-start = ((s32[16,4,16]{2,1,0:T(4,128)}), s32[16,4,16]{2,1,0:T(4,128)S(1)}, u32[]{:S(2)}, u32[]{:S(2)}) async-start(s32[16,4,16]{2,1,0:T(4,128)} %broadcast_in_dim.2), calls=%async_computation | async-start | bytes 65536 | tf_op jit(solution)/shard_map/all_to_all | solution.py:240
  15.2 7.3 %copy-start.5 = (bf16[16,2,512]{2,1,0:T(2,128)(2,1)S(1)}, bf16[16,2,512]{2,1,0:T(2,128)(2,1)}, u32[]{:S(2)}) copy-start(bf16[16,2,512]{2,1,0:T(2,128)(2,1)} %param.9) | copy-start | bytes 98308
  16.7 5.8 %copy-start.1 = (s32[16,4,16]{2,1,0:T(4,128)}, s32[16,4,16]{2,1,0:T(4,128)S(1)}, u32[]{:S(2)}) copy-start(s32[16,4,16]{2,1,0:T(4,128)S(1)} %all-to-all-done) | copy-start | bytes 12292
  16.7 36.6 %all-to-all-start.2 = ((bf16[16,4,2,16,512]{4,3,2,1,0:T(8,128)(2,1)}), bf16[16,4,2,16,512]{4,3,2,1,0:T(8,128)(2,1)}, u32[]{:S(2)}, u32[]{:S(2)}) async-start(bf16[16,4,2,16,512]{4,3,2,1,0:T(8,128)(2,1)} %outer.1), calls=%async_computation.2 | async-start | bytes 4194304 | tf_op jit(solution)/shard_map/all_to_all | solution.py:240
  22.5 1.3 %collective-permute-start = (bf16[32,512]{1,0:T(8,128)(2,1)S(1)}, bf16[32,512]{1,0:T(8,128)(2,1)S(1)}, u32[]{:S(2)}, u32[]{:S(2)}) collective-permute-start(bf16[32,512]{1,0:T(8,128)(2,1)S(1)} %reshape.12), channel_id=1, source_target_pairs={{0,8},{8,0},{1,9},{9,1},{2,10},{10,2},{3,11},{11,3},{4,12},{12,4},... | collective-permute-start | bytes 98312 | tf_op jit(solution)/shard_map/ppermute | solution.py:248
  23.8 23.7 %copy-start.6 = (bf16[2,32,512]{2,1,0:T(8,128)(2,1)}, bf16[2,32,512]{2,1,0:T(8,128)(2,1)S(1)}, u32[]{:S(2)}) copy-start(bf16[2,32,512]{2,1,0:T(8,128)(2,1)S(1)} %pad_maximum_fusion.refs_0_) | copy-start | bytes 196612
  23.8 12.1 %collective-permute-start.7 = (bf16[2,32,512]{2,1,0:T(8,128)(2,1)S(1)}, bf16[2,32,512]{2,1,0:T(8,128)(2,1)S(1)}, u32[]{:S(2)}, u32[]{:S(2)}) collective-permute-start(bf16[2,32,512]{2,1,0:T(8,128)(2,1)S(1)} %pad_maximum_fusion.refs_0_), channel_id=1, source_target_pairs={{0,224},{32,0},{64,32},{96,64},{128,96},{160,128},{192,160},{224,1... | collective-permute-start | bytes 196616 | tf_op jit(solution)/shard_map/ppermute | solution.py:244
  24.0 14.3 %collective-permute-start.6 = (bf16[2,32,512]{2,1,0:T(8,128)(2,1)S(1)}, bf16[2,32,512]{2,1,0:T(8,128)(2,1)S(1)}, u32[]{:S(2)}, u32[]{:S(2)}) collective-permute-start(bf16[2,32,512]{2,1,0:T(8,128)(2,1)S(1)} %pad_maximum_fusion.refs_0_), channel_id=1, source_target_pairs={{0,192},{32,224},{64,0},{96,32},{128,64},{160,96},{192,128},{224,1... | collective-permute-start | bytes 196616 | tf_op jit(solution)/shard_map/ppermute | solution.py:244
  29.4 11.8 %collective-permute-start.5 = (bf16[2,32,512]{2,1,0:T(8,128)(2,1)S(1)}, bf16[2,32,512]{2,1,0:T(8,128)(2,1)S(1)}, u32[]{:S(2)}, u32[]{:S(2)}) collective-permute-start(bf16[2,32,512]{2,1,0:T(8,128)(2,1)S(1)} %pad_maximum_fusion.refs_0_), channel_id=1, source_target_pairs={{0,160},{32,192},{64,224},{96,0},{128,32},{160,64},{192,96},{224,1... | collective-permute-start | bytes 196616 | tf_op jit(solution)/shard_map/ppermute | solution.py:244
  31.3 11.7 %collective-permute-start.4 = (bf16[2,32,512]{2,1,0:T(8,128)(2,1)S(1)}, bf16[2,32,512]{2,1,0:T(8,128)(2,1)S(1)}, u32[]{:S(2)}, u32[]{:S(2)}) collective-permute-start(bf16[2,32,512]{2,1,0:T(8,128)(2,1)S(1)} %pad_maximum_fusion.refs_0_), channel_id=1, source_target_pairs={{0,128},{32,160},{64,192},{96,224},{128,0},{160,32},{192,64},{224,... | collective-permute-start | bytes 196616 | tf_op jit(solution)/shard_map/ppermute | solution.py:244
  31.3 11.7 %collective-permute-start.3 = (bf16[2,32,512]{2,1,0:T(8,128)(2,1)S(1)}, bf16[2,32,512]{2,1,0:T(8,128)(2,1)S(1)}, u32[]{:S(2)}, u32[]{:S(2)}) collective-permute-start(bf16[2,32,512]{2,1,0:T(8,128)(2,1)S(1)} %pad_maximum_fusion.refs_0_), channel_id=1, source_target_pairs={{0,96},{32,128},{64,160},{96,192},{128,224},{160,0},{192,32},{224,... | collective-permute-start | bytes 196616 | tf_op jit(solution)/shard_map/ppermute | solution.py:244
  35.9 11.6 %copy-start.7 = (bf16[2,32,512]{2,1,0:T(8,128)(2,1)}, bf16[2,32,512]{2,1,0:T(8,128)(2,1)S(1)}, u32[]{:S(2)}) copy-start(bf16[2,32,512]{2,1,0:T(8,128)(2,1)S(1)} %collective-permute-done.7.refs_7_) | copy-start | bytes 196612
  35.9 10.8 %collective-permute-start.2 = (bf16[2,32,512]{2,1,0:T(8,128)(2,1)S(1)}, bf16[2,32,512]{2,1,0:T(8,128)(2,1)S(1)}, u32[]{:S(2)}, u32[]{:S(2)}) collective-permute-start(bf16[2,32,512]{2,1,0:T(8,128)(2,1)S(1)} %pad_maximum_fusion.refs_0_), channel_id=1, source_target_pairs={{0,64},{32,96},{64,128},{96,160},{128,192},{160,224},{192,0},{224,... | collective-permute-start | bytes 196616 | tf_op jit(solution)/shard_map/ppermute | solution.py:244
  38.3 9.2 %copy-start.8 = (bf16[2,32,512]{2,1,0:T(8,128)(2,1)}, bf16[2,32,512]{2,1,0:T(8,128)(2,1)S(1)}, u32[]{:S(2)}) copy-start(bf16[2,32,512]{2,1,0:T(8,128)(2,1)S(1)} %collective-permute-done.6.refs_6_) | copy-start | bytes 196612
  38.3 9.2 %collective-permute-start.1 = (bf16[2,32,512]{2,1,0:T(8,128)(2,1)S(1)}, bf16[2,32,512]{2,1,0:T(8,128)(2,1)S(1)}, u32[]{:S(2)}, u32[]{:S(2)}) collective-permute-start(bf16[2,32,512]{2,1,0:T(8,128)(2,1)S(1)} %pad_maximum_fusion.refs_0_), channel_id=1, source_target_pairs={{0,32},{32,64},{64,96},{96,128},{128,160},{160,192},{192,224},{224... | collective-permute-start | bytes 196616 | tf_op jit(solution)/shard_map/ppermute | solution.py:244
  41.2 6.3 %copy-start.9 = (bf16[2,32,512]{2,1,0:T(8,128)(2,1)}, bf16[2,32,512]{2,1,0:T(8,128)(2,1)S(1)}, u32[]{:S(2)}) copy-start(bf16[2,32,512]{2,1,0:T(8,128)(2,1)S(1)} %collective-permute-done.5.refs_5_) | copy-start | bytes 196612
  43.1 4.4 %copy-start.10 = (bf16[2,32,512]{2,1,0:T(8,128)(2,1)}, bf16[2,32,512]{2,1,0:T(8,128)(2,1)S(1)}, u32[]{:S(2)}) copy-start(bf16[2,32,512]{2,1,0:T(8,128)(2,1)S(1)} %collective-permute-done.4.refs_4_) | copy-start | bytes 196612
  43.1 4.4 %copy-start.11 = (bf16[2,32,512]{2,1,0:T(8,128)(2,1)}, bf16[2,32,512]{2,1,0:T(8,128)(2,1)S(1)}, u32[]{:S(2)}) copy-start(bf16[2,32,512]{2,1,0:T(8,128)(2,1)S(1)} %collective-permute-done.3.refs_3_) | copy-start | bytes 196612
  46.7 0.9 copy-start.12
  47.5 0.6 copy-start.13
  53.3 7.2 %copy-start.2 = (s32[16,4,16]{2,1,0:T(4,128)S(1)}, s32[16,4,16]{2,1,0:T(4,128)}, u32[]{:S(2)}) copy-start(s32[16,4,16]{2,1,0:T(4,128)} %copy-done.1) | copy-start | bytes 12292
  53.3 7.2 %copy-start.4 = (s32[2]{0:T(128)S(1)}, s32[2]{0:T(128)}, u32[]{:S(2)}) copy-start(s32[2]{0:T(128)} %pad_add_fusion.at) | copy-start | bytes 28
  53.3 40.7 %all-to-all-start.1 = ((bf16[16,4,2,16,512]{4,3,2,1,0:T(8,128)(2,1)}), bf16[16,4,2,16,512]{4,3,2,1,0:T(8,128)(2,1)S(1)}, u32[]{:S(2)}, u32[]{:S(2)}) async-start(bf16[16,4,2,16,512]{4,3,2,1,0:T(8,128)(2,1)} %merge.1), calls=%async_computation.1 | async-start | bytes 4194304 | tf_op jit(solution)/shard_map/all_to_all | solution.py:240
  60.5 33.5 %copy-start = (bf16[4,256,512]{2,1,0:T(8,128)(2,1)S(1)}, bf16[4,256,512]{2,1,0:T(8,128)(2,1)}, u32[]{:S(2)}) copy-start(bf16[4,256,512]{2,1,0:T(8,128)(2,1)} %grad.3) | copy-start | bytes 3145732
  60.5 33.5 %copy-start.3 = (s32[4]{0:T(128)S(1)}, s32[4]{0:T(128)}, u32[]{:S(2)}) copy-start(s32[4]{0:T(128)} %counts.3) | copy-start | bytes 52
  65.1 2.0 %collective-permute-start.8 = (f32[256,512]{1,0:T(8,128)S(1)}, f32[256,512]{1,0:T(8,128)S(1)}, u32[]{:S(2)}, u32[]{:S(2)}) collective-permute-start(f32[256,512]{1,0:T(8,128)S(1)} %get-tuple-element.13), channel_id=1, source_target_pairs={{0,8},{8,0},{1,9},{9,1},{2,10},{10,2},{3,11},{11,3},{4,12},{12,4},... | collective-permute-start | bytes 1572872 | tf_op jit(solution)/shard_map/ppermute | solution.py:248
  67.8 10.7 %collective-permute-start.9 = (f32[32,512]{1,0:T(8,128)S(1)}, f32[32,512]{1,0:T(8,128)S(1)}, u32[]{:S(2)}, u32[]{:S(2)}) collective-permute-start(f32[32,512]{1,0:T(8,128)S(1)} %get-tuple-element.15), channel_id=1, source_target_pairs={{0,32},{32,64},{64,96},{96,128},{128,160},{160,192},{192,224},{224... | collective-permute-start | bytes 196616 | tf_op jit(solution)/shard_map/ppermute | solution.py:244
  68.2 10.7 %collective-permute-start.10 = (f32[32,512]{1,0:T(8,128)S(1)}, f32[32,512]{1,0:T(8,128)S(1)}, u32[]{:S(2)}, u32[]{:S(2)}) collective-permute-start(f32[32,512]{1,0:T(8,128)S(1)} %get-tuple-element.16), channel_id=1, source_target_pairs={{0,64},{32,96},{64,128},{96,160},{128,192},{160,224},{192,0},{224,... | collective-permute-start | bytes 196616 | tf_op jit(solution)/shard_map/ppermute | solution.py:244
  70.4 23.6 %collective-permute-start.11 = (f32[32,512]{1,0:T(8,128)}, f32[32,512]{1,0:T(8,128)}, u32[]{:S(2)}, u32[]{:S(2)}) collective-permute-start(f32[32,512]{1,0:T(8,128)} %get-tuple-element.17), channel_id=1, source_target_pairs={{0,96},{32,128},{64,160},{96,192},{128,224},{160,0},{192,32},{224,... | collective-permute-start | bytes 196616 | tf_op jit(solution)/shard_map/ppermute | solution.py:244
  72.9 21.0 %collective-permute-start.12 = (f32[32,512]{1,0:T(8,128)}, f32[32,512]{1,0:T(8,128)}, u32[]{:S(2)}, u32[]{:S(2)}) collective-permute-start(f32[32,512]{1,0:T(8,128)} %get-tuple-element.18), channel_id=1, source_target_pairs={{0,128},{32,160},{64,192},{96,224},{128,0},{160,32},{192,64},{224,... | collective-permute-start | bytes 196616 | tf_op jit(solution)/shard_map/ppermute | solution.py:244
  76.5 17.5 %collective-permute-start.13 = (f32[32,512]{1,0:T(8,128)}, f32[32,512]{1,0:T(8,128)}, u32[]{:S(2)}, u32[]{:S(2)}) collective-permute-start(f32[32,512]{1,0:T(8,128)} %get-tuple-element.19), channel_id=1, source_target_pairs={{0,160},{32,192},{64,224},{96,0},{128,32},{160,64},{192,96},{224,1... | collective-permute-start | bytes 196616 | tf_op jit(solution)/shard_map/ppermute | solution.py:244
  78.5 15.5 %collective-permute-start.14 = (f32[32,512]{1,0:T(8,128)S(1)}, f32[32,512]{1,0:T(8,128)}, u32[]{:S(2)}, u32[]{:S(2)}) collective-permute-start(f32[32,512]{1,0:T(8,128)S(1)} %get-tuple-element.20), channel_id=1, source_target_pairs={{0,192},{32,224},{64,0},{96,32},{128,64},{160,96},{192,128},{224,1... | collective-permute-start | bytes 196616 | tf_op jit(solution)/shard_map/ppermute | solution.py:244
  78.9 15.1 %collective-permute-start.15 = (f32[32,512]{1,0:T(8,128)S(1)}, f32[32,512]{1,0:T(8,128)}, u32[]{:S(2)}, u32[]{:S(2)}) collective-permute-start(f32[32,512]{1,0:T(8,128)S(1)} %get-tuple-element.21), channel_id=1, source_target_pairs={{0,224},{32,0},{64,32},{96,64},{128,96},{160,128},{192,160},{224,1... | collective-permute-start | bytes 196616 | tf_op jit(solution)/shard_map/ppermute | solution.py:244

commit v4 on v2

v4 whole, which is shorter than its diff:
```python
import jax
import jax.numpy as jnp
from jax import lax
from jax.experimental import pallas as pl
from jax.experimental.pallas import tpu as pltpu
from jax.sharding import Mesh, PartitionSpec as P

AXES = (("z", 8), ("xl", 2), ("core", 2), ("y", 4), ("xh", 2))
NAMES = tuple(name for name, _ in AXES)
PLANE = ("xl", "core", "y", "xh")
NZ = 8
NG = 32
ROWS = 2
PER = NZ * ROWS
D = 512
E = 16
K = 4
M = 256
STACK_MIB = 62
MERGE_MIB = 60
MIX_MIB = 56
BACK_MIB = 24
F32 = jnp.float32
BF16 = jnp.bfloat16
LANES = 128
TILES = D // LANES
PART = E * ROWS
WIDTH = NZ * PART
CARD = K * TILES
GROUP = 8
STEP = GROUP * K


def vmem(mib):
    return pltpu.CompilerParams(vmem_limit_bytes=mib * 1024 * 1024)


def row_of(shape, dim):
    return lax.broadcasted_iota(jnp.int32, shape, dim)


def order():
    to = row_of((D, 1), 0)
    source = (((to >> 1) & (NZ - 1)) << 6) + ((to >> 4) << 1) + (to & 1)
    return jnp.where(source == row_of((1, D), 1), 1.0, 0.0).astype(BF16)


def matmul(a, b, dims):
    return lax.dot_general(a, b, (dims, ((), ())), preferred_element_type=F32)


def masked_of(grad, count):
    return jnp.where(row_of((M, 1), 0) < count, grad, jnp.zeros_like(grad))


def card(fixed):
    lane = row_of((E, LANES), 1)
    row = row_of((E, LANES), 0)
    high = (fixed >> 6).astype(F32) * (1.0 / 64.0)
    low = (fixed & 63).astype(F32) * (1.0 / 4096.0)
    first = jnp.where(lane == row, 1.0, 0.0).astype(BF16)
    second = jnp.where(lane == row + E, 1.0, 0.0).astype(BF16)
    return matmul(high.astype(BF16), first, ((1,), (0,))) + matmul(low.astype(BF16), second, ((1,), (0,)))


def outer_kernel(counts, fixed, x, grad, out, pick, held, sheet, sem):
    k = pl.program_id(0)

    def copy(step):
        return pltpu.make_async_copy(
            held.at[:, pl.ds(step * TILES, TILES)], out.at[:, pl.ds(step * TILES, TILES)], sem.at[step]
        )

    def copy_card():
        return pltpu.make_async_copy(held.at[:, pl.ds(CARD, 1)], out.at[:, pl.ds(CARD, 1)], sem.at[K])

    @pl.when(k == 0)
    def _():
        pick[...] = order()
        sheet[...] = jnp.zeros_like(sheet)
        sheet[0:K] = card(fixed[...])
        held[:, CARD] = jnp.broadcast_to(sheet[...].astype(BF16)[None], (NG, PER, LANES))
        copy_card().start()

    turned = matmul(pick[...], x[0], ((1,), (1,))).astype(BF16)
    masked = masked_of(grad[0], counts[k])
    product = matmul(turned, masked, ((1,), (0,))).astype(BF16)
    for tile in range(TILES):
        part = product[:, tile * LANES : (tile + 1) * LANES]
        held[:, k * TILES + tile] = part.reshape(NG, PER, LANES)
    copy(k).start()

    @pl.when(k == K - 1)
    def _():
        copy_card().wait()
        for step in range(K):
            copy(step).wait()


def outer(counts, fixed, x, grad):
    return pl.pallas_call(
        outer_kernel,
        grid_spec=pltpu.PrefetchScalarGridSpec(
            num_scalar_prefetch=1,
            grid=(K,),
            in_specs=[
                pl.BlockSpec((K, E), lambda k, c: (0, 0)),
                pl.BlockSpec((1, M, D), lambda k, c: (k, 0, 0)),
                pl.BlockSpec((1, M, D), lambda k, c: (k, 0, 0)),
            ],
            out_specs=pl.BlockSpec(memory_space=pl.ANY),
            scratch_shapes=[
                pltpu.VMEM((D, D), BF16),
                pltpu.VMEM((NG, CARD + 1, PER, LANES), BF16),
                pltpu.VMEM((PER, LANES), F32),
                pltpu.SemaphoreType.DMA((K + 1,)),
            ],
        ),
        out_shape=jax.ShapeDtypeStruct((NG, CARD + 1, PER, LANES), BF16),
        compiler_params=vmem(56),
        cost_estimate=pl.CostEstimate(flops=2 * K * D * D * (M + M), bytes_accessed=4 << 20, transcendentals=0),
        name="outer",
    )(counts, fixed, x, grad)


def spread(cards, system, z, away):
    chosen = jnp.where(system(row_of((STEP, 1), 0)) == row_of((1, GROUP * PER), 1), 1.0, 0.0).astype(BF16)
    values = matmul(chosen, cards, ((1,), (0,))).astype(BF16)
    lane = row_of((LANES, 2 * WIDTH), 0)
    col = row_of((LANES, 2 * WIDTH), 1)
    widen = jnp.where(lane == ((col >> 1) & (E - 1)) + (col // WIDTH) * E, 1.0, 0.0).astype(BF16)
    wide = matmul(values, widen, ((1,), (0,)))
    row = row_of((STEP * PER, 1), 0) & (PER - 1)
    place = row_of((1, 2 * WIDTH), 1)
    line = (z + away * ((place & (WIDTH - 1)) >> 5) + NZ) & (NZ - 1)
    same = row == (line << 1) + (place & 1)
    tall = jnp.broadcast_to(wide[:, None, :], (STEP, PER, 2 * WIDTH)).reshape(STEP * PER, 2 * WIDTH)
    return jnp.where(same, tall, 0.0).astype(BF16)


def stack_kernel(*refs):
    *blocks, out = refs
    for n, block in enumerate(blocks):
        for half in (0, WIDTH):
            out[half + n * PART : half + (n + 1) * PART] = block[...]


def stack(blocks):
    return pl.pallas_call(
        stack_kernel,
        out_shape=jax.ShapeDtypeStruct((2 * WIDTH, D), BF16),
        compiler_params=vmem(STACK_MIB),
        cost_estimate=pl.CostEstimate(flops=0, bytes_accessed=6 * WIDTH * D, transcendentals=0),
        name="stack",
    )(*blocks)


def merge_kernel(z, cards, rows, out):
    tiles = cards[...].reshape(GROUP * PER, LANES)
    factor = spread(tiles, lambda s: ((s >> 2) << 4) + (s & 3), z[0], -1)
    out[...] = matmul(factor, rows[...], ((1,), (0,))).astype(BF16).reshape(GROUP, K, PER, D)


def merge(z, message, rows):
    return pl.pallas_call(
        merge_kernel,
        grid_spec=pltpu.PrefetchScalarGridSpec(
            num_scalar_prefetch=1,
            grid=(NG // GROUP,),
            in_specs=[
                pl.BlockSpec((GROUP, 1, PER, LANES), lambda s, z: (s, CARD, 0, 0)),
                pl.BlockSpec((2 * WIDTH, D), lambda s, z: (0, 0)),
            ],
            out_specs=pl.BlockSpec((GROUP, K, PER, D), lambda s, z: (s, 0, 0, 0)),
        ),
        out_shape=jax.ShapeDtypeStruct((NG, K, PER, D), BF16),
        compiler_params=vmem(MERGE_MIB),
        cost_estimate=pl.CostEstimate(flops=4 * NG * K * PER * WIDTH * D, bytes_accessed=3 << 20, transcendentals=0),
        name="merge",
    )(z, message, rows)


def mix_kernel(z, message, *refs):
    *outs, total = refs
    step = pl.program_id(0)
    tiles = message[:, CARD].reshape(GROUP * PER, LANES)
    factor = spread(tiles, lambda s: ((s & (GROUP - 1)) << 4) + (s >> 3), z[0], 1)
    columns = []
    for tile in range(TILES):
        parts = [message[:, k * TILES + tile].reshape(GROUP * PER, LANES) for k in range(K)]
        columns.append(jnp.concatenate(parts, axis=0))
    terms = jnp.concatenate(columns, axis=1)
    both = matmul(factor, terms, ((0,), (0,)))
    part = both[:WIDTH] + both[WIDTH:]

    @pl.when(step == 0)
    def _():
        total[...] = part

    @pl.when(step > 0)
    def _():
        total[...] += part

    @pl.when(step == pl.num_programs(0) - 1)
    def _():
        for n, out in enumerate(outs):
            out[...] = total[n * PART : (n + 1) * PART]


def mix(z, message):
    return pl.pallas_call(
        mix_kernel,
        grid_spec=pltpu.PrefetchScalarGridSpec(
            num_scalar_prefetch=1,
            grid=(NG // GROUP,),
            in_specs=[pl.BlockSpec((GROUP, CARD + 1, PER, LANES), lambda s, z: (s, 0, 0, 0))],
            out_specs=[pl.BlockSpec((PART, D), lambda s, z: (0, 0))] * NZ,
            scratch_shapes=[pltpu.VMEM((WIDTH, D), F32)],
        ),
        out_shape=[jax.ShapeDtypeStruct((PART, D), F32)] * NZ,
        compiler_params=vmem(MIX_MIB),
        cost_estimate=pl.CostEstimate(flops=4 * NG * K * PER * WIDTH * D, bytes_accessed=3 << 20, transcendentals=0),
        name="mix",
    )(z, message)


def total_kernel(*refs):
    *sums, out = refs
    total = sums[0][...]
    for part in sums[1:]:
        total += part[...]
    for e in range(E):
        out[e] = total[ROWS * e : ROWS * (e + 1)]


def total(sums):
    return pl.pallas_call(
        total_kernel,
        out_shape=jax.ShapeDtypeStruct((E, ROWS, D), F32),
        compiler_params=vmem(8),
        cost_estimate=pl.CostEstimate(flops=WIDTH * D, bytes_accessed=5 * WIDTH * D, transcendentals=0),
        name="total",
    )(*sums)


def back_kernel(counts, grad, merged, out, pick):
    k = pl.program_id(0)

    @pl.when(k == 0)
    def _():
        pick[...] = order()

    masked = masked_of(grad[0], counts[k])
    weights = merged[...].reshape(D, D)
    moved = matmul(masked, weights, ((1,), (1,))).astype(BF16)
    out[0] = matmul(moved, pick[...], ((1,), (0,))).astype(BF16)


def back(counts, grad, merged):
    return pl.pallas_call(
        back_kernel,
        grid_spec=pltpu.PrefetchScalarGridSpec(
            num_scalar_prefetch=1,
            grid=(K,),
            in_specs=[
                pl.BlockSpec((1, M, D), lambda k, c: (k, 0, 0)),
                pl.BlockSpec((NG, 1, PER, D), lambda k, c: (0, k, 0, 0)),
            ],
            out_specs=pl.BlockSpec((1, M, D), lambda k, c: (k, 0, 0)),
            scratch_shapes=[pltpu.VMEM((D, D), BF16)],
        ),
        out_shape=jax.ShapeDtypeStruct((K, M, D), BF16),
        compiler_params=vmem(BACK_MIB),
        cost_estimate=pl.CostEstimate(flops=4 * K * M * D * D, bytes_accessed=4 << 20, transcendentals=0),
        name="back",
    )(counts, grad, merged)


def swap(array, axes):
    return lax.all_to_all(array, axes, 0, 0, tiled=True)


def along_z(array, by):
    return lax.ppermute(array, "z", [(i, (i + by) % NZ) for i in range(NZ)])


def shards(inputs, out_grad, coeff_fixed, atom_counts, experts):
    z = lax.axis_index("z").astype(jnp.int32).reshape(1)
    message = swap(outer(atom_counts, coeff_fixed, inputs, out_grad), PLANE)
    own = experts.reshape(PART, D)
    rows = stack([own] + [along_z(own, n) for n in range(1, NZ)])
    merged = swap(merge(z, message, rows), PLANE)
    mixed = mix(z, message)
    sums = [mixed[0]] + [along_z(mixed[n], n) for n in range(1, NZ)]
    return back(atom_counts, out_grad, merged), total(sums)


def solution(mesh):
    split = Mesh(mesh.devices.reshape([size for _, size in AXES]), NAMES)
    placed = (
        P(NAMES, None, None),
        P(NAMES, None, None),
        P(NAMES, None),
        P(NAMES),
        P(None, NAMES, None),
    )
    return jax.shard_map(
        shards,
        mesh=split,
        in_specs=placed,
        out_specs=(P(NAMES, None, None), P(None, NAMES, None)),
        check_vma=False,
    )
```

time: 97.2 us -> 93.4 us (0.961)
  the two profiles are of different devices: /device:TPU:9 before, /device:TPU:34 now
where the time goes in v4:
time: 93.4 us; the launch traced here: 92.7 us
  starting transfers between devices  46.7 us (50%)
  Pallas kernels  23 us (25%)
  waiting for transfers between devices  20.6 us (22%)
  local copies, waits for them, and re-layouts  1.51 us (2%)
    ppermute x14, starting transfers between devices, along_z(): return lax.ppermute(array, 'z', [(i, (i + by) % NZ) for i in range(NZ)])  30.5 us
    all_to_all x2, starting transfers between devices, swap(): return lax.all_to_all(array, axes, 0, 0, tiled=True)  16.2 us
    ppermute x14, waiting for transfers between devices, along_z(): return lax.ppermute(array, 'z', [(i, (i + by) % NZ) for i in range(NZ)])  15.1 us
    pallas_call x1, Pallas kernels, outer(): pl.pallas_call(outer_kernel, grid_spec=pltpu.PrefetchScalarGridSpec(num_s...  6.44 us
    all_to_all x2, waiting for transfers between devices, swap(): return lax.all_to_all(array, axes, 0, 0, tiled=True)  5.59 us
    pallas_call x1, Pallas kernels, mix(): pl.pallas_call(mix_kernel, grid_spec=pltpu.PrefetchScalarGridSpec(num_sca...  5.46 us
    pallas_call x1, Pallas kernels, merge(): pl.pallas_call(merge_kernel, grid_spec=pltpu.PrefetchScalarGridSpec(num_s...  4.82 us
    pallas_call x1, Pallas kernels, back(): pl.pallas_call(back_kernel, grid_spec=pltpu.PrefetchScalarGridSpec(num_sc...  3.9 us
  transfers between devices with their start and end apart: 16, of which 7 were waited for; matrix products, arithmetic and copies ran while one was open for 0% of the time, Pallas kernels for 8%

profile of v4, /device:TPU:34, one launch (start us, length us, event | category | flops | bytes accessed | tf_op | source)
XLA Modules:
  0.0 92.7 jit_solution(9362860544480168836)
XLA Ops:
  0.6 6.4 %outer.1 = bf16[32,17,16,128]{3,2,1,0:T(8,128)(2,1)} custom-call(s32[4]{0:T(128)} %counts.3, s32[4,16]{1,0:T(4,128)} %fixed.1, bf16[4,256,512]{2,1,0:T(8,128)(2,1)} %x.1, bf16[4,256,512]{2,1,0:T(8,128)(2,1)} %grad.3), custom_call_target="tpu_custom_call" | custom-call | flops 1073741824 | bytes 4194304 | tf_op jit(solution)/shard_map/outer/pallas_call | solution.py:101
  7.1 0.0 copy-start.11
  7.1 7.7 %all-to-all-start = ((bf16[32,17,16,128]{3,2,1,0:T(8,128)(2,1)}), bf16[32,17,16,128]{3,2,1,0:T(8,128)(2,1)}, u32[]{:S(2)}, u32[]{:S(2)}) async-start(bf16[32,17,16,128]{3,2,1,0:T(8,128)(2,1)} %outer.1), calls=%async_computation | async-start | bytes 4456448 | tf_op jit(solution)/shard_map/all_to_all | solution.py:280
  14.8 0.0 copy-done.11
  14.8 0.0 copy-start.3
  14.8 2.0 %collective-permute-start = (bf16[32,512]{1,0:T(8,128)(2,1)S(1)}, bf16[32,512]{1,0:T(8,128)(2,1)S(1)}, u32[]{:S(2)}, u32[]{:S(2)}) collective-permute-start(bf16[32,512]{1,0:T(8,128)(2,1)S(1)} %reshape.11.refs_0_), channel_id=1, source_target_pairs={{0,32},{32,64},{64,96},{96,128},{128,160},{160,192},{192,224},{224... | collective-permute-start | bytes 98312 | tf_op jit(solution)/shard_map/ppermute | solution.py:284
  16.8 4.5 %collective-permute-start.1 = (bf16[32,512]{1,0:T(8,128)(2,1)S(1)}, bf16[32,512]{1,0:T(8,128)(2,1)S(1)}, u32[]{:S(2)}, u32[]{:S(2)}) collective-permute-start(bf16[32,512]{1,0:T(8,128)(2,1)S(1)} %reshape.11.refs_0_), channel_id=1, source_target_pairs={{0,64},{32,96},{64,128},{96,160},{128,192},{160,224},{192,0},{224,... | collective-permute-start | bytes 98312 | tf_op jit(solution)/shard_map/ppermute | solution.py:284
  21.3 1.9 %collective-permute-start.2 = (bf16[32,512]{1,0:T(8,128)(2,1)S(1)}, bf16[32,512]{1,0:T(8,128)(2,1)S(1)}, u32[]{:S(2)}, u32[]{:S(2)}) collective-permute-start(bf16[32,512]{1,0:T(8,128)(2,1)S(1)} %reshape.11.refs_0_), channel_id=1, source_target_pairs={{0,96},{32,128},{64,160},{96,192},{128,224},{160,0},{192,32},{224,... | collective-permute-start | bytes 98312 | tf_op jit(solution)/shard_map/ppermute | solution.py:284
  23.2 1.4 %collective-permute-start.3 = (bf16[32,512]{1,0:T(8,128)(2,1)S(1)}, bf16[32,512]{1,0:T(8,128)(2,1)S(1)}, u32[]{:S(2)}, u32[]{:S(2)}) collective-permute-start(bf16[32,512]{1,0:T(8,128)(2,1)S(1)} %reshape.11.refs_0_), channel_id=1, source_target_pairs={{0,128},{32,160},{64,192},{96,224},{128,0},{160,32},{192,64},{224,... | collective-permute-start | bytes 98312 | tf_op jit(solution)/shard_map/ppermute | solution.py:284
  24.7 3.1 %collective-permute-start.4 = (bf16[32,512]{1,0:T(8,128)(2,1)S(1)}, bf16[32,512]{1,0:T(8,128)(2,1)S(1)}, u32[]{:S(2)}, u32[]{:S(2)}) collective-permute-start(bf16[32,512]{1,0:T(8,128)(2,1)S(1)} %reshape.11.refs_0_), channel_id=1, source_target_pairs={{0,160},{32,192},{64,224},{96,0},{128,32},{160,64},{192,96},{224,1... | collective-permute-start | bytes 98312 | tf_op jit(solution)/shard_map/ppermute | solution.py:284
  27.8 0.0 collective-permute-done.refs_1_
  27.8 2.4 %collective-permute-start.5 = (bf16[32,512]{1,0:T(8,128)(2,1)S(1)}, bf16[32,512]{1,0:T(8,128)(2,1)S(1)}, u32[]{:S(2)}, u32[]{:S(2)}) collective-permute-start(bf16[32,512]{1,0:T(8,128)(2,1)S(1)} %reshape.11.refs_0_), channel_id=1, source_target_pairs={{0,192},{32,224},{64,0},{96,32},{128,64},{160,96},{192,128},{224,1... | collective-permute-start | bytes 98312 | tf_op jit(solution)/shard_map/ppermute | solution.py:284
  30.2 0.0 collective-permute-done.1.refs_2_
  30.2 2.2 %collective-permute-start.6 = (bf16[32,512]{1,0:T(8,128)(2,1)S(1)}, bf16[32,512]{1,0:T(8,128)(2,1)S(1)}, u32[]{:S(2)}, u32[]{:S(2)}) collective-permute-start(bf16[32,512]{1,0:T(8,128)(2,1)S(1)} %reshape.11.refs_0_), channel_id=1, source_target_pairs={{0,224},{32,0},{64,32},{96,64},{128,96},{160,128},{192,160},{224,1... | collective-permute-start | bytes 98312 | tf_op jit(solution)/shard_map/ppermute | solution.py:284
  32.4 0.0 collective-permute-done.2.refs_3_
  32.4 0.0 collective-permute-done.3.refs_4_
  32.4 0.0 copy-start.7
  32.4 0.0 collective-permute-done.4.refs_5_
  32.4 0.0 copy-start.8
  32.4 0.5 collective-permute-done.5.refs_6_
  32.9 1.2 %collective-permute-done.6.refs_7_ = bf16[32,512]{1,0:T(8,128)(2,1)S(1)} collective-permute-done((bf16[32,512]{1,0:T(8,128)(2,1)S(1)}, bf16[32,512]{1,0:T(8,128)(2,1)S(1)}, u32[]{:S(2)}, u32[]{:S(2)}) %collective-permute-start.6) | collective-permute-done | bytes 32800 | tf_op jit(solution)/shard_map/ppermute | solution.py:284
  34.1 0.0 copy-done.3
  34.2 0.6 copy-done.10
  34.8 1.7 %stack.1.rows = bf16[512,512]{1,0:T(8,128)(2,1)} custom-call(bf16[32,512]{1,0:T(8,128)(2,1)} %copy-done.3, bf16[32,512]{1,0:T(8,128)(2,1)} %copy-done.4, bf16[32,512]{1,0:T(8,128)(2,1)} %copy-done.5, bf16[32,512]{1,0:T(8,128)(2,1)} %copy-done.6, bf16[32,512]{1,0:T(8,128)(2,1)} %copy-done.7, bf16[32,512]{1,0:T(8,128)(2,1)} %copy-done.8, ...), custom_call_target="tpu_custom_call" | custom-call | bytes 786432 | tf_op jit(solution)/shard_map/stack/pallas_call | solution.py:149
  36.5 5.6 %all-to-all-done.cards.message = bf16[32,17,16,128]{3,2,1,0:T(8,128)(2,1)} async-done(((bf16[32,17,16,128]{3,2,1,0:T(8,128)(2,1)}), bf16[32,17,16,128]{3,2,1,0:T(8,128)(2,1)}, u32[]{:S(2)}, u32[]{:S(2)}) %all-to-all-start) | async-done | bytes 2228256 | tf_op jit(solution)/shard_map/all_to_all | solution.py:280
  42.1 4.8 %merge.1 = bf16[32,4,16,512]{3,2,1,0:T(8,128)(2,1)} custom-call(s32[1]{0:T(128)} %bitcast.z, bf16[32,17,16,128]{3,2,1,0:T(8,128)(2,1)} %all-to-all-done.cards.message, bf16[512,512]{1,0:T(8,128)(2,1)} %stack.1.rows), custom_call_target="tpu_custom_call" | custom-call | flops 1073741824 | bytes 3145728 | tf_op jit(solution)/shard_map/merge/pallas_call | solution.py:165
  46.9 8.6 %all-to-all-start.1 = ((bf16[32,4,16,512]{3,2,1,0:T(8,128)(2,1)}), bf16[32,4,16,512]{3,2,1,0:T(8,128)(2,1)S(1)}, u32[]{:S(2)}, u32[]{:S(2)}) async-start(bf16[32,4,16,512]{3,2,1,0:T(8,128)(2,1)} %merge.1), calls=%async_computation.1 | async-start | bytes 4194304 | tf_op jit(solution)/shard_map/all_to_all | solution.py:280
  55.4 0.0 copy-start
  55.5 0.0 copy-start.2
  55.5 5.5 %mix.1 = (f32[32,512]{1,0:T(8,128)}, f32[32,512]{1,0:T(8,128)}, f32[32,512]{1,0:T(8,128)}, f32[32,512]{1,0:T(8,128)}, f32[32,512]{1,0:T(8,128)}, /*index=5*/f32[...) custom-call(s32[1]{0:T(128)} %bitcast.z, bf16[32,17,16,128]{3,2,1,0:T(8,128)(2,1)} %all-to-all-done.cards.message), custom_call_target="tpu_custom_call" | custom-call | flops 1073741824 | bytes 3145728 | tf_op jit(solution)/shard_map/mix/pallas_call | solution.py:211
  60.9 6.3 %collective-permute-start.10 = (f32[32,512]{1,0:T(8,128)}, f32[32,512]{1,0:T(8,128)S(1)}, u32[]{:S(2)}, u32[]{:S(2)}) collective-permute-start(f32[32,512]{1,0:T(8,128)} %get-tuple-element.14), channel_id=1, source_target_pairs={{0,128},{32,160},{64,192},{96,224},{128,0},{160,32},{192,64},{224,... | collective-permute-start | bytes 196616 | tf_op jit(solution)/shard_map/ppermute | solution.py:284
  67.2 0.1 collective-permute-start.11
  67.3 1.0 %collective-permute-start.12 = (f32[32,512]{1,0:T(8,128)}, f32[32,512]{1,0:T(8,128)S(1)}, u32[]{:S(2)}, u32[]{:S(2)}) collective-permute-start(f32[32,512]{1,0:T(8,128)} %get-tuple-element.16), channel_id=1, source_target_pairs={{0,192},{32,224},{64,0},{96,32},{128,64},{160,96},{192,128},{224,1... | collective-permute-start | bytes 196616 | tf_op jit(solution)/shard_map/ppermute | solution.py:284
  68.3 4.5 %collective-permute-start.13 = (f32[32,512]{1,0:T(8,128)}, f32[32,512]{1,0:T(8,128)S(1)}, u32[]{:S(2)}, u32[]{:S(2)}) collective-permute-start(f32[32,512]{1,0:T(8,128)} %get-tuple-element.17), channel_id=1, source_target_pairs={{0,224},{32,0},{64,32},{96,64},{128,96},{160,128},{192,160},{224,1... | collective-permute-start | bytes 196616 | tf_op jit(solution)/shard_map/ppermute | solution.py:284
  72.8 0.0 collective-permute-start.7
  72.8 0.0 collective-permute-done.10.refs_4_
  72.8 1.0 %collective-permute-start.8 = (f32[32,512]{1,0:T(8,128)}, f32[32,512]{1,0:T(8,128)S(1)}, u32[]{:S(2)}, u32[]{:S(2)}) collective-permute-start(f32[32,512]{1,0:T(8,128)} %get-tuple-element.12), channel_id=1, source_target_pairs={{0,64},{32,96},{64,128},{96,160},{128,192},{160,224},{192,0},{224,... | collective-permute-start | bytes 196616 | tf_op jit(solution)/shard_map/ppermute | solution.py:284
  73.9 5.2 %collective-permute-done.11.refs_5_ = f32[32,512]{1,0:T(8,128)S(1)} collective-permute-done((f32[32,512]{1,0:T(8,128)}, f32[32,512]{1,0:T(8,128)S(1)}, u32[]{:S(2)}, u32[]{:S(2)}) %collective-permute-start.11) | collective-permute-done | bytes 65568 | tf_op jit(solution)/shard_map/ppermute | solution.py:284
  79.0 0.0 collective-permute-start.9
  79.0 0.0 collective-permute-done.12.refs_6_
  79.0 0.6 collective-permute-done.13.refs_7_
  79.7 0.0 collective-permute-done.7.refs_1_
  79.7 2.2 %collective-permute-done.8.refs_2_ = f32[32,512]{1,0:T(8,128)S(1)} collective-permute-done((f32[32,512]{1,0:T(8,128)}, f32[32,512]{1,0:T(8,128)S(1)}, u32[]{:S(2)}, u32[]{:S(2)}) %collective-permute-start.8) | collective-permute-done | bytes 65568 | tf_op jit(solution)/shard_map/ppermute | solution.py:284
  81.9 5.3 %collective-permute-done.9.refs_3_ = f32[32,512]{1,0:T(8,128)S(1)} collective-permute-done((f32[32,512]{1,0:T(8,128)}, f32[32,512]{1,0:T(8,128)S(1)}, u32[]{:S(2)}, u32[]{:S(2)}) %collective-permute-start.9) | collective-permute-done | bytes 65568 | tf_op jit(solution)/shard_map/ppermute | solution.py:284
  87.2 0.8 copy-done.1
  88.1 0.7 total.1
  88.7 0.0 all-to-all-done.1.merged
  88.8 3.9 %back.1 = bf16[4,256,512]{2,1,0:T(8,128)(2,1)} custom-call(s32[4]{0:T(128)S(1)} %copy-done.2, bf16[4,256,512]{2,1,0:T(8,128)(2,1)S(1)} %copy-done, bf16[32,4,16,512]{3,2,1,0:T(8,128)(2,1)S(1)} %all-to-all-done.1.merged), custom_call_target="tpu_custom_call" | custom-call | flops 1073741824 | bytes 4194304 | tf_op jit(solution)/shard_map/back/pallas_call | solution.py:260
  (15 shorter events, 0.0 us)
Async XLA Ops:
  7.1 7.7 %copy-start.11 = (bf16[16,2,512]{2,1,0:T(2,128)(2,1)S(1)}, bf16[16,2,512]{2,1,0:T(2,128)(2,1)}, u32[]{:S(2)}) copy-start(bf16[16,2,512]{2,1,0:T(2,128)(2,1)} %param.9) | copy-start | bytes 98308
  7.1 35.0 %all-to-all-start = ((bf16[32,17,16,128]{3,2,1,0:T(8,128)(2,1)}), bf16[32,17,16,128]{3,2,1,0:T(8,128)(2,1)}, u32[]{:S(2)}, u32[]{:S(2)}) async-start(bf16[32,17,16,128]{3,2,1,0:T(8,128)(2,1)} %outer.1), calls=%async_computation | async-start | bytes 4456448 | tf_op jit(solution)/shard_map/all_to_all | solution.py:280
  14.8 19.3 %copy-start.3 = (bf16[32,512]{1,0:T(8,128)(2,1)}, bf16[32,512]{1,0:T(8,128)(2,1)S(1)}, u32[]{:S(2)}) copy-start(bf16[32,512]{1,0:T(8,128)(2,1)S(1)} %reshape.11.refs_0_) | copy-start | bytes 98308
  14.8 13.0 %collective-permute-start = (bf16[32,512]{1,0:T(8,128)(2,1)S(1)}, bf16[32,512]{1,0:T(8,128)(2,1)S(1)}, u32[]{:S(2)}, u32[]{:S(2)}) collective-permute-start(bf16[32,512]{1,0:T(8,128)(2,1)S(1)} %reshape.11.refs_0_), channel_id=1, source_target_pairs={{0,32},{32,64},{64,96},{96,128},{128,160},{160,192},{192,224},{224... | collective-permute-start | bytes 98312 | tf_op jit(solution)/shard_map/ppermute | solution.py:284
  16.8 13.4 %collective-permute-start.1 = (bf16[32,512]{1,0:T(8,128)(2,1)S(1)}, bf16[32,512]{1,0:T(8,128)(2,1)S(1)}, u32[]{:S(2)}, u32[]{:S(2)}) collective-permute-start(bf16[32,512]{1,0:T(8,128)(2,1)S(1)} %reshape.11.refs_0_), channel_id=1, source_target_pairs={{0,64},{32,96},{64,128},{96,160},{128,192},{160,224},{192,0},{224,... | collective-permute-start | bytes 98312 | tf_op jit(solution)/shard_map/ppermute | solution.py:284
  21.3 11.1 %collective-permute-start.2 = (bf16[32,512]{1,0:T(8,128)(2,1)S(1)}, bf16[32,512]{1,0:T(8,128)(2,1)S(1)}, u32[]{:S(2)}, u32[]{:S(2)}) collective-permute-start(bf16[32,512]{1,0:T(8,128)(2,1)S(1)} %reshape.11.refs_0_), channel_id=1, source_target_pairs={{0,96},{32,128},{64,160},{96,192},{128,224},{160,0},{192,32},{224,... | collective-permute-start | bytes 98312 | tf_op jit(solution)/shard_map/ppermute | solution.py:284
  23.2 9.2 %collective-permute-start.3 = (bf16[32,512]{1,0:T(8,128)(2,1)S(1)}, bf16[32,512]{1,0:T(8,128)(2,1)S(1)}, u32[]{:S(2)}, u32[]{:S(2)}) collective-permute-start(bf16[32,512]{1,0:T(8,128)(2,1)S(1)} %reshape.11.refs_0_), channel_id=1, source_target_pairs={{0,128},{32,160},{64,192},{96,224},{128,0},{160,32},{192,64},{224,... | collective-permute-start | bytes 98312 | tf_op jit(solution)/shard_map/ppermute | solution.py:284
  24.7 7.8 %collective-permute-start.4 = (bf16[32,512]{1,0:T(8,128)(2,1)S(1)}, bf16[32,512]{1,0:T(8,128)(2,1)S(1)}, u32[]{:S(2)}, u32[]{:S(2)}) collective-permute-start(bf16[32,512]{1,0:T(8,128)(2,1)S(1)} %reshape.11.refs_0_), channel_id=1, source_target_pairs={{0,160},{32,192},{64,224},{96,0},{128,32},{160,64},{192,96},{224,1... | collective-permute-start | bytes 98312 | tf_op jit(solution)/shard_map/ppermute | solution.py:284
  27.8 6.3 %copy-start.4 = (bf16[32,512]{1,0:T(8,128)(2,1)}, bf16[32,512]{1,0:T(8,128)(2,1)S(1)}, u32[]{:S(2)}) copy-start(bf16[32,512]{1,0:T(8,128)(2,1)S(1)} %collective-permute-done.refs_1_) | copy-start | bytes 98308
  27.8 5.1 %collective-permute-start.5 = (bf16[32,512]{1,0:T(8,128)(2,1)S(1)}, bf16[32,512]{1,0:T(8,128)(2,1)S(1)}, u32[]{:S(2)}, u32[]{:S(2)}) collective-permute-start(bf16[32,512]{1,0:T(8,128)(2,1)S(1)} %reshape.11.refs_0_), channel_id=1, source_target_pairs={{0,192},{32,224},{64,0},{96,32},{128,64},{160,96},{192,128},{224,1... | collective-permute-start | bytes 98312 | tf_op jit(solution)/shard_map/ppermute | solution.py:284
  30.2 3.9 %copy-start.5 = (bf16[32,512]{1,0:T(8,128)(2,1)}, bf16[32,512]{1,0:T(8,128)(2,1)S(1)}, u32[]{:S(2)}) copy-start(bf16[32,512]{1,0:T(8,128)(2,1)S(1)} %collective-permute-done.1.refs_2_) | copy-start | bytes 98308
  30.2 3.9 %collective-permute-start.6 = (bf16[32,512]{1,0:T(8,128)(2,1)S(1)}, bf16[32,512]{1,0:T(8,128)(2,1)S(1)}, u32[]{:S(2)}, u32[]{:S(2)}) collective-permute-start(bf16[32,512]{1,0:T(8,128)(2,1)S(1)} %reshape.11.refs_0_), channel_id=1, source_target_pairs={{0,224},{32,0},{64,32},{96,64},{128,96},{160,128},{192,160},{224,1... | collective-permute-start | bytes 98312 | tf_op jit(solution)/shard_map/ppermute | solution.py:284
  32.4 1.7 %copy-start.6 = (bf16[32,512]{1,0:T(8,128)(2,1)}, bf16[32,512]{1,0:T(8,128)(2,1)S(1)}, u32[]{:S(2)}) copy-start(bf16[32,512]{1,0:T(8,128)(2,1)S(1)} %collective-permute-done.2.refs_3_) | copy-start | bytes 98308
  32.4 1.7 %copy-start.7 = (bf16[32,512]{1,0:T(8,128)(2,1)}, bf16[32,512]{1,0:T(8,128)(2,1)S(1)}, u32[]{:S(2)}) copy-start(bf16[32,512]{1,0:T(8,128)(2,1)S(1)} %collective-permute-done.3.refs_4_) | copy-start | bytes 98308
  32.4 1.7 %copy-start.8 = (bf16[32,512]{1,0:T(8,128)(2,1)}, bf16[32,512]{1,0:T(8,128)(2,1)S(1)}, u32[]{:S(2)}) copy-start(bf16[32,512]{1,0:T(8,128)(2,1)S(1)} %collective-permute-done.4.refs_5_) | copy-start | bytes 98308
  32.9 1.2 %copy-start.9 = (bf16[32,512]{1,0:T(8,128)(2,1)}, bf16[32,512]{1,0:T(8,128)(2,1)S(1)}, u32[]{:S(2)}) copy-start(bf16[32,512]{1,0:T(8,128)(2,1)S(1)} %collective-permute-done.5.refs_6_) | copy-start | bytes 98308
  34.2 0.6 copy-start.10
  46.9 41.9 %all-to-all-start.1 = ((bf16[32,4,16,512]{3,2,1,0:T(8,128)(2,1)}), bf16[32,4,16,512]{3,2,1,0:T(8,128)(2,1)S(1)}, u32[]{:S(2)}, u32[]{:S(2)}) async-start(bf16[32,4,16,512]{3,2,1,0:T(8,128)(2,1)} %merge.1), calls=%async_computation.1 | async-start | bytes 4194304 | tf_op jit(solution)/shard_map/all_to_all | solution.py:280
  55.4 33.3 %copy-start = (bf16[4,256,512]{2,1,0:T(8,128)(2,1)S(1)}, bf16[4,256,512]{2,1,0:T(8,128)(2,1)}, u32[]{:S(2)}) copy-start(bf16[4,256,512]{2,1,0:T(8,128)(2,1)} %grad.3) | copy-start | bytes 3145732
  55.5 33.3 %copy-start.2 = (s32[4]{0:T(128)S(1)}, s32[4]{0:T(128)}, u32[]{:S(2)}) copy-start(s32[4]{0:T(128)} %counts.3) | copy-start | bytes 52
  60.9 11.9 %collective-permute-start.10 = (f32[32,512]{1,0:T(8,128)}, f32[32,512]{1,0:T(8,128)S(1)}, u32[]{:S(2)}, u32[]{:S(2)}) collective-permute-start(f32[32,512]{1,0:T(8,128)} %get-tuple-element.14), channel_id=1, source_target_pairs={{0,128},{32,160},{64,192},{96,224},{128,0},{160,32},{192,64},{224,... | collective-permute-start | bytes 196616 | tf_op jit(solution)/shard_map/ppermute | solution.py:284
  67.2 11.8 %collective-permute-start.11 = (f32[32,512]{1,0:T(8,128)}, f32[32,512]{1,0:T(8,128)S(1)}, u32[]{:S(2)}, u32[]{:S(2)}) collective-permute-start(f32[32,512]{1,0:T(8,128)} %get-tuple-element.15), channel_id=1, source_target_pairs={{0,160},{32,192},{64,224},{96,0},{128,32},{160,64},{192,96},{224,1... | collective-permute-start | bytes 196616 | tf_op jit(solution)/shard_map/ppermute | solution.py:284
  67.3 11.7 %collective-permute-start.12 = (f32[32,512]{1,0:T(8,128)}, f32[32,512]{1,0:T(8,128)S(1)}, u32[]{:S(2)}, u32[]{:S(2)}) collective-permute-start(f32[32,512]{1,0:T(8,128)} %get-tuple-element.16), channel_id=1, source_target_pairs={{0,192},{32,224},{64,0},{96,32},{128,64},{160,96},{192,128},{224,1... | collective-permute-start | bytes 196616 | tf_op jit(solution)/shard_map/ppermute | solution.py:284
  68.3 11.3 %collective-permute-start.13 = (f32[32,512]{1,0:T(8,128)}, f32[32,512]{1,0:T(8,128)S(1)}, u32[]{:S(2)}, u32[]{:S(2)}) collective-permute-start(f32[32,512]{1,0:T(8,128)} %get-tuple-element.17), channel_id=1, source_target_pairs={{0,224},{32,0},{64,32},{96,64},{128,96},{160,128},{192,160},{224,1... | collective-permute-start | bytes 196616 | tf_op jit(solution)/shard_map/ppermute | solution.py:284
  72.8 6.9 %collective-permute-start.7 = (f32[32,512]{1,0:T(8,128)}, f32[32,512]{1,0:T(8,128)S(1)}, u32[]{:S(2)}, u32[]{:S(2)}) collective-permute-start(f32[32,512]{1,0:T(8,128)} %get-tuple-element.11), channel_id=1, source_target_pairs={{0,32},{32,64},{64,96},{96,128},{128,160},{160,192},{192,224},{224... | collective-permute-start | bytes 196616 | tf_op jit(solution)/shard_map/ppermute | solution.py:284
  72.8 9.1 %collective-permute-start.8 = (f32[32,512]{1,0:T(8,128)}, f32[32,512]{1,0:T(8,128)S(1)}, u32[]{:S(2)}, u32[]{:S(2)}) collective-permute-start(f32[32,512]{1,0:T(8,128)} %get-tuple-element.12), channel_id=1, source_target_pairs={{0,64},{32,96},{64,128},{96,160},{128,192},{160,224},{192,0},{224,... | collective-permute-start | bytes 196616 | tf_op jit(solution)/shard_map/ppermute | solution.py:284
  79.0 8.2 %collective-permute-start.9 = (f32[32,512]{1,0:T(8,128)}, f32[32,512]{1,0:T(8,128)S(1)}, u32[]{:S(2)}, u32[]{:S(2)}) collective-permute-start(f32[32,512]{1,0:T(8,128)} %get-tuple-element.13), channel_id=1, source_target_pairs={{0,96},{32,128},{64,160},{96,192},{128,224},{160,0},{192,32},{224,... | collective-permute-start | bytes 196616 | tf_op jit(solution)/shard_map/ppermute | solution.py:284
  87.2 0.8 copy-start.1

commit v5 on v4

v5 whole, which is shorter than its diff:
```python
import jax
import jax.numpy as jnp
from jax import lax
from jax.experimental import pallas as pl
from jax.experimental.pallas import tpu as pltpu
from jax.sharding import Mesh, PartitionSpec as P

AXES = (("z", 8), ("xl", 2), ("core", 2), ("y", 4), ("xh", 2))
NAMES = tuple(name for name, _ in AXES)
PLANE = ("xl", "core", "y", "xh")
NZ = 8
NG = 32
ROWS = 2
PER = NZ * ROWS
D = 512
E = 16
K = 4
M = 256
STACK_MIB = 62
MERGE_MIB = 60
MIX_MIB = 56
BACK_MIB = 24
F32 = jnp.float32
BF16 = jnp.bfloat16
LANES = 128
TILES = D // LANES
PART = E * ROWS
WIDTH = NZ * PART
CARD = K * TILES
GROUP = 8
STEP = GROUP * K


def vmem(mib):
    return pltpu.CompilerParams(vmem_limit_bytes=mib * 1024 * 1024)


def row_of(shape, dim):
    return lax.broadcasted_iota(jnp.int32, shape, dim)


def order():
    to = row_of((D, 1), 0)
    source = (((to >> 1) & (NZ - 1)) << 6) + ((to >> 4) << 1) + (to & 1)
    return jnp.where(source == row_of((1, D), 1), 1.0, 0.0).astype(BF16)


def matmul(a, b, dims):
    return lax.dot_general(a, b, (dims, ((), ())), preferred_element_type=F32)


def masked_of(grad, count):
    return jnp.where(row_of((M, 1), 0) < count, grad, jnp.zeros_like(grad))


def card(fixed):
    lane = row_of((E, LANES), 1)
    row = row_of((E, LANES), 0)
    high = (fixed >> 6).astype(F32) * (1.0 / 64.0)
    low = (fixed & 63).astype(F32) * (1.0 / 4096.0)
    first = jnp.where(lane == row, 1.0, 0.0).astype(BF16)
    second = jnp.where(lane == row + E, 1.0, 0.0).astype(BF16)
    return matmul(high.astype(BF16), first, ((1,), (0,))) + matmul(low.astype(BF16), second, ((1,), (0,)))


def outer_kernel(counts, fixed, x, grad, out, xs, grads, pick, held, sheet, ins, outs):
    def fetch(k):
        return (
            pltpu.make_async_copy(x.at[k], xs.at[k], ins.at[2 * k]),
            pltpu.make_async_copy(grad.at[k], grads.at[k], ins.at[2 * k + 1]),
        )

    def send(k):
        place = pl.ds(k * TILES, TILES)
        return pltpu.make_async_copy(held.at[:, place], out.at[:, place], outs.at[k])

    send_card = pltpu.make_async_copy(held.at[:, pl.ds(CARD, 1)], out.at[:, pl.ds(CARD, 1)], outs.at[K])
    fetches = [fetch(k) for k in range(K)]
    for pair in fetches:
        for copy in pair:
            copy.start()
    sheet[...] = jnp.zeros_like(sheet)
    sheet[0:K] = card(fixed[...])
    held[:, CARD] = jnp.broadcast_to(sheet[...].astype(BF16)[None], (NG, PER, LANES))
    send_card.start()
    pick[...] = order()
    for k in range(K):
        fetches[k][0].wait()
        turned = matmul(xs[k], pick[...], ((1,), (1,))).astype(BF16).T
        fetches[k][1].wait()
        product = matmul(turned, masked_of(grads[k], counts[k]), ((1,), (0,))).astype(BF16)
        for tile in range(TILES):
            part = product[:, tile * LANES : (tile + 1) * LANES]
            held[:, k * TILES + tile] = part.reshape(NG, PER, LANES)
        send(k).start()
    send_card.wait()
    for k in range(K):
        send(k).wait()


ANY = pl.BlockSpec(memory_space=pl.ANY)
SCALARS = pl.BlockSpec(memory_space=pltpu.SMEM)
WHOLE = pl.BlockSpec(memory_space=pltpu.VMEM)


def outer(counts, fixed, x, grad):
    return pl.pallas_call(
        outer_kernel,
        in_specs=[SCALARS, WHOLE, ANY, ANY],
        out_specs=ANY,
        scratch_shapes=[
            pltpu.VMEM((K, M, D), BF16),
            pltpu.VMEM((K, M, D), BF16),
            pltpu.VMEM((D, D), BF16),
            pltpu.VMEM((NG, CARD + 1, PER, LANES), BF16),
            pltpu.VMEM((PER, LANES), F32),
            pltpu.SemaphoreType.DMA((2 * K,)),
            pltpu.SemaphoreType.DMA((K + 1,)),
        ],
        out_shape=jax.ShapeDtypeStruct((NG, CARD + 1, PER, LANES), BF16),
        compiler_params=vmem(56),
        cost_estimate=pl.CostEstimate(flops=2 * K * D * D * (M + M), bytes_accessed=4 << 20, transcendentals=0),
        name="outer",
    )(counts, fixed, x, grad)


def one_hot(found):
    return jnp.where(found, 1.0, 0.0).astype(BF16)


def line_of(part, z, away):
    line = (z + away * ((part & (WIDTH - 1)) >> 5) + NZ) & (NZ - 1)
    return (line << 1) + (part & 1)


def source_of(part):
    return ((part >> 1) & (E - 1)) + ((part >> 8) << 4)


def stack_kernel(*refs):
    *blocks, out = refs
    for n, block in enumerate(blocks):
        for half in (0, WIDTH):
            out[half + n * PART : half + (n + 1) * PART] = block[...]


def stack(blocks):
    return pl.pallas_call(
        stack_kernel,
        out_shape=jax.ShapeDtypeStruct((2 * WIDTH, D), BF16),
        compiler_params=vmem(STACK_MIB),
        cost_estimate=pl.CostEstimate(flops=0, bytes_accessed=6 * WIDTH * D, transcendentals=0),
        name="stack",
    )(*blocks)


GROUPS = NG // GROUP
TALL = STEP * PER


def merge_kernel(z, message, rows, out, cards, weights, held, ins, outs):
    fetch_cards = pltpu.make_async_copy(message.at[:, pl.ds(CARD, 1)], cards, ins.at[0])
    fetch_rows = pltpu.make_async_copy(rows, weights, ins.at[1])

    def send(n):
        place = pl.ds(n * GROUP, GROUP)
        return pltpu.make_async_copy(held.at[place], out.at[place], outs.at[n])

    fetch_cards.start()
    fetch_rows.start()
    tall = row_of((TALL, 1), 0)
    pick = one_hot(((tall >> 6) << 4) + ((tall >> 4) & (K - 1)) == row_of((1, GROUP * PER), 1))
    part = row_of((1, 2 * WIDTH), 1)
    widen = one_hot(row_of((LANES, 1), 0) == source_of(part))
    same = (tall & (PER - 1)) == line_of(part, z[0], -1)
    fetch_cards.wait()
    for n in range(GROUPS):
        tiles = cards[n * GROUP : (n + 1) * GROUP].reshape(GROUP * PER, LANES)
        values = matmul(pick, tiles, ((1,), (0,))).astype(BF16)
        factor = jnp.where(same, matmul(values, widen, ((1,), (0,))), 0.0).astype(BF16)
        if n == 0:
            fetch_rows.wait()
        merged = matmul(factor, weights[...], ((1,), (0,))).astype(BF16)
        held[n * GROUP : (n + 1) * GROUP] = merged.reshape(GROUP, K, PER, D)
        send(n).start()
    for n in range(GROUPS):
        send(n).wait()


def merge(z, message, rows):
    return pl.pallas_call(
        merge_kernel,
        in_specs=[SCALARS, ANY, ANY],
        out_specs=ANY,
        scratch_shapes=[
            pltpu.VMEM((NG, 1, PER, LANES), BF16),
            pltpu.VMEM((2 * WIDTH, D), BF16),
            pltpu.VMEM((NG, K, PER, D), BF16),
            pltpu.SemaphoreType.DMA((2,)),
            pltpu.SemaphoreType.DMA((GROUPS,)),
        ],
        out_shape=jax.ShapeDtypeStruct((NG, K, PER, D), BF16),
        compiler_params=vmem(MERGE_MIB),
        cost_estimate=pl.CostEstimate(flops=4 * NG * K * PER * WIDTH * D, bytes_accessed=3 << 20, transcendentals=0),
        name="merge",
    )(z, message, rows)


def mix_kernel(z, message, *refs):
    out, (held, total, ins, outs) = refs[:NZ], refs[NZ:]
    fetches = []
    for n in range(GROUPS):
        place = pl.ds(n * GROUP, GROUP)
        fetches.append(pltpu.make_async_copy(message.at[place], held.at[place], ins.at[n]))
        fetches[n].start()
    tall = row_of((1, TALL), 1)
    pick = one_hot(row_of((GROUP * PER, 1), 0) == (((tall >> 4) & (GROUP - 1)) << 4) + (tall >> 7))
    part = row_of((2 * WIDTH, 1), 0)
    widen = one_hot(source_of(part) == row_of((1, LANES), 1))
    same = line_of(part, z[0], 1) == (tall & (PER - 1))
    for n in range(GROUPS):
        fetches[n].wait()
        place = slice(n * GROUP, (n + 1) * GROUP)
        tiles = held[place, CARD].reshape(GROUP * PER, LANES)
        values = matmul(tiles, pick, ((0,), (0,))).astype(BF16)
        factor = jnp.where(same, matmul(widen, values, ((1,), (0,))), 0.0).astype(BF16)
        columns = []
        for tile in range(TILES):
            pieces = [held[place, k * TILES + tile].reshape(GROUP * PER, LANES) for k in range(K)]
            columns.append(jnp.concatenate(pieces, axis=0))
        both = matmul(factor, jnp.concatenate(columns, axis=1), ((1,), (0,)))
        sums = both[:WIDTH] + both[WIDTH:]
        total[...] = sums if n == 0 else total[...] + sums
    sends = [pltpu.make_async_copy(total.at[pl.ds(n * PART, PART)], out[n], outs.at[n]) for n in range(NZ)]
    for copy in sends:
        copy.start()
    for copy in sends:
        copy.wait()


def mix(z, message):
    return pl.pallas_call(
        mix_kernel,
        in_specs=[SCALARS, ANY],
        out_specs=[ANY] * NZ,
        scratch_shapes=[
            pltpu.VMEM((NG, CARD + 1, PER, LANES), BF16),
            pltpu.VMEM((WIDTH, D), F32),
            pltpu.SemaphoreType.DMA((GROUPS,)),
            pltpu.SemaphoreType.DMA((NZ,)),
        ],
        out_shape=[jax.ShapeDtypeStruct((PART, D), F32)] * NZ,
        compiler_params=vmem(MIX_MIB),
        cost_estimate=pl.CostEstimate(flops=4 * NG * K * PER * WIDTH * D, bytes_accessed=3 << 20, transcendentals=0),
        name="mix",
    )(z, message)


def total_kernel(*refs):
    *sums, out = refs
    total = sums[0][...]
    for part in sums[1:]:
        total += part[...]
    for e in range(E):
        out[e] = total[ROWS * e : ROWS * (e + 1)]


def total(sums):
    return pl.pallas_call(
        total_kernel,
        out_shape=jax.ShapeDtypeStruct((E, ROWS, D), F32),
        compiler_params=vmem(8),
        cost_estimate=pl.CostEstimate(flops=WIDTH * D, bytes_accessed=5 * WIDTH * D, transcendentals=0),
        name="total",
    )(*sums)


def back_kernel(counts, grad, merged, out, pick, held, outs):
    def send(k):
        return pltpu.make_async_copy(held.at[k], out.at[k], outs.at[k])

    pick[...] = order()
    for k in range(K):
        masked = masked_of(grad[k], counts[k])
        moved = matmul(masked, merged[:, k].reshape(D, D), ((1,), (1,))).astype(BF16)
        held[k] = matmul(moved, pick[...], ((1,), (0,))).astype(BF16)
        send(k).start()
    for k in range(K):
        send(k).wait()


def back(counts, grad, merged):
    return pl.pallas_call(
        back_kernel,
        in_specs=[SCALARS, WHOLE, WHOLE],
        out_specs=ANY,
        scratch_shapes=[
            pltpu.VMEM((D, D), BF16),
            pltpu.VMEM((K, M, D), BF16),
            pltpu.SemaphoreType.DMA((K,)),
        ],
        out_shape=jax.ShapeDtypeStruct((K, M, D), BF16),
        compiler_params=vmem(BACK_MIB),
        cost_estimate=pl.CostEstimate(flops=4 * K * M * D * D, bytes_accessed=4 << 20, transcendentals=0),
        name="back",
    )(counts, grad, merged)


def swap(array, axes):
    return lax.all_to_all(array, axes, 0, 0, tiled=True)


def along_z(array, by):
    return lax.ppermute(array, "z", [(i, (i + by) % NZ) for i in range(NZ)])


def shards(inputs, out_grad, coeff_fixed, atom_counts, experts):
    z = lax.axis_index("z").astype(jnp.int32).reshape(1)
    message = swap(outer(atom_counts, coeff_fixed, inputs, out_grad), PLANE)
    own = experts.reshape(PART, D)
    rows = stack([own] + [along_z(own, n) for n in range(1, NZ)])
    merged = swap(merge(z, message, rows), PLANE)
    mixed = mix(z, message)
    sums = [mixed[0]] + [along_z(mixed[n], n) for n in range(1, NZ)]
    return back(atom_counts, out_grad, merged), total(sums)


def solution(mesh):
    split = Mesh(mesh.devices.reshape([size for _, size in AXES]), NAMES)
    placed = (
        P(NAMES, None, None),
        P(NAMES, None, None),
        P(NAMES, None),
        P(NAMES),
        P(None, NAMES, None),
    )
    return jax.shard_map(
        shards,
        mesh=split,
        in_specs=placed,
        out_specs=(P(NAMES, None, None), P(None, NAMES, None)),
        check_vma=False,
    )
```

time: 93.4 us -> 90.5 us (0.969)
  Pallas kernels: 23 us -> 19.6 us
    pallas_call x4, Pallas kernels: 20.6 us -> 17.2 us  [the longest x1 5.37 us: outer(): pl.pallas_call(outer_kernel, in_specs=[SCALARS, WHOLE, ANY, ANY], out_spe...]
where the time goes in v5:
time: 90.5 us; the launch traced here: 90 us
  starting transfers between devices  47 us (52%)
  waiting for transfers between devices  20.9 us (23%)
  Pallas kernels  19.6 us (22%)
  local copies, waits for them, and re-layouts  1.51 us (2%)
  between operations  0.97 us (1%)
    ppermute x14, starting transfers between devices, along_z(): return lax.ppermute(array, 'z', [(i, (i + by) % NZ) for i in range(NZ)])  30.7 us
    all_to_all x2, starting transfers between devices, swap(): return lax.all_to_all(array, axes, 0, 0, tiled=True)  16.2 us
    ppermute x14, waiting for transfers between devices, along_z(): return lax.ppermute(array, 'z', [(i, (i + by) % NZ) for i in range(NZ)])  15.3 us
    all_to_all x2, waiting for transfers between devices, swap(): return lax.all_to_all(array, axes, 0, 0, tiled=True)  5.6 us
    pallas_call x1, Pallas kernels, outer(): pl.pallas_call(outer_kernel, in_specs=[SCALARS, WHOLE, ANY, ANY], out_spe...  5.37 us
    pallas_call x1, Pallas kernels, mix(): pl.pallas_call(mix_kernel, in_specs=[SCALARS, ANY], out_specs=[ANY] * NZ,...  4.69 us
    pallas_call x1, Pallas kernels, merge(): pl.pallas_call(merge_kernel, in_specs=[SCALARS, ANY, ANY], out_specs=ANY,...  4.27 us
    pallas_call x1, Pallas kernels, back(): pl.pallas_call(back_kernel, in_specs=[SCALARS, WHOLE, WHOLE], out_specs=A...  2.9 us
  transfers between devices with their start and end apart: 16, of which 7 were waited for; matrix products, arithmetic and copies ran while one was open for 0% of the time, Pallas kernels for 8%

profile of v5, /device:TPU:34, one launch (start us, length us, event | category | flops | bytes accessed | tf_op | source)
XLA Modules:
  0.0 90.0 jit_solution(5319078484526957806)
XLA Ops:
  0.6 5.4 %outer.1 = bf16[32,17,16,128]{3,2,1,0:T(8,128)(2,1)} custom-call(s32[4]{0:T(128)} %counts.3, s32[4,16]{1,0:T(4,128)} %fixed.1, bf16[4,256,512]{2,1,0:T(8,128)(2,1)} %x.1, bf16[4,256,512]{2,1,0:T(8,128)(2,1)} %grad.3), custom_call_target="tpu_custom_call" | custom-call | flops 1073741824 | bytes 4194304 | tf_op jit(solution)/shard_map/outer/pallas_call | solution.py:107
  6.0 0.0 copy-start.11
  6.0 7.7 %all-to-all-start = ((bf16[32,17,16,128]{3,2,1,0:T(8,128)(2,1)}), bf16[32,17,16,128]{3,2,1,0:T(8,128)(2,1)}, u32[]{:S(2)}, u32[]{:S(2)}) async-start(bf16[32,17,16,128]{3,2,1,0:T(8,128)(2,1)} %outer.1), calls=%async_computation | async-start | bytes 4456448 | tf_op jit(solution)/shard_map/all_to_all | solution.py:310
  13.7 0.0 copy-start.3
  13.8 2.0 %collective-permute-start = (bf16[32,512]{1,0:T(8,128)(2,1)S(1)}, bf16[32,512]{1,0:T(8,128)(2,1)S(1)}, u32[]{:S(2)}, u32[]{:S(2)}) collective-permute-start(bf16[32,512]{1,0:T(8,128)(2,1)S(1)} %reshape.11.refs_0_), channel_id=1, source_target_pairs={{0,32},{32,64},{64,96},{96,128},{128,160},{160,192},{192,224},{224... | collective-permute-start | bytes 98312 | tf_op jit(solution)/shard_map/ppermute | solution.py:314
  15.7 4.5 %collective-permute-start.1 = (bf16[32,512]{1,0:T(8,128)(2,1)S(1)}, bf16[32,512]{1,0:T(8,128)(2,1)S(1)}, u32[]{:S(2)}, u32[]{:S(2)}) collective-permute-start(bf16[32,512]{1,0:T(8,128)(2,1)S(1)} %reshape.11.refs_0_), channel_id=1, source_target_pairs={{0,64},{32,96},{64,128},{96,160},{128,192},{160,224},{192,0},{224,... | collective-permute-start | bytes 98312 | tf_op jit(solution)/shard_map/ppermute | solution.py:314
  20.2 1.9 %collective-permute-start.2 = (bf16[32,512]{1,0:T(8,128)(2,1)S(1)}, bf16[32,512]{1,0:T(8,128)(2,1)S(1)}, u32[]{:S(2)}, u32[]{:S(2)}) collective-permute-start(bf16[32,512]{1,0:T(8,128)(2,1)S(1)} %reshape.11.refs_0_), channel_id=1, source_target_pairs={{0,96},{32,128},{64,160},{96,192},{128,224},{160,0},{192,32},{224,... | collective-permute-start | bytes 98312 | tf_op jit(solution)/shard_map/ppermute | solution.py:314
  22.2 1.5 %collective-permute-start.3 = (bf16[32,512]{1,0:T(8,128)(2,1)S(1)}, bf16[32,512]{1,0:T(8,128)(2,1)S(1)}, u32[]{:S(2)}, u32[]{:S(2)}) collective-permute-start(bf16[32,512]{1,0:T(8,128)(2,1)S(1)} %reshape.11.refs_0_), channel_id=1, source_target_pairs={{0,128},{32,160},{64,192},{96,224},{128,0},{160,32},{192,64},{224,... | collective-permute-start | bytes 98312 | tf_op jit(solution)/shard_map/ppermute | solution.py:314
  23.6 3.1 %collective-permute-start.4 = (bf16[32,512]{1,0:T(8,128)(2,1)S(1)}, bf16[32,512]{1,0:T(8,128)(2,1)S(1)}, u32[]{:S(2)}, u32[]{:S(2)}) collective-permute-start(bf16[32,512]{1,0:T(8,128)(2,1)S(1)} %reshape.11.refs_0_), channel_id=1, source_target_pairs={{0,160},{32,192},{64,224},{96,0},{128,32},{160,64},{192,96},{224,1... | collective-permute-start | bytes 98312 | tf_op jit(solution)/shard_map/ppermute | solution.py:314
  26.7 0.0 collective-permute-done.refs_1_
  26.7 2.4 %collective-permute-start.5 = (bf16[32,512]{1,0:T(8,128)(2,1)S(1)}, bf16[32,512]{1,0:T(8,128)(2,1)S(1)}, u32[]{:S(2)}, u32[]{:S(2)}) collective-permute-start(bf16[32,512]{1,0:T(8,128)(2,1)S(1)} %reshape.11.refs_0_), channel_id=1, source_target_pairs={{0,192},{32,224},{64,0},{96,32},{128,64},{160,96},{192,128},{224,1... | collective-permute-start | bytes 98312 | tf_op jit(solution)/shard_map/ppermute | solution.py:314
  29.1 0.0 collective-permute-done.1.refs_2_
  29.1 2.2 %collective-permute-start.6 = (bf16[32,512]{1,0:T(8,128)(2,1)S(1)}, bf16[32,512]{1,0:T(8,128)(2,1)S(1)}, u32[]{:S(2)}, u32[]{:S(2)}) collective-permute-start(bf16[32,512]{1,0:T(8,128)(2,1)S(1)} %reshape.11.refs_0_), channel_id=1, source_target_pairs={{0,224},{32,0},{64,32},{96,64},{128,96},{160,128},{192,160},{224,1... | collective-permute-start | bytes 98312 | tf_op jit(solution)/shard_map/ppermute | solution.py:314
  31.4 0.0 collective-permute-done.2.refs_3_
  31.4 0.0 collective-permute-done.3.refs_4_
  31.4 0.0 copy-start.7
  31.4 0.0 collective-permute-done.4.refs_5_
  31.4 0.6 collective-permute-done.5.refs_6_
  32.0 1.1 %collective-permute-done.6.refs_7_ = bf16[32,512]{1,0:T(8,128)(2,1)S(1)} collective-permute-done((bf16[32,512]{1,0:T(8,128)(2,1)S(1)}, bf16[32,512]{1,0:T(8,128)(2,1)S(1)}, u32[]{:S(2)}, u32[]{:S(2)}) %collective-permute-start.6) | collective-permute-done | bytes 32800 | tf_op jit(solution)/shard_map/ppermute | solution.py:314
  33.0 0.0 copy-done.5
  33.0 0.0 copy-done.6
  33.0 0.0 copy-done.7
  33.1 0.6 copy-done.10
  33.7 1.7 %stack.1.rows = bf16[512,512]{1,0:T(8,128)(2,1)} custom-call(bf16[32,512]{1,0:T(8,128)(2,1)} %copy-done.3, bf16[32,512]{1,0:T(8,128)(2,1)} %copy-done.4, bf16[32,512]{1,0:T(8,128)(2,1)} %copy-done.5, bf16[32,512]{1,0:T(8,128)(2,1)} %copy-done.6, bf16[32,512]{1,0:T(8,128)(2,1)} %copy-done.7, bf16[32,512]{1,0:T(8,128)(2,1)} %copy-done.8, ...), custom_call_target="tpu_custom_call" | custom-call | bytes 786432 | tf_op jit(solution)/shard_map/stack/pallas_call | solution.py:148
  35.4 5.6 %all-to-all-done.message = bf16[32,17,16,128]{3,2,1,0:T(8,128)(2,1)} async-done(((bf16[32,17,16,128]{3,2,1,0:T(8,128)(2,1)}), bf16[32,17,16,128]{3,2,1,0:T(8,128)(2,1)}, u32[]{:S(2)}, u32[]{:S(2)}) %all-to-all-start) | async-done | bytes 2228256 | tf_op jit(solution)/shard_map/all_to_all | solution.py:310
  41.0 4.3 %merge.1 = bf16[32,4,16,512]{3,2,1,0:T(8,128)(2,1)} custom-call(s32[1]{0:T(128)} %bitcast.z, bf16[32,17,16,128]{3,2,1,0:T(8,128)(2,1)} %all-to-all-done.message, bf16[512,512]{1,0:T(8,128)(2,1)} %stack.1.rows), custom_call_target="tpu_custom_call" | custom-call | flops 1073741824 | bytes 3145728 | tf_op jit(solution)/shard_map/merge/pallas_call | solution.py:191
  45.3 8.5 %all-to-all-start.1 = ((bf16[32,4,16,512]{3,2,1,0:T(8,128)(2,1)}), bf16[32,4,16,512]{3,2,1,0:T(8,128)(2,1)S(1)}, u32[]{:S(2)}, u32[]{:S(2)}) async-start(bf16[32,4,16,512]{3,2,1,0:T(8,128)(2,1)} %merge.1), calls=%async_computation.1 | async-start | bytes 4194304 | tf_op jit(solution)/shard_map/all_to_all | solution.py:310
  53.8 0.0 copy-start
  53.8 0.0 copy-start.2
  53.8 4.7 %mix.1 = (f32[32,512]{1,0:T(8,128)}, f32[32,512]{1,0:T(8,128)}, f32[32,512]{1,0:T(8,128)}, f32[32,512]{1,0:T(8,128)}, f32[32,512]{1,0:T(8,128)}, /*index=5*/f32[...) custom-call(s32[1]{0:T(128)} %bitcast.z, bf16[32,17,16,128]{3,2,1,0:T(8,128)(2,1)} %all-to-all-done.message), custom_call_target="tpu_custom_call" | custom-call | flops 1073741824 | bytes 3145728 | tf_op jit(solution)/shard_map/mix/pallas_call | solution.py:242
  58.5 6.6 %collective-permute-start.10 = (f32[32,512]{1,0:T(8,128)}, f32[32,512]{1,0:T(8,128)S(1)}, u32[]{:S(2)}, u32[]{:S(2)}) collective-permute-start(f32[32,512]{1,0:T(8,128)} %get-tuple-element.14), channel_id=1, source_target_pairs={{0,128},{32,160},{64,192},{96,224},{128,0},{160,32},{192,64},{224,... | collective-permute-start | bytes 196616 | tf_op jit(solution)/shard_map/ppermute | solution.py:314
  65.1 0.1 collective-permute-start.11
  65.2 1.0 %collective-permute-start.12 = (f32[32,512]{1,0:T(8,128)}, f32[32,512]{1,0:T(8,128)S(1)}, u32[]{:S(2)}, u32[]{:S(2)}) collective-permute-start(f32[32,512]{1,0:T(8,128)} %get-tuple-element.16), channel_id=1, source_target_pairs={{0,192},{32,224},{64,0},{96,32},{128,64},{160,96},{192,128},{224,1... | collective-permute-start | bytes 196616 | tf_op jit(solution)/shard_map/ppermute | solution.py:314
  66.2 4.5 %collective-permute-start.13 = (f32[32,512]{1,0:T(8,128)}, f32[32,512]{1,0:T(8,128)S(1)}, u32[]{:S(2)}, u32[]{:S(2)}) collective-permute-start(f32[32,512]{1,0:T(8,128)} %get-tuple-element.17), channel_id=1, source_target_pairs={{0,224},{32,0},{64,32},{96,64},{128,96},{160,128},{192,160},{224,1... | collective-permute-start | bytes 196616 | tf_op jit(solution)/shard_map/ppermute | solution.py:314
  70.7 0.0 collective-permute-start.7
  70.7 0.0 collective-permute-done.10.refs_4_
  70.7 1.0 %collective-permute-start.8 = (f32[32,512]{1,0:T(8,128)}, f32[32,512]{1,0:T(8,128)S(1)}, u32[]{:S(2)}, u32[]{:S(2)}) collective-permute-start(f32[32,512]{1,0:T(8,128)} %get-tuple-element.12), channel_id=1, source_target_pairs={{0,64},{32,96},{64,128},{96,160},{128,192},{160,224},{192,0},{224,... | collective-permute-start | bytes 196616 | tf_op jit(solution)/shard_map/ppermute | solution.py:314
  71.7 5.2 %collective-permute-done.11.refs_5_ = f32[32,512]{1,0:T(8,128)S(1)} collective-permute-done((f32[32,512]{1,0:T(8,128)}, f32[32,512]{1,0:T(8,128)S(1)}, u32[]{:S(2)}, u32[]{:S(2)}) %collective-permute-start.11) | collective-permute-done | bytes 65568 | tf_op jit(solution)/shard_map/ppermute | solution.py:314
  76.9 0.0 collective-permute-start.9
  76.9 0.0 collective-permute-done.12.refs_6_
  76.9 0.7 collective-permute-done.13.refs_7_
  77.6 0.0 collective-permute-done.7.refs_1_
  77.6 2.1 %collective-permute-done.8.refs_2_ = f32[32,512]{1,0:T(8,128)S(1)} collective-permute-done((f32[32,512]{1,0:T(8,128)}, f32[32,512]{1,0:T(8,128)S(1)}, u32[]{:S(2)}, u32[]{:S(2)}) %collective-permute-start.8) | collective-permute-done | bytes 65568 | tf_op jit(solution)/shard_map/ppermute | solution.py:314
  79.7 5.6 %collective-permute-done.9.refs_3_ = f32[32,512]{1,0:T(8,128)S(1)} collective-permute-done((f32[32,512]{1,0:T(8,128)}, f32[32,512]{1,0:T(8,128)S(1)}, u32[]{:S(2)}, u32[]{:S(2)}) %collective-permute-start.9) | collective-permute-done | bytes 65568 | tf_op jit(solution)/shard_map/ppermute | solution.py:314
  85.4 0.8 copy-done.1
  86.2 0.7 total.1
  86.9 0.0 all-to-all-done.1.merged
  86.9 2.9 %back.1 = bf16[4,256,512]{2,1,0:T(8,128)(2,1)} custom-call(s32[4]{0:T(128)S(1)} %copy-done.2, bf16[4,256,512]{2,1,0:T(8,128)(2,1)S(1)} %copy-done, bf16[32,4,16,512]{3,2,1,0:T(8,128)(2,1)S(1)} %all-to-all-done.1.merged), custom_call_target="tpu_custom_call" | custom-call | flops 1073741824 | bytes 4194304 | tf_op jit(solution)/shard_map/back/pallas_call | solution.py:293
  (15 shorter events, 0.0 us)
Async XLA Ops:
  6.0 7.7 %copy-start.11 = (bf16[16,2,512]{2,1,0:T(2,128)(2,1)S(1)}, bf16[16,2,512]{2,1,0:T(2,128)(2,1)}, u32[]{:S(2)}) copy-start(bf16[16,2,512]{2,1,0:T(2,128)(2,1)} %param.9) | copy-start | bytes 98308
  6.0 35.0 %all-to-all-start = ((bf16[32,17,16,128]{3,2,1,0:T(8,128)(2,1)}), bf16[32,17,16,128]{3,2,1,0:T(8,128)(2,1)}, u32[]{:S(2)}, u32[]{:S(2)}) async-start(bf16[32,17,16,128]{3,2,1,0:T(8,128)(2,1)} %outer.1), calls=%async_computation | async-start | bytes 4456448 | tf_op jit(solution)/shard_map/all_to_all | solution.py:310
  13.7 19.3 %copy-start.3 = (bf16[32,512]{1,0:T(8,128)(2,1)}, bf16[32,512]{1,0:T(8,128)(2,1)S(1)}, u32[]{:S(2)}) copy-start(bf16[32,512]{1,0:T(8,128)(2,1)S(1)} %reshape.11.refs_0_) | copy-start | bytes 98308
  13.8 13.0 %collective-permute-start = (bf16[32,512]{1,0:T(8,128)(2,1)S(1)}, bf16[32,512]{1,0:T(8,128)(2,1)S(1)}, u32[]{:S(2)}, u32[]{:S(2)}) collective-permute-start(bf16[32,512]{1,0:T(8,128)(2,1)S(1)} %reshape.11.refs_0_), channel_id=1, source_target_pairs={{0,32},{32,64},{64,96},{96,128},{128,160},{160,192},{192,224},{224... | collective-permute-start | bytes 98312 | tf_op jit(solution)/shard_map/ppermute | solution.py:314
  15.7 13.4 %collective-permute-start.1 = (bf16[32,512]{1,0:T(8,128)(2,1)S(1)}, bf16[32,512]{1,0:T(8,128)(2,1)S(1)}, u32[]{:S(2)}, u32[]{:S(2)}) collective-permute-start(bf16[32,512]{1,0:T(8,128)(2,1)S(1)} %reshape.11.refs_0_), channel_id=1, source_target_pairs={{0,64},{32,96},{64,128},{96,160},{128,192},{160,224},{192,0},{224,... | collective-permute-start | bytes 98312 | tf_op jit(solution)/shard_map/ppermute | solution.py:314
  20.2 11.1 %collective-permute-start.2 = (bf16[32,512]{1,0:T(8,128)(2,1)S(1)}, bf16[32,512]{1,0:T(8,128)(2,1)S(1)}, u32[]{:S(2)}, u32[]{:S(2)}) collective-permute-start(bf16[32,512]{1,0:T(8,128)(2,1)S(1)} %reshape.11.refs_0_), channel_id=1, source_target_pairs={{0,96},{32,128},{64,160},{96,192},{128,224},{160,0},{192,32},{224,... | collective-permute-start | bytes 98312 | tf_op jit(solution)/shard_map/ppermute | solution.py:314
  22.2 9.2 %collective-permute-start.3 = (bf16[32,512]{1,0:T(8,128)(2,1)S(1)}, bf16[32,512]{1,0:T(8,128)(2,1)S(1)}, u32[]{:S(2)}, u32[]{:S(2)}) collective-permute-start(bf16[32,512]{1,0:T(8,128)(2,1)S(1)} %reshape.11.refs_0_), channel_id=1, source_target_pairs={{0,128},{32,160},{64,192},{96,224},{128,0},{160,32},{192,64},{224,... | collective-permute-start | bytes 98312 | tf_op jit(solution)/shard_map/ppermute | solution.py:314
  23.6 7.8 %collective-permute-start.4 = (bf16[32,512]{1,0:T(8,128)(2,1)S(1)}, bf16[32,512]{1,0:T(8,128)(2,1)S(1)}, u32[]{:S(2)}, u32[]{:S(2)}) collective-permute-start(bf16[32,512]{1,0:T(8,128)(2,1)S(1)} %reshape.11.refs_0_), channel_id=1, source_target_pairs={{0,160},{32,192},{64,224},{96,0},{128,32},{160,64},{192,96},{224,1... | collective-permute-start | bytes 98312 | tf_op jit(solution)/shard_map/ppermute | solution.py:314
  26.7 6.3 %copy-start.4 = (bf16[32,512]{1,0:T(8,128)(2,1)}, bf16[32,512]{1,0:T(8,128)(2,1)S(1)}, u32[]{:S(2)}) copy-start(bf16[32,512]{1,0:T(8,128)(2,1)S(1)} %collective-permute-done.refs_1_) | copy-start | bytes 98308
  26.7 5.2 %collective-permute-start.5 = (bf16[32,512]{1,0:T(8,128)(2,1)S(1)}, bf16[32,512]{1,0:T(8,128)(2,1)S(1)}, u32[]{:S(2)}, u32[]{:S(2)}) collective-permute-start(bf16[32,512]{1,0:T(8,128)(2,1)S(1)} %reshape.11.refs_0_), channel_id=1, source_target_pairs={{0,192},{32,224},{64,0},{96,32},{128,64},{160,96},{192,128},{224,1... | collective-permute-start | bytes 98312 | tf_op jit(solution)/shard_map/ppermute | solution.py:314
  29.1 3.9 %copy-start.5 = (bf16[32,512]{1,0:T(8,128)(2,1)}, bf16[32,512]{1,0:T(8,128)(2,1)S(1)}, u32[]{:S(2)}) copy-start(bf16[32,512]{1,0:T(8,128)(2,1)S(1)} %collective-permute-done.1.refs_2_) | copy-start | bytes 98308
  29.1 3.9 %collective-permute-start.6 = (bf16[32,512]{1,0:T(8,128)(2,1)S(1)}, bf16[32,512]{1,0:T(8,128)(2,1)S(1)}, u32[]{:S(2)}, u32[]{:S(2)}) collective-permute-start(bf16[32,512]{1,0:T(8,128)(2,1)S(1)} %reshape.11.refs_0_), channel_id=1, source_target_pairs={{0,224},{32,0},{64,32},{96,64},{128,96},{160,128},{192,160},{224,1... | collective-permute-start | bytes 98312 | tf_op jit(solution)/shard_map/ppermute | solution.py:314
  31.4 1.7 %copy-start.6 = (bf16[32,512]{1,0:T(8,128)(2,1)}, bf16[32,512]{1,0:T(8,128)(2,1)S(1)}, u32[]{:S(2)}) copy-start(bf16[32,512]{1,0:T(8,128)(2,1)S(1)} %collective-permute-done.2.refs_3_) | copy-start | bytes 98308
  31.4 1.7 %copy-start.7 = (bf16[32,512]{1,0:T(8,128)(2,1)}, bf16[32,512]{1,0:T(8,128)(2,1)S(1)}, u32[]{:S(2)}) copy-start(bf16[32,512]{1,0:T(8,128)(2,1)S(1)} %collective-permute-done.3.refs_4_) | copy-start | bytes 98308
  31.4 1.7 %copy-start.8 = (bf16[32,512]{1,0:T(8,128)(2,1)}, bf16[32,512]{1,0:T(8,128)(2,1)S(1)}, u32[]{:S(2)}) copy-start(bf16[32,512]{1,0:T(8,128)(2,1)S(1)} %collective-permute-done.4.refs_5_) | copy-start | bytes 98308
  32.0 1.1 %copy-start.9 = (bf16[32,512]{1,0:T(8,128)(2,1)}, bf16[32,512]{1,0:T(8,128)(2,1)S(1)}, u32[]{:S(2)}) copy-start(bf16[32,512]{1,0:T(8,128)(2,1)S(1)} %collective-permute-done.5.refs_6_) | copy-start | bytes 98308
  33.1 0.6 copy-start.10
  45.3 41.6 %all-to-all-start.1 = ((bf16[32,4,16,512]{3,2,1,0:T(8,128)(2,1)}), bf16[32,4,16,512]{3,2,1,0:T(8,128)(2,1)S(1)}, u32[]{:S(2)}, u32[]{:S(2)}) async-start(bf16[32,4,16,512]{3,2,1,0:T(8,128)(2,1)} %merge.1), calls=%async_computation.1 | async-start | bytes 4194304 | tf_op jit(solution)/shard_map/all_to_all | solution.py:310
  53.8 33.1 %copy-start = (bf16[4,256,512]{2,1,0:T(8,128)(2,1)S(1)}, bf16[4,256,512]{2,1,0:T(8,128)(2,1)}, u32[]{:S(2)}) copy-start(bf16[4,256,512]{2,1,0:T(8,128)(2,1)} %grad.3) | copy-start | bytes 3145732
  53.8 33.1 %copy-start.2 = (s32[4]{0:T(128)S(1)}, s32[4]{0:T(128)}, u32[]{:S(2)}) copy-start(s32[4]{0:T(128)} %counts.3) | copy-start | bytes 52
  58.5 12.2 %collective-permute-start.10 = (f32[32,512]{1,0:T(8,128)}, f32[32,512]{1,0:T(8,128)S(1)}, u32[]{:S(2)}, u32[]{:S(2)}) collective-permute-start(f32[32,512]{1,0:T(8,128)} %get-tuple-element.14), channel_id=1, source_target_pairs={{0,128},{32,160},{64,192},{96,224},{128,0},{160,32},{192,64},{224,... | collective-permute-start | bytes 196616 | tf_op jit(solution)/shard_map/ppermute | solution.py:314
  65.1 11.8 %collective-permute-start.11 = (f32[32,512]{1,0:T(8,128)}, f32[32,512]{1,0:T(8,128)S(1)}, u32[]{:S(2)}, u32[]{:S(2)}) collective-permute-start(f32[32,512]{1,0:T(8,128)} %get-tuple-element.15), channel_id=1, source_target_pairs={{0,160},{32,192},{64,224},{96,0},{128,32},{160,64},{192,96},{224,1... | collective-permute-start | bytes 196616 | tf_op jit(solution)/shard_map/ppermute | solution.py:314
  65.2 11.7 %collective-permute-start.12 = (f32[32,512]{1,0:T(8,128)}, f32[32,512]{1,0:T(8,128)S(1)}, u32[]{:S(2)}, u32[]{:S(2)}) collective-permute-start(f32[32,512]{1,0:T(8,128)} %get-tuple-element.16), channel_id=1, source_target_pairs={{0,192},{32,224},{64,0},{96,32},{128,64},{160,96},{192,128},{224,1... | collective-permute-start | bytes 196616 | tf_op jit(solution)/shard_map/ppermute | solution.py:314
  66.2 11.4 %collective-permute-start.13 = (f32[32,512]{1,0:T(8,128)}, f32[32,512]{1,0:T(8,128)S(1)}, u32[]{:S(2)}, u32[]{:S(2)}) collective-permute-start(f32[32,512]{1,0:T(8,128)} %get-tuple-element.17), channel_id=1, source_target_pairs={{0,224},{32,0},{64,32},{96,64},{128,96},{160,128},{192,160},{224,1... | collective-permute-start | bytes 196616 | tf_op jit(solution)/shard_map/ppermute | solution.py:314
  70.7 6.9 %collective-permute-start.7 = (f32[32,512]{1,0:T(8,128)}, f32[32,512]{1,0:T(8,128)S(1)}, u32[]{:S(2)}, u32[]{:S(2)}) collective-permute-start(f32[32,512]{1,0:T(8,128)} %get-tuple-element.11), channel_id=1, source_target_pairs={{0,32},{32,64},{64,96},{96,128},{128,160},{160,192},{192,224},{224... | collective-permute-start | bytes 196616 | tf_op jit(solution)/shard_map/ppermute | solution.py:314
  70.7 9.0 %collective-permute-start.8 = (f32[32,512]{1,0:T(8,128)}, f32[32,512]{1,0:T(8,128)S(1)}, u32[]{:S(2)}, u32[]{:S(2)}) collective-permute-start(f32[32,512]{1,0:T(8,128)} %get-tuple-element.12), channel_id=1, source_target_pairs={{0,64},{32,96},{64,128},{96,160},{128,192},{160,224},{192,0},{224,... | collective-permute-start | bytes 196616 | tf_op jit(solution)/shard_map/ppermute | solution.py:314
  76.9 8.5 %collective-permute-start.9 = (f32[32,512]{1,0:T(8,128)}, f32[32,512]{1,0:T(8,128)S(1)}, u32[]{:S(2)}, u32[]{:S(2)}) collective-permute-start(f32[32,512]{1,0:T(8,128)} %get-tuple-element.13), channel_id=1, source_target_pairs={{0,96},{32,128},{64,160},{96,192},{128,224},{160,0},{192,32},{224,... | collective-permute-start | bytes 196616 | tf_op jit(solution)/shard_map/ppermute | solution.py:314
  85.4 0.8 copy-start.1

commit v6 on v5

--- a/solution.py
+++ b/solution.py
@@ -18,7 +18,7 @@
 M = 256
 STACK_MIB = 62
 MERGE_MIB = 60
-MIX_MIB = 56
+MIX_MIB = 24
 BACK_MIB = 24
 F32 = jnp.float32
 BF16 = jnp.bfloat16
@@ -207,7 +207,7 @@
 
 
 def mix_kernel(z, message, *refs):
-    out, (held, total, ins, outs) = refs[:NZ], refs[NZ:]
+    out, (held, total, low, ins, outs) = refs[:NZ], refs[NZ:]
     fetches = []
     for n in range(GROUPS):
         place = pl.ds(n * GROUP, GROUP)
@@ -231,7 +231,11 @@
         both = matmul(factor, jnp.concatenate(columns, axis=1), ((1,), (0,)))
         sums = both[:WIDTH] + both[WIDTH:]
         total[...] = sums if n == 0 else total[...] + sums
-    sends = [pltpu.make_async_copy(total.at[pl.ds(n * PART, PART)], out[n], outs.at[n]) for n in range(NZ)]
+    low[...] = total[...].astype(BF16)
+    out[0][...] = total[:PART]
+    sends = []
+    for n in range(1, NZ):
+        sends.append(pltpu.make_async_copy(low.at[pl.ds(n * PART, PART)], out[n], outs.at[n - 1]))
     for copy in sends:
         copy.start()
     for copy in sends:
@@ -242,37 +246,39 @@
     return pl.pallas_call(
         mix_kernel,
         in_specs=[SCALARS, ANY],
-        out_specs=[ANY] * NZ,
+        out_specs=[WHOLE] + [ANY] * (NZ - 1),
         scratch_shapes=[
             pltpu.VMEM((NG, CARD + 1, PER, LANES), BF16),
             pltpu.VMEM((WIDTH, D), F32),
+            pltpu.VMEM((WIDTH, D), BF16),
             pltpu.SemaphoreType.DMA((GROUPS,)),
-            pltpu.SemaphoreType.DMA((NZ,)),
+            pltpu.SemaphoreType.DMA((NZ - 1,)),
         ],
-        out_shape=[jax.ShapeDtypeStruct((PART, D), F32)] * NZ,
+        out_shape=[jax.ShapeDtypeStruct((PART, D), F32)]
+        + [jax.ShapeDtypeStruct((PART, D), BF16)] * (NZ - 1),
         compiler_params=vmem(MIX_MIB),
         cost_estimate=pl.CostEstimate(flops=4 * NG * K * PER * WIDTH * D, bytes_accessed=3 << 20, transcendentals=0),
         name="mix",
     )(z, message)
 
 
-def total_kernel(*refs):
+def total_kernel(own, *refs):
     *sums, out = refs
-    total = sums[0][...]
-    for part in sums[1:]:
-        total += part[...]
+    total = own[...]
+    for part in sums:
+        total += part[...].astype(F32)
     for e in range(E):
         out[e] = total[ROWS * e : ROWS * (e + 1)]
 
 
-def total(sums):
+def total(own, sums):
     return pl.pallas_call(
         total_kernel,
         out_shape=jax.ShapeDtypeStruct((E, ROWS, D), F32),
         compiler_params=vmem(8),
         cost_estimate=pl.CostEstimate(flops=WIDTH * D, bytes_accessed=5 * WIDTH * D, transcendentals=0),
         name="total",
-    )(*sums)
+    )(own, *sums)
 
 
 def back_kernel(counts, grad, merged, out, pick, held, outs):
@@ -321,8 +327,8 @@
     rows = stack([own] + [along_z(own, n) for n in range(1, NZ)])
     merged = swap(merge(z, message, rows), PLANE)
     mixed = mix(z, message)
-    sums = [mixed[0]] + [along_z(mixed[n], n) for n in range(1, NZ)]
-    return back(atom_counts, out_grad, merged), total(sums)
+    sums = [along_z(mixed[n], n) for n in range(1, NZ)]
+    return back(atom_counts, out_grad, merged), total(mixed[0], sums)
 
 
 def solution(mesh):

time: 90.5 us -> 87.3 us (0.965)
  the two profiles are of different devices: /device:TPU:34 before, /device:TPU:9 now
where the time goes in v6:
time: 87.3 us; the launch traced here: 85.9 us
  starting transfers between devices  45.2 us (52%)
  waiting for transfers between devices  19.9 us (23%)
  Pallas kernels  19.2 us (22%)
  between operations  0.97 us (1%)
    ppermute x14, starting transfers between devices, along_z(): return lax.ppermute(array, 'z', [(i, (i + by) % NZ) for i in range(NZ)])  31.9 us
    all_to_all x2, waiting for transfers between devices, swap(): return lax.all_to_all(array, axes, 0, 0, tiled=True)  13.7 us
    all_to_all x2, starting transfers between devices, swap(): return lax.all_to_all(array, axes, 0, 0, tiled=True)  13.3 us
    ppermute x14, waiting for transfers between devices, along_z(): return lax.ppermute(array, 'z', [(i, (i + by) % NZ) for i in range(NZ)])  6.24 us
    pallas_call x1, Pallas kernels, outer(): pl.pallas_call(outer_kernel, in_specs=[SCALARS, WHOLE, ANY, ANY], out_spe...  5.43 us
    pallas_call x1, Pallas kernels, merge(): pl.pallas_call(merge_kernel, in_specs=[SCALARS, ANY, ANY], out_specs=ANY,...  4.28 us
    pallas_call x1, Pallas kernels, mix(): pl.pallas_call(mix_kernel, in_specs=[SCALARS, ANY], out_specs=[WHOLE] + [...  4.21 us
    pallas_call x1, Pallas kernels, back(): pl.pallas_call(back_kernel, in_specs=[SCALARS, WHOLE, WHOLE], out_specs=A...  2.91 us
  transfers between devices with their start and end apart: 16, of which 7 were waited for; matrix products, arithmetic and copies ran while one was open for 0% of the time, Pallas kernels for 8%

profile of v6, /device:TPU:9, one launch (start us, length us, event | category | flops | bytes accessed | tf_op | source)
XLA Modules:
  0.0 85.9 jit_solution(4908702109328138722)
XLA Ops:
  0.6 5.4 %outer.1 = bf16[32,17,16,128]{3,2,1,0:T(8,128)(2,1)} custom-call(s32[4]{0:T(128)} %counts.3, s32[4,16]{1,0:T(4,128)} %fixed.1, bf16[4,256,512]{2,1,0:T(8,128)(2,1)} %x.1, bf16[4,256,512]{2,1,0:T(8,128)(2,1)} %grad.3), custom_call_target="tpu_custom_call" | custom-call | flops 1073741824 | bytes 4194304 | tf_op jit(solution)/shard_map/outer/pallas_call | solution.py:107
  6.1 0.0 copy-start.10
  6.1 7.9 %all-to-all-start = ((bf16[32,17,16,128]{3,2,1,0:T(8,128)(2,1)}), bf16[32,17,16,128]{3,2,1,0:T(8,128)(2,1)}, u32[]{:S(2)}, u32[]{:S(2)}) async-start(bf16[32,17,16,128]{3,2,1,0:T(8,128)(2,1)} %outer.1), calls=%async_computation | async-start | bytes 4456448 | tf_op jit(solution)/shard_map/all_to_all | solution.py:316
  14.0 0.0 copy-done.10
  14.0 0.0 copy-start.2
  14.0 1.7 %collective-permute-start = (bf16[32,512]{1,0:T(8,128)(2,1)S(1)}, bf16[32,512]{1,0:T(8,128)(2,1)S(1)}, u32[]{:S(2)}, u32[]{:S(2)}) collective-permute-start(bf16[32,512]{1,0:T(8,128)(2,1)S(1)} %reshape.11.refs_0_), channel_id=1, source_target_pairs={{0,32},{32,64},{64,96},{96,128},{128,160},{160,192},{192,224},{224... | collective-permute-start | bytes 98312 | tf_op jit(solution)/shard_map/ppermute | solution.py:320
  15.7 3.0 %collective-permute-start.1 = (bf16[32,512]{1,0:T(8,128)(2,1)S(1)}, bf16[32,512]{1,0:T(8,128)(2,1)S(1)}, u32[]{:S(2)}, u32[]{:S(2)}) collective-permute-start(bf16[32,512]{1,0:T(8,128)(2,1)S(1)} %reshape.11.refs_0_), channel_id=1, source_target_pairs={{0,64},{32,96},{64,128},{96,160},{128,192},{160,224},{192,0},{224,... | collective-permute-start | bytes 98312 | tf_op jit(solution)/shard_map/ppermute | solution.py:320
  18.7 3.7 %collective-permute-start.2 = (bf16[32,512]{1,0:T(8,128)(2,1)S(1)}, bf16[32,512]{1,0:T(8,128)(2,1)S(1)}, u32[]{:S(2)}, u32[]{:S(2)}) collective-permute-start(bf16[32,512]{1,0:T(8,128)(2,1)S(1)} %reshape.11.refs_0_), channel_id=1, source_target_pairs={{0,96},{32,128},{64,160},{96,192},{128,224},{160,0},{192,32},{224,... | collective-permute-start | bytes 98312 | tf_op jit(solution)/shard_map/ppermute | solution.py:320
  22.5 0.5 collective-permute-start.3
  22.9 4.5 %collective-permute-start.4 = (bf16[32,512]{1,0:T(8,128)(2,1)S(1)}, bf16[32,512]{1,0:T(8,128)(2,1)S(1)}, u32[]{:S(2)}, u32[]{:S(2)}) collective-permute-start(bf16[32,512]{1,0:T(8,128)(2,1)S(1)} %reshape.11.refs_0_), channel_id=1, source_target_pairs={{0,160},{32,192},{64,224},{96,0},{128,32},{160,64},{192,96},{224,1... | collective-permute-start | bytes 98312 | tf_op jit(solution)/shard_map/ppermute | solution.py:320
  27.4 0.0 collective-permute-done.refs_1_
  27.4 2.4 %collective-permute-start.5 = (bf16[32,512]{1,0:T(8,128)(2,1)S(1)}, bf16[32,512]{1,0:T(8,128)(2,1)S(1)}, u32[]{:S(2)}, u32[]{:S(2)}) collective-permute-start(bf16[32,512]{1,0:T(8,128)(2,1)S(1)} %reshape.11.refs_0_), channel_id=1, source_target_pairs={{0,192},{32,224},{64,0},{96,32},{128,64},{160,96},{192,128},{224,1... | collective-permute-start | bytes 98312 | tf_op jit(solution)/shard_map/ppermute | solution.py:320
  29.8 0.0 collective-permute-done.1.refs_2_
  29.8 0.7 collective-permute-start.6
  30.5 0.0 collective-permute-done.2.refs_3_
  30.5 0.0 collective-permute-done.3.refs_4_
  30.6 0.0 copy-start.6
  30.6 0.0 collective-permute-done.4.refs_5_
  30.6 2.4 %collective-permute-done.5.refs_6_ = bf16[32,512]{1,0:T(8,128)(2,1)S(1)} collective-permute-done((bf16[32,512]{1,0:T(8,128)(2,1)S(1)}, bf16[32,512]{1,0:T(8,128)(2,1)S(1)}, u32[]{:S(2)}, u32[]{:S(2)}) %collective-permute-start.5) | collective-permute-done | bytes 32800 | tf_op jit(solution)/shard_map/ppermute | solution.py:320
  33.0 0.7 collective-permute-done.6.refs_7_
  33.8 0.0 copy-done.5
  33.8 0.0 copy-done.6
  33.8 0.0 copy-done.7
  33.8 0.6 copy-done.9
  34.4 1.7 %stack.1.rows = bf16[512,512]{1,0:T(8,128)(2,1)} custom-call(bf16[32,512]{1,0:T(8,128)(2,1)} %copy-done.2, bf16[32,512]{1,0:T(8,128)(2,1)} %copy-done.3, bf16[32,512]{1,0:T(8,128)(2,1)} %copy-done.4, bf16[32,512]{1,0:T(8,128)(2,1)} %copy-done.5, bf16[32,512]{1,0:T(8,128)(2,1)} %copy-done.6, bf16[32,512]{1,0:T(8,128)(2,1)} %copy-done.7, ...), custom_call_target="tpu_custom_call" | custom-call | bytes 786432 | tf_op jit(solution)/shard_map/stack/pallas_call | solution.py:148
  36.1 8.3 %all-to-all-done.message = bf16[32,17,16,128]{3,2,1,0:T(8,128)(2,1)} async-done(((bf16[32,17,16,128]{3,2,1,0:T(8,128)(2,1)}), bf16[32,17,16,128]{3,2,1,0:T(8,128)(2,1)}, u32[]{:S(2)}, u32[]{:S(2)}) %all-to-all-start) | async-done | bytes 2228256 | tf_op jit(solution)/shard_map/all_to_all | solution.py:316
  44.4 4.3 %merge.1 = bf16[32,4,16,512]{3,2,1,0:T(8,128)(2,1)} custom-call(s32[1]{0:T(128)} %bitcast.z, bf16[32,17,16,128]{3,2,1,0:T(8,128)(2,1)} %all-to-all-done.message, bf16[512,512]{1,0:T(8,128)(2,1)} %stack.1.rows), custom_call_target="tpu_custom_call" | custom-call | flops 1073741824 | bytes 3145728 | tf_op jit(solution)/shard_map/merge/pallas_call | solution.py:191
  48.7 5.3 %all-to-all-start.1 = ((bf16[32,4,16,512]{3,2,1,0:T(8,128)(2,1)}), bf16[32,4,16,512]{3,2,1,0:T(8,128)(2,1)S(1)}, u32[]{:S(2)}, u32[]{:S(2)}) async-start(bf16[32,4,16,512]{3,2,1,0:T(8,128)(2,1)} %merge.1), calls=%async_computation.1 | async-start | bytes 4194304 | tf_op jit(solution)/shard_map/all_to_all | solution.py:316
  54.0 0.0 copy-start
  54.1 0.0 copy-start.1
  54.1 4.2 %mix.1 = (f32[32,512]{1,0:T(8,128)S(1)}, bf16[32,512]{1,0:T(8,128)(2,1)S(1)}, bf16[32,512]{1,0:T(8,128)(2,1)S(1)}, bf16[32,512]{1,0:T(8,128)(2,1)S(1)}, bf16[32,...) custom-call(s32[1]{0:T(128)} %bitcast.z, ...), custom_call_target="tpu_custom_call" | custom-call | flops 1073741824 | bytes 3145728 | tf_op jit(solution)/shard_map/mix/pallas_call | solution.py:246
  58.3 7.1 %collective-permute-start.10 = (bf16[32,512]{1,0:T(8,128)(2,1)S(1)}, bf16[32,512]{1,0:T(8,128)(2,1)S(1)}, u32[]{:S(2)}, u32[]{:S(2)}) collective-permute-start(bf16[32,512]{1,0:T(8,128)(2,1)S(1)} %get-tuple-element.14), channel_id=1, source_target_pairs={{0,128},{32,160},{64,192},{96,224},{128,0},{160,32},{192,64},{224,... | collective-permute-start | bytes 98312 | tf_op jit(solution)/shard_map/ppermute | solution.py:320
  65.4 0.0 collective-permute-start.11
  65.4 4.0 %collective-permute-start.12 = (bf16[32,512]{1,0:T(8,128)(2,1)S(1)}, bf16[32,512]{1,0:T(8,128)(2,1)S(1)}, u32[]{:S(2)}, u32[]{:S(2)}) collective-permute-start(bf16[32,512]{1,0:T(8,128)(2,1)S(1)} %get-tuple-element.16), channel_id=1, source_target_pairs={{0,192},{32,224},{64,0},{96,32},{128,64},{160,96},{192,128},{224,1... | collective-permute-start | bytes 98312 | tf_op jit(solution)/shard_map/ppermute | solution.py:320
  69.5 0.7 collective-permute-start.13
  70.2 0.7 collective-permute-start.7
  70.9 0.0 collective-permute-done.10.refs_3_
  70.9 0.0 collective-permute-start.8
  70.9 0.0 collective-permute-done.11.refs_4_
  70.9 2.8 %collective-permute-start.9 = (bf16[32,512]{1,0:T(8,128)(2,1)S(1)}, bf16[32,512]{1,0:T(8,128)(2,1)S(1)}, u32[]{:S(2)}, u32[]{:S(2)}) collective-permute-start(bf16[32,512]{1,0:T(8,128)(2,1)S(1)} %get-tuple-element.13), channel_id=1, source_target_pairs={{0,96},{32,128},{64,160},{96,192},{128,224},{160,0},{192,32},{224,... | collective-permute-start | bytes 98312 | tf_op jit(solution)/shard_map/ppermute | solution.py:320
  73.7 0.0 collective-permute-done.12.refs_5_
  73.8 0.0 collective-permute-done.13.refs_6_
  73.8 0.6 collective-permute-done.7.refs_0_
  74.3 1.8 %collective-permute-done.8.refs_1_ = bf16[32,512]{1,0:T(8,128)(2,1)S(1)} collective-permute-done((bf16[32,512]{1,0:T(8,128)(2,1)S(1)}, bf16[32,512]{1,0:T(8,128)(2,1)S(1)}, u32[]{:S(2)}, u32[]{:S(2)}) %collective-permute-start.8) | collective-permute-done | bytes 32800 | tf_op jit(solution)/shard_map/ppermute | solution.py:320
  76.1 0.7 collective-permute-done.9.refs_2_
  76.8 0.7 total.1
  77.5 5.4 %all-to-all-done.1.merged = bf16[32,4,16,512]{3,2,1,0:T(8,128)(2,1)S(1)} async-done(((bf16[32,4,16,512]{3,2,1,0:T(8,128)(2,1)}), bf16[32,4,16,512]{3,2,1,0:T(8,128)(2,1)S(1)}, u32[]{:S(2)}, u32[]{:S(2)}) %all-to-all-start.1) | async-done | bytes 2097184 | tf_op jit(solution)/shard_map/all_to_all | solution.py:316
  82.9 2.9 %back.1 = bf16[4,256,512]{2,1,0:T(8,128)(2,1)} custom-call(s32[4]{0:T(128)S(1)} %copy-done.1, bf16[4,256,512]{2,1,0:T(8,128)(2,1)S(1)} %copy-done, bf16[32,4,16,512]{3,2,1,0:T(8,128)(2,1)S(1)} %all-to-all-done.1.merged), custom_call_target="tpu_custom_call" | custom-call | flops 1073741824 | bytes 4194304 | tf_op jit(solution)/shard_map/back/pallas_call | solution.py:299
  (13 shorter events, 0.0 us)
Async XLA Ops:
  6.1 7.9 %copy-start.10 = (bf16[16,2,512]{2,1,0:T(2,128)(2,1)S(1)}, bf16[16,2,512]{2,1,0:T(2,128)(2,1)}, u32[]{:S(2)}) copy-start(bf16[16,2,512]{2,1,0:T(2,128)(2,1)} %param.9) | copy-start | bytes 98308
  6.1 38.3 %all-to-all-start = ((bf16[32,17,16,128]{3,2,1,0:T(8,128)(2,1)}), bf16[32,17,16,128]{3,2,1,0:T(8,128)(2,1)}, u32[]{:S(2)}, u32[]{:S(2)}) async-start(bf16[32,17,16,128]{3,2,1,0:T(8,128)(2,1)} %outer.1), calls=%async_computation | async-start | bytes 4456448 | tf_op jit(solution)/shard_map/all_to_all | solution.py:316
  14.0 19.7 %copy-start.2 = (bf16[32,512]{1,0:T(8,128)(2,1)}, bf16[32,512]{1,0:T(8,128)(2,1)S(1)}, u32[]{:S(2)}) copy-start(bf16[32,512]{1,0:T(8,128)(2,1)S(1)} %reshape.11.refs_0_) | copy-start | bytes 98308
  14.0 13.4 %collective-permute-start = (bf16[32,512]{1,0:T(8,128)(2,1)S(1)}, bf16[32,512]{1,0:T(8,128)(2,1)S(1)}, u32[]{:S(2)}, u32[]{:S(2)}) collective-permute-start(bf16[32,512]{1,0:T(8,128)(2,1)S(1)} %reshape.11.refs_0_), channel_id=1, source_target_pairs={{0,32},{32,64},{64,96},{96,128},{128,160},{160,192},{192,224},{224... | collective-permute-start | bytes 98312 | tf_op jit(solution)/shard_map/ppermute | solution.py:320
  15.7 14.1 %collective-permute-start.1 = (bf16[32,512]{1,0:T(8,128)(2,1)S(1)}, bf16[32,512]{1,0:T(8,128)(2,1)S(1)}, u32[]{:S(2)}, u32[]{:S(2)}) collective-permute-start(bf16[32,512]{1,0:T(8,128)(2,1)S(1)} %reshape.11.refs_0_), channel_id=1, source_target_pairs={{0,64},{32,96},{64,128},{96,160},{128,192},{160,224},{192,0},{224,... | collective-permute-start | bytes 98312 | tf_op jit(solution)/shard_map/ppermute | solution.py:320
  18.7 11.8 %collective-permute-start.2 = (bf16[32,512]{1,0:T(8,128)(2,1)S(1)}, bf16[32,512]{1,0:T(8,128)(2,1)S(1)}, u32[]{:S(2)}, u32[]{:S(2)}) collective-permute-start(bf16[32,512]{1,0:T(8,128)(2,1)S(1)} %reshape.11.refs_0_), channel_id=1, source_target_pairs={{0,96},{32,128},{64,160},{96,192},{128,224},{160,0},{192,32},{224,... | collective-permute-start | bytes 98312 | tf_op jit(solution)/shard_map/ppermute | solution.py:320
  22.5 8.1 %collective-permute-start.3 = (bf16[32,512]{1,0:T(8,128)(2,1)S(1)}, bf16[32,512]{1,0:T(8,128)(2,1)S(1)}, u32[]{:S(2)}, u32[]{:S(2)}) collective-permute-start(bf16[32,512]{1,0:T(8,128)(2,1)S(1)} %reshape.11.refs_0_), channel_id=1, source_target_pairs={{0,128},{32,160},{64,192},{96,224},{128,0},{160,32},{192,64},{224,... | collective-permute-start | bytes 98312 | tf_op jit(solution)/shard_map/ppermute | solution.py:320
  22.9 7.6 %collective-permute-start.4 = (bf16[32,512]{1,0:T(8,128)(2,1)S(1)}, bf16[32,512]{1,0:T(8,128)(2,1)S(1)}, u32[]{:S(2)}, u32[]{:S(2)}) collective-permute-start(bf16[32,512]{1,0:T(8,128)(2,1)S(1)} %reshape.11.refs_0_), channel_id=1, source_target_pairs={{0,160},{32,192},{64,224},{96,0},{128,32},{160,64},{192,96},{224,1... | collective-permute-start | bytes 98312 | tf_op jit(solution)/shard_map/ppermute | solution.py:320
  27.4 6.3 %copy-start.3 = (bf16[32,512]{1,0:T(8,128)(2,1)}, bf16[32,512]{1,0:T(8,128)(2,1)S(1)}, u32[]{:S(2)}) copy-start(bf16[32,512]{1,0:T(8,128)(2,1)S(1)} %collective-permute-done.refs_1_) | copy-start | bytes 98308
  27.4 5.6 %collective-permute-start.5 = (bf16[32,512]{1,0:T(8,128)(2,1)S(1)}, bf16[32,512]{1,0:T(8,128)(2,1)S(1)}, u32[]{:S(2)}, u32[]{:S(2)}) collective-permute-start(bf16[32,512]{1,0:T(8,128)(2,1)S(1)} %reshape.11.refs_0_), channel_id=1, source_target_pairs={{0,192},{32,224},{64,0},{96,32},{128,64},{160,96},{192,128},{224,1... | collective-permute-start | bytes 98312 | tf_op jit(solution)/shard_map/ppermute | solution.py:320
  29.8 3.9 %copy-start.4 = (bf16[32,512]{1,0:T(8,128)(2,1)}, bf16[32,512]{1,0:T(8,128)(2,1)S(1)}, u32[]{:S(2)}) copy-start(bf16[32,512]{1,0:T(8,128)(2,1)S(1)} %collective-permute-done.1.refs_2_) | copy-start | bytes 98308
  29.8 3.9 %collective-permute-start.6 = (bf16[32,512]{1,0:T(8,128)(2,1)S(1)}, bf16[32,512]{1,0:T(8,128)(2,1)S(1)}, u32[]{:S(2)}, u32[]{:S(2)}) collective-permute-start(bf16[32,512]{1,0:T(8,128)(2,1)S(1)} %reshape.11.refs_0_), channel_id=1, source_target_pairs={{0,224},{32,0},{64,32},{96,64},{128,96},{160,128},{192,160},{224,1... | collective-permute-start | bytes 98312 | tf_op jit(solution)/shard_map/ppermute | solution.py:320
  30.5 3.2 %copy-start.5 = (bf16[32,512]{1,0:T(8,128)(2,1)}, bf16[32,512]{1,0:T(8,128)(2,1)S(1)}, u32[]{:S(2)}) copy-start(bf16[32,512]{1,0:T(8,128)(2,1)S(1)} %collective-permute-done.2.refs_3_) | copy-start | bytes 98308
  30.6 3.2 %copy-start.6 = (bf16[32,512]{1,0:T(8,128)(2,1)}, bf16[32,512]{1,0:T(8,128)(2,1)S(1)}, u32[]{:S(2)}) copy-start(bf16[32,512]{1,0:T(8,128)(2,1)S(1)} %collective-permute-done.3.refs_4_) | copy-start | bytes 98308
  30.6 3.2 %copy-start.7 = (bf16[32,512]{1,0:T(8,128)(2,1)}, bf16[32,512]{1,0:T(8,128)(2,1)S(1)}, u32[]{:S(2)}) copy-start(bf16[32,512]{1,0:T(8,128)(2,1)S(1)} %collective-permute-done.4.refs_5_) | copy-start | bytes 98308
  33.0 0.8 copy-start.8
  33.8 0.6 copy-start.9
  48.7 34.2 %all-to-all-start.1 = ((bf16[32,4,16,512]{3,2,1,0:T(8,128)(2,1)}), bf16[32,4,16,512]{3,2,1,0:T(8,128)(2,1)S(1)}, u32[]{:S(2)}, u32[]{:S(2)}) async-start(bf16[32,4,16,512]{3,2,1,0:T(8,128)(2,1)} %merge.1), calls=%async_computation.1 | async-start | bytes 4194304 | tf_op jit(solution)/shard_map/all_to_all | solution.py:316
  54.0 28.8 %copy-start = (bf16[4,256,512]{2,1,0:T(8,128)(2,1)S(1)}, bf16[4,256,512]{2,1,0:T(8,128)(2,1)}, u32[]{:S(2)}) copy-start(bf16[4,256,512]{2,1,0:T(8,128)(2,1)} %grad.3) | copy-start | bytes 3145732
  54.1 28.8 %copy-start.1 = (s32[4]{0:T(128)S(1)}, s32[4]{0:T(128)}, u32[]{:S(2)}) copy-start(s32[4]{0:T(128)} %counts.3) | copy-start | bytes 52
  58.3 12.7 %collective-permute-start.10 = (bf16[32,512]{1,0:T(8,128)(2,1)S(1)}, bf16[32,512]{1,0:T(8,128)(2,1)S(1)}, u32[]{:S(2)}, u32[]{:S(2)}) collective-permute-start(bf16[32,512]{1,0:T(8,128)(2,1)S(1)} %get-tuple-element.14), channel_id=1, source_target_pairs={{0,128},{32,160},{64,192},{96,224},{128,0},{160,32},{192,64},{224,... | collective-permute-start | bytes 98312 | tf_op jit(solution)/shard_map/ppermute | solution.py:320
  65.4 5.5 %collective-permute-start.11 = (bf16[32,512]{1,0:T(8,128)(2,1)S(1)}, bf16[32,512]{1,0:T(8,128)(2,1)S(1)}, u32[]{:S(2)}, u32[]{:S(2)}) collective-permute-start(bf16[32,512]{1,0:T(8,128)(2,1)S(1)} %get-tuple-element.15), channel_id=1, source_target_pairs={{0,160},{32,192},{64,224},{96,0},{128,32},{160,64},{192,96},{224,1... | collective-permute-start | bytes 98312 | tf_op jit(solution)/shard_map/ppermute | solution.py:320
  65.4 8.3 %collective-permute-start.12 = (bf16[32,512]{1,0:T(8,128)(2,1)S(1)}, bf16[32,512]{1,0:T(8,128)(2,1)S(1)}, u32[]{:S(2)}, u32[]{:S(2)}) collective-permute-start(bf16[32,512]{1,0:T(8,128)(2,1)S(1)} %get-tuple-element.16), channel_id=1, source_target_pairs={{0,192},{32,224},{64,0},{96,32},{128,64},{160,96},{192,128},{224,1... | collective-permute-start | bytes 98312 | tf_op jit(solution)/shard_map/ppermute | solution.py:320
  69.5 4.3 %collective-permute-start.13 = (bf16[32,512]{1,0:T(8,128)(2,1)S(1)}, bf16[32,512]{1,0:T(8,128)(2,1)S(1)}, u32[]{:S(2)}, u32[]{:S(2)}) collective-permute-start(bf16[32,512]{1,0:T(8,128)(2,1)S(1)} %get-tuple-element.17), channel_id=1, source_target_pairs={{0,224},{32,0},{64,32},{96,64},{128,96},{160,128},{192,160},{224,1... | collective-permute-start | bytes 98312 | tf_op jit(solution)/shard_map/ppermute | solution.py:320
  70.2 4.1 %collective-permute-start.7 = (bf16[32,512]{1,0:T(8,128)(2,1)S(1)}, bf16[32,512]{1,0:T(8,128)(2,1)S(1)}, u32[]{:S(2)}, u32[]{:S(2)}) collective-permute-start(bf16[32,512]{1,0:T(8,128)(2,1)S(1)} %get-tuple-element.11), channel_id=1, source_target_pairs={{0,32},{32,64},{64,96},{96,128},{128,160},{160,192},{192,224},{224... | collective-permute-start | bytes 98312 | tf_op jit(solution)/shard_map/ppermute | solution.py:320
  70.9 5.2 %collective-permute-start.8 = (bf16[32,512]{1,0:T(8,128)(2,1)S(1)}, bf16[32,512]{1,0:T(8,128)(2,1)S(1)}, u32[]{:S(2)}, u32[]{:S(2)}) collective-permute-start(bf16[32,512]{1,0:T(8,128)(2,1)S(1)} %get-tuple-element.12), channel_id=1, source_target_pairs={{0,64},{32,96},{64,128},{96,160},{128,192},{160,224},{192,0},{224,... | collective-permute-start | bytes 98312 | tf_op jit(solution)/shard_map/ppermute | solution.py:320
  70.9 5.9 %collective-permute-start.9 = (bf16[32,512]{1,0:T(8,128)(2,1)S(1)}, bf16[32,512]{1,0:T(8,128)(2,1)S(1)}, u32[]{:S(2)}, u32[]{:S(2)}) collective-permute-start(bf16[32,512]{1,0:T(8,128)(2,1)S(1)} %get-tuple-element.13), channel_id=1, source_target_pairs={{0,96},{32,128},{64,160},{96,192},{128,224},{160,0},{192,32},{224,... | collective-permute-start | bytes 98312 | tf_op jit(solution)/shard_map/ppermute | solution.py:320

commit v7 on v6

--- a/solution.py
+++ b/solution.py
@@ -76,9 +76,9 @@
 
     send_card = pltpu.make_async_copy(held.at[:, pl.ds(CARD, 1)], out.at[:, pl.ds(CARD, 1)], outs.at[K])
     fetches = [fetch(k) for k in range(K)]
-    for pair in fetches:
-        for copy in pair:
-            copy.start()
+    for side in range(2):
+        for pair in fetches:
+            pair[side].start()
     sheet[...] = jnp.zeros_like(sheet)
     sheet[0:K] = card(fixed[...])
     held[:, CARD] = jnp.broadcast_to(sheet[...].astype(BF16)[None], (NG, PER, LANES))
@@ -86,7 +86,9 @@
     pick[...] = order()
     for k in range(K):
         fetches[k][0].wait()
-        turned = matmul(xs[k], pick[...], ((1,), (1,))).astype(BF16).T
+    moved = matmul(xs[...].reshape(K * M, D), pick[...], ((1,), (1,))).astype(BF16)
+    for k in range(K):
+        turned = moved[k * M : (k + 1) * M].T
         fetches[k][1].wait()
         product = matmul(turned, masked_of(grads[k], counts[k]), ((1,), (0,))).astype(BF16)
         for tile in range(TILES):
@@ -137,28 +139,36 @@
     return ((part >> 1) & (E - 1)) + ((part >> 8) << 4)
 
 
-def stack_kernel(*refs):
+HALF = 8
+LINES = HALF // ROWS
+
+
+def stack_kernel(z, *refs):
     *blocks, out = refs
     for n, block in enumerate(blocks):
-        for half in (0, WIDTH):
-            out[half + n * PART : half + (n + 1) * PART] = block[...]
-
-
-def stack(blocks):
+        line = (z[0] - n + NZ) & (NZ - 1)
+        half, place = line // LINES, (line & (LINES - 1)) * PART
+        for part in range(2):
+            out[half, pl.ds(pl.multiple_of(part * LINES * PART + place, PART), PART)] = block[...]
+
+
+def stack(z, blocks):
     return pl.pallas_call(
         stack_kernel,
-        out_shape=jax.ShapeDtypeStruct((2 * WIDTH, D), BF16),
+        in_specs=[SCALARS] + [WHOLE] * NZ,
+        out_specs=WHOLE,
+        out_shape=jax.ShapeDtypeStruct((2, WIDTH, D), BF16),
         compiler_params=vmem(STACK_MIB),
         cost_estimate=pl.CostEstimate(flops=0, bytes_accessed=6 * WIDTH * D, transcendentals=0),
         name="stack",
-    )(*blocks)
+    )(z, *blocks)
 
 
 GROUPS = NG // GROUP
 TALL = STEP * PER
 
 
-def merge_kernel(z, message, rows, out, cards, weights, held, ins, outs):
+def merge_kernel(message, rows, out, cards, weights, wide, held, ins, outs):
     fetch_cards = pltpu.make_async_copy(message.at[:, pl.ds(CARD, 1)], cards, ins.at[0])
     fetch_rows = pltpu.make_async_copy(rows, weights, ins.at[1])
 
@@ -168,42 +178,46 @@
 
     fetch_cards.start()
     fetch_rows.start()
-    tall = row_of((TALL, 1), 0)
-    pick = one_hot(((tall >> 6) << 4) + ((tall >> 4) & (K - 1)) == row_of((1, GROUP * PER), 1))
-    part = row_of((1, 2 * WIDTH), 1)
-    widen = one_hot(row_of((LANES, 1), 0) == source_of(part))
-    same = (tall & (PER - 1)) == line_of(part, z[0], -1)
+    system = row_of((NG * K, 1), 0)
+    pick = one_hot(((system >> 2) << 4) + (system & (K - 1)) == row_of((1, NG * PER), 1))
+    col = row_of((1, WIDTH), 1)
+    source = ((col >> 1) & (E - 1)) + ((col >> 7) << 4)
+    widen = one_hot(row_of((LANES, 1), 0) == source)
+    place = (((col >> 5) & (LINES - 1)) << 1) + (col & 1)
+    same = row_of((HALF, 1), 0) == place
     fetch_cards.wait()
+    values = matmul(pick, cards[...].reshape(NG * PER, LANES), ((1,), (0,))).astype(BF16)
+    wide[...] = matmul(values, widen, ((1,), (0,)))
+    fetch_rows.wait()
     for n in range(GROUPS):
-        tiles = cards[n * GROUP : (n + 1) * GROUP].reshape(GROUP * PER, LANES)
-        values = matmul(pick, tiles, ((1,), (0,))).astype(BF16)
-        factor = jnp.where(same, matmul(values, widen, ((1,), (0,))), 0.0).astype(BF16)
-        if n == 0:
-            fetch_rows.wait()
-        merged = matmul(factor, weights[...], ((1,), (0,))).astype(BF16)
+        tall = jnp.where(same[None], wide[n * STEP : (n + 1) * STEP][:, None, :], 0.0)
+        factor = tall.reshape(STEP * HALF, WIDTH).astype(BF16)
+        halves = [matmul(factor, weights[h], ((1,), (0,))).reshape(STEP, HALF, D) for h in range(2)]
+        merged = jnp.concatenate(halves, axis=1).astype(BF16)
         held[n * GROUP : (n + 1) * GROUP] = merged.reshape(GROUP, K, PER, D)
         send(n).start()
     for n in range(GROUPS):
         send(n).wait()
 
 
-def merge(z, message, rows):
+def merge(message, rows):
     return pl.pallas_call(
         merge_kernel,
-        in_specs=[SCALARS, ANY, ANY],
+        in_specs=[ANY, ANY],
         out_specs=ANY,
         scratch_shapes=[
             pltpu.VMEM((NG, 1, PER, LANES), BF16),
-            pltpu.VMEM((2 * WIDTH, D), BF16),
+            pltpu.VMEM((2, WIDTH, D), BF16),
+            pltpu.VMEM((NG * K, WIDTH), F32),
             pltpu.VMEM((NG, K, PER, D), BF16),
             pltpu.SemaphoreType.DMA((2,)),
             pltpu.SemaphoreType.DMA((GROUPS,)),
         ],
         out_shape=jax.ShapeDtypeStruct((NG, K, PER, D), BF16),
         compiler_params=vmem(MERGE_MIB),
-        cost_estimate=pl.CostEstimate(flops=4 * NG * K * PER * WIDTH * D, bytes_accessed=3 << 20, transcendentals=0),
+        cost_estimate=pl.CostEstimate(flops=2 * NG * K * PER * WIDTH * D, bytes_accessed=3 << 20, transcendentals=0),
         name="merge",
-    )(z, message, rows)
+    )(message, rows)
 
 
 def mix_kernel(z, message, *refs):
@@ -324,8 +338,8 @@
     z = lax.axis_index("z").astype(jnp.int32).reshape(1)
     message = swap(outer(atom_counts, coeff_fixed, inputs, out_grad), PLANE)
     own = experts.reshape(PART, D)
-    rows = stack([own] + [along_z(own, n) for n in range(1, NZ)])
-    merged = swap(merge(z, message, rows), PLANE)
+    rows = stack(z, [own] + [along_z(own, n) for n in range(1, NZ)])
+    merged = swap(merge(message, rows), PLANE)
     mixed = mix(z, message)
     sums = [along_z(mixed[n], n) for n in range(1, NZ)]
     return back(atom_counts, out_grad, merged), total(mixed[0], sums)

time: 87.3 us -> 85.3 us (0.977)
  Pallas kernels: 19.2 us -> 17.2 us
    pallas_call x2, Pallas kernels: 5.98 us -> 4.63 us  [the longest x1 2.91 us: merge(): pl.pallas_call(merge_kernel, in_specs=[ANY, ANY], out_specs=ANY, scratch_...]
where the time goes in v7:
time: 85.3 us; the launch traced here: 83.9 us
  starting transfers between devices  45.1 us (53%)
  waiting for transfers between devices  20.1 us (24%)
  Pallas kernels  17.2 us (20%)
  between operations  0.96 us (1%)
    ppermute x14, starting transfers between devices, along_z(): return lax.ppermute(array, 'z', [(i, (i + by) % NZ) for i in range(NZ)])  31.8 us
    all_to_all x2, waiting for transfers between devices, swap(): return lax.all_to_all(array, axes, 0, 0, tiled=True)  13.9 us
    all_to_all x2, starting transfers between devices, swap(): return lax.all_to_all(array, axes, 0, 0, tiled=True)  13.3 us
    ppermute x14, waiting for transfers between devices, along_z(): return lax.ppermute(array, 'z', [(i, (i + by) % NZ) for i in range(NZ)])  6.22 us
    pallas_call x1, Pallas kernels, outer(): pl.pallas_call(outer_kernel, in_specs=[SCALARS, WHOLE, ANY, ANY], out_spe...  4.77 us
    pallas_call x1, Pallas kernels, mix(): pl.pallas_call(mix_kernel, in_specs=[SCALARS, ANY], out_specs=[WHOLE] + [...  4.2 us
    pallas_call x1, Pallas kernels, merge(): pl.pallas_call(merge_kernel, in_specs=[ANY, ANY], out_specs=ANY, scratch_...  2.91 us
    pallas_call x1, Pallas kernels, back(): pl.pallas_call(back_kernel, in_specs=[SCALARS, WHOLE, WHOLE], out_specs=A...  2.9 us
  transfers between devices with their start and end apart: 16, of which 7 were waited for; matrix products, arithmetic and copies ran while one was open for 0% of the time, Pallas kernels for 8%

profile of v7, /device:TPU:9, one launch (start us, length us, event | category | flops | bytes accessed | tf_op | source)
XLA Modules:
  0.0 83.9 jit_solution(2401836551558564039)
XLA Ops:
  0.6 4.8 %outer.1 = bf16[32,17,16,128]{3,2,1,0:T(8,128)(2,1)} custom-call(s32[4]{0:T(128)} %counts.3, s32[4,16]{1,0:T(4,128)} %fixed.1, bf16[4,256,512]{2,1,0:T(8,128)(2,1)} %x.1, bf16[4,256,512]{2,1,0:T(8,128)(2,1)} %grad.3), custom_call_target="tpu_custom_call" | custom-call | flops 1073741824 | bytes 4194304 | tf_op jit(solution)/shard_map/outer/pallas_call | solution.py:109
  5.4 0.0 copy-start.3
  5.4 7.9 %all-to-all-start = ((bf16[32,17,16,128]{3,2,1,0:T(8,128)(2,1)}), bf16[32,17,16,128]{3,2,1,0:T(8,128)(2,1)}, u32[]{:S(2)}, u32[]{:S(2)}) async-start(bf16[32,17,16,128]{3,2,1,0:T(8,128)(2,1)} %outer.1), calls=%async_computation | async-start | bytes 4456448 | tf_op jit(solution)/shard_map/all_to_all | solution.py:330
  13.3 0.0 copy-done.3
  13.4 0.0 copy-start.2
  13.4 1.7 %collective-permute-start = (bf16[32,512]{1,0:T(8,128)(2,1)S(1)}, bf16[32,512]{1,0:T(8,128)(2,1)S(1)}, u32[]{:S(2)}, u32[]{:S(2)}) collective-permute-start(bf16[32,512]{1,0:T(8,128)(2,1)S(1)} %reshape.11.refs_0_), channel_id=1, source_target_pairs={{0,32},{32,64},{64,96},{96,128},{128,160},{160,192},{192,224},{224... | collective-permute-start | bytes 98312 | tf_op jit(solution)/shard_map/ppermute | solution.py:334
  15.1 3.0 %collective-permute-start.1 = (bf16[32,512]{1,0:T(8,128)(2,1)S(1)}, bf16[32,512]{1,0:T(8,128)(2,1)S(1)}, u32[]{:S(2)}, u32[]{:S(2)}) collective-permute-start(bf16[32,512]{1,0:T(8,128)(2,1)S(1)} %reshape.11.refs_0_), channel_id=1, source_target_pairs={{0,64},{32,96},{64,128},{96,160},{128,192},{160,224},{192,0},{224,... | collective-permute-start | bytes 98312 | tf_op jit(solution)/shard_map/ppermute | solution.py:334
  18.1 3.7 %collective-permute-start.2 = (bf16[32,512]{1,0:T(8,128)(2,1)S(1)}, bf16[32,512]{1,0:T(8,128)(2,1)S(1)}, u32[]{:S(2)}, u32[]{:S(2)}) collective-permute-start(bf16[32,512]{1,0:T(8,128)(2,1)S(1)} %reshape.11.refs_0_), channel_id=1, source_target_pairs={{0,96},{32,128},{64,160},{96,192},{128,224},{160,0},{192,32},{224,... | collective-permute-start | bytes 98312 | tf_op jit(solution)/shard_map/ppermute | solution.py:334
  21.8 0.5 collective-permute-start.3
  22.3 4.5 %collective-permute-start.4 = (bf16[32,512]{1,0:T(8,128)(2,1)S(1)}, bf16[32,512]{1,0:T(8,128)(2,1)S(1)}, u32[]{:S(2)}, u32[]{:S(2)}) collective-permute-start(bf16[32,512]{1,0:T(8,128)(2,1)S(1)} %reshape.11.refs_0_), channel_id=1, source_target_pairs={{0,160},{32,192},{64,224},{96,0},{128,32},{160,64},{192,96},{224,1... | collective-permute-start | bytes 98312 | tf_op jit(solution)/shard_map/ppermute | solution.py:334
  26.8 0.0 collective-permute-done.refs_1_
  26.8 2.4 %collective-permute-start.5 = (bf16[32,512]{1,0:T(8,128)(2,1)S(1)}, bf16[32,512]{1,0:T(8,128)(2,1)S(1)}, u32[]{:S(2)}, u32[]{:S(2)}) collective-permute-start(bf16[32,512]{1,0:T(8,128)(2,1)S(1)} %reshape.11.refs_0_), channel_id=1, source_target_pairs={{0,192},{32,224},{64,0},{96,32},{128,64},{160,96},{192,128},{224,1... | collective-permute-start | bytes 98312 | tf_op jit(solution)/shard_map/ppermute | solution.py:334
  29.2 0.0 collective-permute-done.1.refs_2_
  29.2 0.7 collective-permute-start.6
  29.9 0.0 collective-permute-done.2.refs_3_
  29.9 0.0 collective-permute-done.3.refs_4_
  29.9 0.0 copy-start.7
  29.9 0.0 collective-permute-done.4.refs_5_
  29.9 0.0 copy-start.8
  30.0 2.4 %collective-permute-done.5.refs_6_ = bf16[32,512]{1,0:T(8,128)(2,1)S(1)} collective-permute-done((bf16[32,512]{1,0:T(8,128)(2,1)S(1)}, bf16[32,512]{1,0:T(8,128)(2,1)S(1)}, u32[]{:S(2)}, u32[]{:S(2)}) %collective-permute-start.5) | collective-permute-done | bytes 32800 | tf_op jit(solution)/shard_map/ppermute | solution.py:334
  32.4 0.7 collective-permute-done.6.refs_7_
  33.1 0.0 copy-done.4
  33.2 0.5 copy-done.10
  33.7 1.7 %stack.1.rows = bf16[2,256,512]{2,1,0:T(8,128)(2,1)} custom-call(s32[1]{0:T(128)} %bitcast.z, bf16[32,512]{1,0:T(8,128)(2,1)} %copy-done.2, bf16[32,512]{1,0:T(8,128)(2,1)} %copy-done.4, bf16[32,512]{1,0:T(8,128)(2,1)} %copy-done.5, bf16[32,512]{1,0:T(8,128)(2,1)} %copy-done.6, bf16[32,512]{1,0:T(8,128)(2,1)} %copy-done.7, bf16[32,512]{1,0:T(8,128)(2,1)} %copy-done.8, ...), custom_call_target="tpu_custom_call" | custom-call | bytes 786432 | tf_op jit(solution)/shard_map/stack/pallas_call | solution.py:156
  35.4 8.3 %all-to-all-done.message = bf16[32,17,16,128]{3,2,1,0:T(8,128)(2,1)} async-done(((bf16[32,17,16,128]{3,2,1,0:T(8,128)(2,1)}), bf16[32,17,16,128]{3,2,1,0:T(8,128)(2,1)}, u32[]{:S(2)}, u32[]{:S(2)}) %all-to-all-start) | async-done | bytes 2228256 | tf_op jit(solution)/shard_map/all_to_all | solution.py:330
  43.7 2.9 %merge.1 = bf16[32,4,16,512]{3,2,1,0:T(8,128)(2,1)} custom-call(bf16[32,17,16,128]{3,2,1,0:T(8,128)(2,1)} %all-to-all-done.message, bf16[2,256,512]{2,1,0:T(8,128)(2,1)} %stack.1.rows), custom_call_target="tpu_custom_call" | custom-call | flops 536870912 | bytes 3145728 | tf_op jit(solution)/shard_map/merge/pallas_call | solution.py:204
  46.7 5.3 %all-to-all-start.1 = ((bf16[32,4,16,512]{3,2,1,0:T(8,128)(2,1)}), bf16[32,4,16,512]{3,2,1,0:T(8,128)(2,1)S(1)}, u32[]{:S(2)}, u32[]{:S(2)}) async-start(bf16[32,4,16,512]{3,2,1,0:T(8,128)(2,1)} %merge.1), calls=%async_computation.1 | async-start | bytes 4194304 | tf_op jit(solution)/shard_map/all_to_all | solution.py:330
  52.0 0.0 copy-start
  52.0 0.0 copy-start.1
  52.0 4.2 %mix.1 = (f32[32,512]{1,0:T(8,128)S(1)}, bf16[32,512]{1,0:T(8,128)(2,1)S(1)}, bf16[32,512]{1,0:T(8,128)(2,1)S(1)}, bf16[32,512]{1,0:T(8,128)(2,1)S(1)}, bf16[32,...) custom-call(s32[1]{0:T(128)} %bitcast.z, ...), custom_call_target="tpu_custom_call" | custom-call | flops 1073741824 | bytes 3145728 | tf_op jit(solution)/shard_map/mix/pallas_call | solution.py:260
  56.3 7.0 %collective-permute-start.10 = (bf16[32,512]{1,0:T(8,128)(2,1)S(1)}, bf16[32,512]{1,0:T(8,128)(2,1)S(1)}, u32[]{:S(2)}, u32[]{:S(2)}) collective-permute-start(bf16[32,512]{1,0:T(8,128)(2,1)S(1)} %get-tuple-element.14), channel_id=1, source_target_pairs={{0,128},{32,160},{64,192},{96,224},{128,0},{160,32},{192,64},{224,... | collective-permute-start | bytes 98312 | tf_op jit(solution)/shard_map/ppermute | solution.py:334
  63.3 0.0 collective-permute-start.11
  63.3 4.0 %collective-permute-start.12 = (bf16[32,512]{1,0:T(8,128)(2,1)S(1)}, bf16[32,512]{1,0:T(8,128)(2,1)S(1)}, u32[]{:S(2)}, u32[]{:S(2)}) collective-permute-start(bf16[32,512]{1,0:T(8,128)(2,1)S(1)} %get-tuple-element.16), channel_id=1, source_target_pairs={{0,192},{32,224},{64,0},{96,32},{128,64},{160,96},{192,128},{224,1... | collective-permute-start | bytes 98312 | tf_op jit(solution)/shard_map/ppermute | solution.py:334
  67.3 0.7 collective-permute-start.13
  68.0 0.7 collective-permute-start.7
  68.8 0.0 collective-permute-done.10.refs_3_
  68.8 0.0 collective-permute-start.8
  68.8 0.0 collective-permute-done.11.refs_4_
  68.8 2.8 %collective-permute-start.9 = (bf16[32,512]{1,0:T(8,128)(2,1)S(1)}, bf16[32,512]{1,0:T(8,128)(2,1)S(1)}, u32[]{:S(2)}, u32[]{:S(2)}) collective-permute-start(bf16[32,512]{1,0:T(8,128)(2,1)S(1)} %get-tuple-element.13), channel_id=1, source_target_pairs={{0,96},{32,128},{64,160},{96,192},{128,224},{160,0},{192,32},{224,... | collective-permute-start | bytes 98312 | tf_op jit(solution)/shard_map/ppermute | solution.py:334
  71.6 0.0 collective-permute-done.12.refs_5_
  71.6 0.0 collective-permute-done.13.refs_6_
  71.6 0.6 collective-permute-done.7.refs_0_
  72.2 1.8 %collective-permute-done.8.refs_1_ = bf16[32,512]{1,0:T(8,128)(2,1)S(1)} collective-permute-done((bf16[32,512]{1,0:T(8,128)(2,1)S(1)}, bf16[32,512]{1,0:T(8,128)(2,1)S(1)}, u32[]{:S(2)}, u32[]{:S(2)}) %collective-permute-start.8) | collective-permute-done | bytes 32800 | tf_op jit(solution)/shard_map/ppermute | solution.py:334
  73.9 0.7 collective-permute-done.9.refs_2_
  74.6 0.7 total.1
  75.3 5.5 %all-to-all-done.1.merged = bf16[32,4,16,512]{3,2,1,0:T(8,128)(2,1)S(1)} async-done(((bf16[32,4,16,512]{3,2,1,0:T(8,128)(2,1)}), bf16[32,4,16,512]{3,2,1,0:T(8,128)(2,1)S(1)}, u32[]{:S(2)}, u32[]{:S(2)}) %all-to-all-start.1) | async-done | bytes 2097184 | tf_op jit(solution)/shard_map/all_to_all | solution.py:330
  80.8 0.0 copy-done.1
  80.8 2.9 %back.1 = bf16[4,256,512]{2,1,0:T(8,128)(2,1)} custom-call(s32[4]{0:T(128)S(1)} %copy-done.1, bf16[4,256,512]{2,1,0:T(8,128)(2,1)S(1)} %copy-done, bf16[32,4,16,512]{3,2,1,0:T(8,128)(2,1)S(1)} %all-to-all-done.1.merged), custom_call_target="tpu_custom_call" | custom-call | flops 1073741824 | bytes 4194304 | tf_op jit(solution)/shard_map/back/pallas_call | solution.py:313
  (13 shorter events, 0.0 us)
Async XLA Ops:
  5.4 7.9 %copy-start.3 = (bf16[16,2,512]{2,1,0:T(2,128)(2,1)S(1)}, bf16[16,2,512]{2,1,0:T(2,128)(2,1)}, u32[]{:S(2)}) copy-start(bf16[16,2,512]{2,1,0:T(2,128)(2,1)} %param.9) | copy-start | bytes 98308
  5.4 38.3 %all-to-all-start = ((bf16[32,17,16,128]{3,2,1,0:T(8,128)(2,1)}), bf16[32,17,16,128]{3,2,1,0:T(8,128)(2,1)}, u32[]{:S(2)}, u32[]{:S(2)}) async-start(bf16[32,17,16,128]{3,2,1,0:T(8,128)(2,1)} %outer.1), calls=%async_computation | async-start | bytes 4456448 | tf_op jit(solution)/shard_map/all_to_all | solution.py:330
  13.4 19.7 %copy-start.2 = (bf16[32,512]{1,0:T(8,128)(2,1)}, bf16[32,512]{1,0:T(8,128)(2,1)S(1)}, u32[]{:S(2)}) copy-start(bf16[32,512]{1,0:T(8,128)(2,1)S(1)} %reshape.11.refs_0_) | copy-start | bytes 98308
  13.4 13.4 %collective-permute-start = (bf16[32,512]{1,0:T(8,128)(2,1)S(1)}, bf16[32,512]{1,0:T(8,128)(2,1)S(1)}, u32[]{:S(2)}, u32[]{:S(2)}) collective-permute-start(bf16[32,512]{1,0:T(8,128)(2,1)S(1)} %reshape.11.refs_0_), channel_id=1, source_target_pairs={{0,32},{32,64},{64,96},{96,128},{128,160},{160,192},{192,224},{224... | collective-permute-start | bytes 98312 | tf_op jit(solution)/shard_map/ppermute | solution.py:334
  15.1 14.1 %collective-permute-start.1 = (bf16[32,512]{1,0:T(8,128)(2,1)S(1)}, bf16[32,512]{1,0:T(8,128)(2,1)S(1)}, u32[]{:S(2)}, u32[]{:S(2)}) collective-permute-start(bf16[32,512]{1,0:T(8,128)(2,1)S(1)} %reshape.11.refs_0_), channel_id=1, source_target_pairs={{0,64},{32,96},{64,128},{96,160},{128,192},{160,224},{192,0},{224,... | collective-permute-start | bytes 98312 | tf_op jit(solution)/shard_map/ppermute | solution.py:334
  18.1 11.8 %collective-permute-start.2 = (bf16[32,512]{1,0:T(8,128)(2,1)S(1)}, bf16[32,512]{1,0:T(8,128)(2,1)S(1)}, u32[]{:S(2)}, u32[]{:S(2)}) collective-permute-start(bf16[32,512]{1,0:T(8,128)(2,1)S(1)} %reshape.11.refs_0_), channel_id=1, source_target_pairs={{0,96},{32,128},{64,160},{96,192},{128,224},{160,0},{192,32},{224,... | collective-permute-start | bytes 98312 | tf_op jit(solution)/shard_map/ppermute | solution.py:334
  21.8 8.1 %collective-permute-start.3 = (bf16[32,512]{1,0:T(8,128)(2,1)S(1)}, bf16[32,512]{1,0:T(8,128)(2,1)S(1)}, u32[]{:S(2)}, u32[]{:S(2)}) collective-permute-start(bf16[32,512]{1,0:T(8,128)(2,1)S(1)} %reshape.11.refs_0_), channel_id=1, source_target_pairs={{0,128},{32,160},{64,192},{96,224},{128,0},{160,32},{192,64},{224,... | collective-permute-start | bytes 98312 | tf_op jit(solution)/shard_map/ppermute | solution.py:334
  22.3 7.6 %collective-permute-start.4 = (bf16[32,512]{1,0:T(8,128)(2,1)S(1)}, bf16[32,512]{1,0:T(8,128)(2,1)S(1)}, u32[]{:S(2)}, u32[]{:S(2)}) collective-permute-start(bf16[32,512]{1,0:T(8,128)(2,1)S(1)} %reshape.11.refs_0_), channel_id=1, source_target_pairs={{0,160},{32,192},{64,224},{96,0},{128,32},{160,64},{192,96},{224,1... | collective-permute-start | bytes 98312 | tf_op jit(solution)/shard_map/ppermute | solution.py:334
  26.8 6.3 %copy-start.4 = (bf16[32,512]{1,0:T(8,128)(2,1)}, bf16[32,512]{1,0:T(8,128)(2,1)S(1)}, u32[]{:S(2)}) copy-start(bf16[32,512]{1,0:T(8,128)(2,1)S(1)} %collective-permute-done.refs_1_) | copy-start | bytes 98308
  26.8 5.6 %collective-permute-start.5 = (bf16[32,512]{1,0:T(8,128)(2,1)S(1)}, bf16[32,512]{1,0:T(8,128)(2,1)S(1)}, u32[]{:S(2)}, u32[]{:S(2)}) collective-permute-start(bf16[32,512]{1,0:T(8,128)(2,1)S(1)} %reshape.11.refs_0_), channel_id=1, source_target_pairs={{0,192},{32,224},{64,0},{96,32},{128,64},{160,96},{192,128},{224,1... | collective-permute-start | bytes 98312 | tf_op jit(solution)/shard_map/ppermute | solution.py:334
  29.2 3.9 %copy-start.5 = (bf16[32,512]{1,0:T(8,128)(2,1)}, bf16[32,512]{1,0:T(8,128)(2,1)S(1)}, u32[]{:S(2)}) copy-start(bf16[32,512]{1,0:T(8,128)(2,1)S(1)} %collective-permute-done.1.refs_2_) | copy-start | bytes 98308
  29.2 3.9 %collective-permute-start.6 = (bf16[32,512]{1,0:T(8,128)(2,1)S(1)}, bf16[32,512]{1,0:T(8,128)(2,1)S(1)}, u32[]{:S(2)}, u32[]{:S(2)}) collective-permute-start(bf16[32,512]{1,0:T(8,128)(2,1)S(1)} %reshape.11.refs_0_), channel_id=1, source_target_pairs={{0,224},{32,0},{64,32},{96,64},{128,96},{160,128},{192,160},{224,1... | collective-permute-start | bytes 98312 | tf_op jit(solution)/shard_map/ppermute | solution.py:334
  29.9 3.2 %copy-start.6 = (bf16[32,512]{1,0:T(8,128)(2,1)}, bf16[32,512]{1,0:T(8,128)(2,1)S(1)}, u32[]{:S(2)}) copy-start(bf16[32,512]{1,0:T(8,128)(2,1)S(1)} %collective-permute-done.2.refs_3_) | copy-start | bytes 98308
  29.9 3.2 %copy-start.7 = (bf16[32,512]{1,0:T(8,128)(2,1)}, bf16[32,512]{1,0:T(8,128)(2,1)S(1)}, u32[]{:S(2)}) copy-start(bf16[32,512]{1,0:T(8,128)(2,1)S(1)} %collective-permute-done.3.refs_4_) | copy-start | bytes 98308
  29.9 3.2 %copy-start.8 = (bf16[32,512]{1,0:T(8,128)(2,1)}, bf16[32,512]{1,0:T(8,128)(2,1)S(1)}, u32[]{:S(2)}) copy-start(bf16[32,512]{1,0:T(8,128)(2,1)S(1)} %collective-permute-done.4.refs_5_) | copy-start | bytes 98308
  32.4 0.7 copy-start.9
  33.1 0.6 copy-start.10
  46.7 34.2 %all-to-all-start.1 = ((bf16[32,4,16,512]{3,2,1,0:T(8,128)(2,1)}), bf16[32,4,16,512]{3,2,1,0:T(8,128)(2,1)S(1)}, u32[]{:S(2)}, u32[]{:S(2)}) async-start(bf16[32,4,16,512]{3,2,1,0:T(8,128)(2,1)} %merge.1), calls=%async_computation.1 | async-start | bytes 4194304 | tf_op jit(solution)/shard_map/all_to_all | solution.py:330
  52.0 28.8 %copy-start = (bf16[4,256,512]{2,1,0:T(8,128)(2,1)S(1)}, bf16[4,256,512]{2,1,0:T(8,128)(2,1)}, u32[]{:S(2)}) copy-start(bf16[4,256,512]{2,1,0:T(8,128)(2,1)} %grad.3) | copy-start | bytes 3145732
  52.0 28.8 %copy-start.1 = (s32[4]{0:T(128)S(1)}, s32[4]{0:T(128)}, u32[]{:S(2)}) copy-start(s32[4]{0:T(128)} %counts.3) | copy-start | bytes 52
  56.3 12.5 %collective-permute-start.10 = (bf16[32,512]{1,0:T(8,128)(2,1)S(1)}, bf16[32,512]{1,0:T(8,128)(2,1)S(1)}, u32[]{:S(2)}, u32[]{:S(2)}) collective-permute-start(bf16[32,512]{1,0:T(8,128)(2,1)S(1)} %get-tuple-element.14), channel_id=1, source_target_pairs={{0,128},{32,160},{64,192},{96,224},{128,0},{160,32},{192,64},{224,... | collective-permute-start | bytes 98312 | tf_op jit(solution)/shard_map/ppermute | solution.py:334
  63.3 5.5 %collective-permute-start.11 = (bf16[32,512]{1,0:T(8,128)(2,1)S(1)}, bf16[32,512]{1,0:T(8,128)(2,1)S(1)}, u32[]{:S(2)}, u32[]{:S(2)}) collective-permute-start(bf16[32,512]{1,0:T(8,128)(2,1)S(1)} %get-tuple-element.15), channel_id=1, source_target_pairs={{0,160},{32,192},{64,224},{96,0},{128,32},{160,64},{192,96},{224,1... | collective-permute-start | bytes 98312 | tf_op jit(solution)/shard_map/ppermute | solution.py:334
  63.3 8.3 %collective-permute-start.12 = (bf16[32,512]{1,0:T(8,128)(2,1)S(1)}, bf16[32,512]{1,0:T(8,128)(2,1)S(1)}, u32[]{:S(2)}, u32[]{:S(2)}) collective-permute-start(bf16[32,512]{1,0:T(8,128)(2,1)S(1)} %get-tuple-element.16), channel_id=1, source_target_pairs={{0,192},{32,224},{64,0},{96,32},{128,64},{160,96},{192,128},{224,1... | collective-permute-start | bytes 98312 | tf_op jit(solution)/shard_map/ppermute | solution.py:334
  67.3 4.3 %collective-permute-start.13 = (bf16[32,512]{1,0:T(8,128)(2,1)S(1)}, bf16[32,512]{1,0:T(8,128)(2,1)S(1)}, u32[]{:S(2)}, u32[]{:S(2)}) collective-permute-start(bf16[32,512]{1,0:T(8,128)(2,1)S(1)} %get-tuple-element.17), channel_id=1, source_target_pairs={{0,224},{32,0},{64,32},{96,64},{128,96},{160,128},{192,160},{224,1... | collective-permute-start | bytes 98312 | tf_op jit(solution)/shard_map/ppermute | solution.py:334
  68.0 4.2 %collective-permute-start.7 = (bf16[32,512]{1,0:T(8,128)(2,1)S(1)}, bf16[32,512]{1,0:T(8,128)(2,1)S(1)}, u32[]{:S(2)}, u32[]{:S(2)}) collective-permute-start(bf16[32,512]{1,0:T(8,128)(2,1)S(1)} %get-tuple-element.11), channel_id=1, source_target_pairs={{0,32},{32,64},{64,96},{96,128},{128,160},{160,192},{192,224},{224... | collective-permute-start | bytes 98312 | tf_op jit(solution)/shard_map/ppermute | solution.py:334
  68.8 5.2 %collective-permute-start.8 = (bf16[32,512]{1,0:T(8,128)(2,1)S(1)}, bf16[32,512]{1,0:T(8,128)(2,1)S(1)}, u32[]{:S(2)}, u32[]{:S(2)}) collective-permute-start(bf16[32,512]{1,0:T(8,128)(2,1)S(1)} %get-tuple-element.12), channel_id=1, source_target_pairs={{0,64},{32,96},{64,128},{96,160},{128,192},{160,224},{192,0},{224,... | collective-permute-start | bytes 98312 | tf_op jit(solution)/shard_map/ppermute | solution.py:334
  68.8 5.9 %collective-permute-start.9 = (bf16[32,512]{1,0:T(8,128)(2,1)S(1)}, bf16[32,512]{1,0:T(8,128)(2,1)S(1)}, u32[]{:S(2)}, u32[]{:S(2)}) collective-permute-start(bf16[32,512]{1,0:T(8,128)(2,1)S(1)} %get-tuple-element.13), channel_id=1, source_target_pairs={{0,96},{32,128},{64,160},{96,192},{128,224},{160,0},{192,32},{224,... | collective-permute-start | bytes 98312 | tf_op jit(solution)/shard_map/ppermute | solution.py:334

commit v8 on v7

--- a/solution.py
+++ b/solution.py
@@ -141,27 +141,29 @@
 
 HALF = 8
 LINES = HALF // ROWS
-
-
-def stack_kernel(z, *refs):
-    *blocks, out = refs
-    for n, block in enumerate(blocks):
-        line = (z[0] - n + NZ) & (NZ - 1)
+BACK = (0, 4, 2, 6, 1, 5, 3, 7)
+
+
+def stack_kernel(z, near, far, out):
+    for n in range(NZ):
+        source = near if n < NZ // 2 else far
+        block = source[(n % (NZ // 2)) * PART : (n % (NZ // 2) + 1) * PART]
+        line = (z[0] - BACK[n] + NZ) & (NZ - 1)
         half, place = line // LINES, (line & (LINES - 1)) * PART
         for part in range(2):
-            out[half, pl.ds(pl.multiple_of(part * LINES * PART + place, PART), PART)] = block[...]
-
-
-def stack(z, blocks):
+            out[half, pl.ds(pl.multiple_of(part * LINES * PART + place, PART), PART)] = block
+
+
+def stack(z, near, far):
     return pl.pallas_call(
         stack_kernel,
-        in_specs=[SCALARS] + [WHOLE] * NZ,
+        in_specs=[SCALARS, WHOLE, WHOLE],
         out_specs=WHOLE,
         out_shape=jax.ShapeDtypeStruct((2, WIDTH, D), BF16),
         compiler_params=vmem(STACK_MIB),
         cost_estimate=pl.CostEstimate(flops=0, bytes_accessed=6 * WIDTH * D, transcendentals=0),
         name="stack",
-    )(z, *blocks)
+    )(z, near, far)
 
 
 GROUPS = NG // GROUP
@@ -295,16 +297,20 @@
     )(own, *sums)
 
 
-def back_kernel(counts, grad, merged, out, pick, held, outs):
+def back_kernel(counts, grad, merged, out, pick, near, held, outs):
     def send(k):
         return pltpu.make_async_copy(held.at[k], out.at[k], outs.at[k])
 
-    pick[...] = order()
     for k in range(K):
         masked = masked_of(grad[k], counts[k])
-        moved = matmul(masked, merged[:, k].reshape(D, D), ((1,), (1,))).astype(BF16)
-        held[k] = matmul(moved, pick[...], ((1,), (0,))).astype(BF16)
-        send(k).start()
+        near[k] = matmul(masked, merged[:, k].reshape(D, D), ((1,), (1,))).astype(BF16)
+        if k == 0:
+            pick[...] = order()
+        if k % 2 == 1:
+            done = matmul(near[k - 1 : k + 1].reshape(2 * M, D), pick[...], ((1,), (0,))).astype(BF16)
+            held[k - 1 : k + 1] = done.reshape(2, M, D)
+            send(k - 1).start()
+            send(k).start()
     for k in range(K):
         send(k).wait()
 
@@ -316,6 +322,7 @@
         out_specs=ANY,
         scratch_shapes=[
             pltpu.VMEM((D, D), BF16),
+            pltpu.VMEM((K, M, D), BF16),
             pltpu.VMEM((K, M, D), BF16),
             pltpu.SemaphoreType.DMA((K,)),
         ],
@@ -338,7 +345,9 @@
     z = lax.axis_index("z").astype(jnp.int32).reshape(1)
     message = swap(outer(atom_counts, coeff_fixed, inputs, out_grad), PLANE)
     own = experts.reshape(PART, D)
-    rows = stack(z, [own] + [along_z(own, n) for n in range(1, NZ)])
+    near = jnp.concatenate([own, along_z(own, 4)])
+    near = jnp.concatenate([near, along_z(near, 2)])
+    rows = stack(z, near, along_z(near, 1))
     merged = swap(merge(message, rows), PLANE)
     mixed = mix(z, message)
     sums = [along_z(mixed[n], n) for n in range(1, NZ)]

time: 85.3 us -> 84.8 us (level)
  starting transfers between devices: 45.1 us -> 39.3 us
  waiting for transfers between devices: 20.1 us -> 25.7 us
    ppermute x14 -> x10, waiting for transfers between devices: 6.22 us -> 13.9 us  [along_z(): return lax.ppermute(array, 'z', [(i, (i + by) % NZ) for i in range(NZ)])]
    ppermute x14 -> x10, starting transfers between devices: 31.8 us -> 26.1 us  [along_z(): return lax.ppermute(array, 'z', [(i, (i + by) % NZ) for i in range(NZ)])]
    all_to_all x2, waiting for transfers between devices: 13.9 us -> 11.8 us  [swap(): return lax.all_to_all(array, axes, 0, 0, tiled=True)]
  transfers between devices with their start and end apart: 16 -> 12, of which waited for: 7 -> 7; matrix products, arithmetic and copies ran while one was open for 0% -> 0% of each run, Pallas kernels for 8% -> 8%
where the time goes in v8:
time: 84.8 us; the launch traced here: 83.5 us
  starting transfers between devices  39.3 us (46%)
  waiting for transfers between devices  25.7 us (30%)
  Pallas kernels  17.1 us (20%)
    ppermute x10, starting transfers between devices, along_z(): return lax.ppermute(array, 'z', [(i, (i + by) % NZ) for i in range(NZ)])  26.1 us
    ppermute x10, waiting for transfers between devices, along_z(): return lax.ppermute(array, 'z', [(i, (i + by) % NZ) for i in range(NZ)])  13.9 us
    all_to_all x2, starting transfers between devices, swap(): return lax.all_to_all(array, axes, 0, 0, tiled=True)  13.2 us
    all_to_all x2, waiting for transfers between devices, swap(): return lax.all_to_all(array, axes, 0, 0, tiled=True)  11.8 us
    pallas_call x1, Pallas kernels, outer(): pl.pallas_call(outer_kernel, in_specs=[SCALARS, WHOLE, ANY, ANY], out_spe...  4.75 us
    pallas_call x1, Pallas kernels, mix(): pl.pallas_call(mix_kernel, in_specs=[SCALARS, ANY], out_specs=[WHOLE] + [...  4.2 us
    pallas_call x1, Pallas kernels, merge(): pl.pallas_call(merge_kernel, in_specs=[ANY, ANY], out_specs=ANY, scratch_...  2.87 us
    pallas_call x1, Pallas kernels, back(): pl.pallas_call(back_kernel, in_specs=[SCALARS, WHOLE, WHOLE], out_specs=A...  2.78 us
  transfers between devices with their start and end apart: 12, of which 7 were waited for; matrix products, arithmetic and copies ran while one was open for 0% of the time, Pallas kernels for 8%

profile of v8, /device:TPU:9, one launch (start us, length us, event | category | flops | bytes accessed | tf_op | source)
XLA Modules:
  0.0 83.5 jit_solution(4844512954696867154)
XLA Ops:
  0.6 4.7 %outer.1 = bf16[32,17,16,128]{3,2,1,0:T(8,128)(2,1)} custom-call(s32[4]{0:T(128)} %counts.3, s32[4,16]{1,0:T(4,128)} %fixed.1, bf16[4,256,512]{2,1,0:T(8,128)(2,1)} %x.1, bf16[4,256,512]{2,1,0:T(8,128)(2,1)} %grad.3), custom_call_target="tpu_custom_call" | custom-call | flops 1073741824 | bytes 4194304 | tf_op jit(solution)/shard_map/outer/pallas_call | solution.py:109
  5.4 0.0 copy-start.4
  5.4 7.9 %all-to-all-start = ((bf16[32,17,16,128]{3,2,1,0:T(8,128)(2,1)}), bf16[32,17,16,128]{3,2,1,0:T(8,128)(2,1)}, u32[]{:S(2)}, u32[]{:S(2)}) async-start(bf16[32,17,16,128]{3,2,1,0:T(8,128)(2,1)} %outer.1), calls=%async_computation | async-start | bytes 4456448 | tf_op jit(solution)/shard_map/all_to_all | solution.py:337
  13.3 0.0 copy-done.4
  13.3 7.0 %collective-permute-start = (bf16[32,512]{1,0:T(8,128)(2,1)S(1)}, bf16[32,512]{1,0:T(8,128)(2,1)S(1)}, u32[]{:S(2)}, u32[]{:S(2)}) collective-permute-start(bf16[32,512]{1,0:T(8,128)(2,1)S(1)} %reshape.11), channel_id=1, source_target_pairs={{0,128},{32,160},{64,192},{96,224},{128,0},{160,32},{192,64},{224,... | collective-permute-start | bytes 98312 | tf_op jit(solution)/shard_map/ppermute | solution.py:341
  20.3 1.7 %collective-permute-done = bf16[32,512]{1,0:T(8,128)(2,1)S(1)} collective-permute-done((bf16[32,512]{1,0:T(8,128)(2,1)S(1)}, bf16[32,512]{1,0:T(8,128)(2,1)S(1)}, u32[]{:S(2)}, u32[]{:S(2)}) %collective-permute-start) | collective-permute-done | bytes 32800 | tf_op jit(solution)/shard_map/ppermute | solution.py:341
  22.0 1.0 %collective-permute-start.1 = (bf16[64,512]{1,0:T(8,128)(2,1)S(1)}, bf16[64,512]{1,0:T(8,128)(2,1)S(1)}, u32[]{:S(2)}, u32[]{:S(2)}) collective-permute-start(bf16[64,512]{1,0:T(8,128)(2,1)S(1)} %pad_maximum_fusion), channel_id=1, source_target_pairs={{0,64},{32,96},{64,128},{96,160},{128,192},{160,224},{192,0},{224,... | collective-permute-start | bytes 196616 | tf_op jit(solution)/shard_map/ppermute | solution.py:341
  23.1 4.8 %collective-permute-done.1 = bf16[64,512]{1,0:T(8,128)(2,1)S(1)} collective-permute-done((bf16[64,512]{1,0:T(8,128)(2,1)S(1)}, bf16[64,512]{1,0:T(8,128)(2,1)S(1)}, u32[]{:S(2)}, u32[]{:S(2)}) %collective-permute-start.1) | collective-permute-done | bytes 65568 | tf_op jit(solution)/shard_map/ppermute | solution.py:341
  27.9 0.0 copy-start.2
  27.9 1.5 %collective-permute-start.2 = (bf16[128,512]{1,0:T(8,128)(2,1)S(1)}, bf16[128,512]{1,0:T(8,128)(2,1)S(1)}, u32[]{:S(2)}, u32[]{:S(2)}) collective-permute-start(bf16[128,512]{1,0:T(8,128)(2,1)S(1)} %constant_dynamic-update-slice_fusion.near), channel_id=1, source_target_pairs={{0,32},{32,64},{64,96},{96,128},{128,160},{160,192},{192,224},{224... | collective-permute-start | bytes 393224 | tf_op jit(solution)/shard_map/ppermute | solution.py:341
  29.4 4.3 %collective-permute-done.2.far = bf16[128,512]{1,0:T(8,128)(2,1)S(1)} collective-permute-done((bf16[128,512]{1,0:T(8,128)(2,1)S(1)}, bf16[128,512]{1,0:T(8,128)(2,1)S(1)}, u32[]{:S(2)}, u32[]{:S(2)}) %collective-permute-start.2) | collective-permute-done | bytes 131104 | tf_op jit(solution)/shard_map/ppermute | solution.py:341
  33.7 0.0 copy-start.3
  33.7 0.0 copy-done.2
  33.7 0.6 copy-done.3
  34.4 1.8 %stack.1.rows = bf16[2,256,512]{2,1,0:T(8,128)(2,1)} custom-call(s32[1]{0:T(128)} %bitcast.z, bf16[128,512]{1,0:T(8,128)(2,1)} %copy-done.2, bf16[128,512]{1,0:T(8,128)(2,1)} %copy-done.3), custom_call_target="tpu_custom_call" | custom-call | bytes 786432 | tf_op jit(solution)/shard_map/stack/pallas_call | solution.py:158
  36.2 7.5 %all-to-all-done.message = bf16[32,17,16,128]{3,2,1,0:T(8,128)(2,1)} async-done(((bf16[32,17,16,128]{3,2,1,0:T(8,128)(2,1)}), bf16[32,17,16,128]{3,2,1,0:T(8,128)(2,1)}, u32[]{:S(2)}, u32[]{:S(2)}) %all-to-all-start) | async-done | bytes 2228256 | tf_op jit(solution)/shard_map/all_to_all | solution.py:337
  43.7 2.9 %merge.1 = bf16[32,4,16,512]{3,2,1,0:T(8,128)(2,1)} custom-call(bf16[32,17,16,128]{3,2,1,0:T(8,128)(2,1)} %all-to-all-done.message, bf16[2,256,512]{2,1,0:T(8,128)(2,1)} %stack.1.rows), custom_call_target="tpu_custom_call" | custom-call | flops 536870912 | bytes 3145728 | tf_op jit(solution)/shard_map/merge/pallas_call | solution.py:206
  46.6 5.3 %all-to-all-start.1 = ((bf16[32,4,16,512]{3,2,1,0:T(8,128)(2,1)}), bf16[32,4,16,512]{3,2,1,0:T(8,128)(2,1)S(1)}, u32[]{:S(2)}, u32[]{:S(2)}) async-start(bf16[32,4,16,512]{3,2,1,0:T(8,128)(2,1)} %merge.1), calls=%async_computation.1 | async-start | bytes 4194304 | tf_op jit(solution)/shard_map/all_to_all | solution.py:337
  51.9 0.0 copy-start
  51.9 0.0 copy-start.1
  52.0 4.2 %mix.1 = (f32[32,512]{1,0:T(8,128)S(1)}, bf16[32,512]{1,0:T(8,128)(2,1)S(1)}, bf16[32,512]{1,0:T(8,128)(2,1)S(1)}, bf16[32,512]{1,0:T(8,128)(2,1)S(1)}, bf16[32,...) custom-call(s32[1]{0:T(128)} %bitcast.z, ...), custom_call_target="tpu_custom_call" | custom-call | flops 1073741824 | bytes 3145728 | tf_op jit(solution)/shard_map/mix/pallas_call | solution.py:262
  56.2 1.7 %collective-permute-start.3 = (bf16[32,512]{1,0:T(8,128)(2,1)S(1)}, bf16[32,512]{1,0:T(8,128)(2,1)S(1)}, u32[]{:S(2)}, u32[]{:S(2)}) collective-permute-start(bf16[32,512]{1,0:T(8,128)(2,1)S(1)} %get-tuple-element.11), channel_id=1, source_target_pairs={{0,32},{32,64},{64,96},{96,128},{128,160},{160,192},{192,224},{224... | collective-permute-start | bytes 98312 | tf_op jit(solution)/shard_map/ppermute | solution.py:341
  57.9 3.0 %collective-permute-start.4 = (bf16[32,512]{1,0:T(8,128)(2,1)S(1)}, bf16[32,512]{1,0:T(8,128)(2,1)S(1)}, u32[]{:S(2)}, u32[]{:S(2)}) collective-permute-start(bf16[32,512]{1,0:T(8,128)(2,1)S(1)} %get-tuple-element.12), channel_id=1, source_target_pairs={{0,64},{32,96},{64,128},{96,160},{128,192},{160,224},{192,0},{224,... | collective-permute-start | bytes 98312 | tf_op jit(solution)/shard_map/ppermute | solution.py:341
  60.9 3.8 %collective-permute-start.5 = (bf16[32,512]{1,0:T(8,128)(2,1)S(1)}, bf16[32,512]{1,0:T(8,128)(2,1)S(1)}, u32[]{:S(2)}, u32[]{:S(2)}) collective-permute-start(bf16[32,512]{1,0:T(8,128)(2,1)S(1)} %get-tuple-element.13), channel_id=1, source_target_pairs={{0,96},{32,128},{64,160},{96,192},{128,224},{160,0},{192,32},{224,... | collective-permute-start | bytes 98312 | tf_op jit(solution)/shard_map/ppermute | solution.py:341
  64.6 0.4 collective-permute-start.6
  65.1 4.5 %collective-permute-start.7 = (bf16[32,512]{1,0:T(8,128)(2,1)S(1)}, bf16[32,512]{1,0:T(8,128)(2,1)S(1)}, u32[]{:S(2)}, u32[]{:S(2)}) collective-permute-start(bf16[32,512]{1,0:T(8,128)(2,1)S(1)} %get-tuple-element.15), channel_id=1, source_target_pairs={{0,160},{32,192},{64,224},{96,0},{128,32},{160,64},{192,96},{224,1... | collective-permute-start | bytes 98312 | tf_op jit(solution)/shard_map/ppermute | solution.py:341
  69.6 0.0 collective-permute-done.3.refs_0_
  69.6 2.4 %collective-permute-start.8 = (bf16[32,512]{1,0:T(8,128)(2,1)S(1)}, bf16[32,512]{1,0:T(8,128)(2,1)S(1)}, u32[]{:S(2)}, u32[]{:S(2)}) collective-permute-start(bf16[32,512]{1,0:T(8,128)(2,1)S(1)} %get-tuple-element.16), channel_id=1, source_target_pairs={{0,192},{32,224},{64,0},{96,32},{128,64},{160,96},{192,128},{224,1... | collective-permute-start | bytes 98312 | tf_op jit(solution)/shard_map/ppermute | solution.py:341
  71.9 0.0 collective-permute-done.4.refs_1_
  71.9 0.7 collective-permute-start.9
  72.7 0.0 collective-permute-done.5.refs_2_
  72.7 0.0 collective-permute-done.6.refs_3_
  72.7 0.0 collective-permute-done.7.refs_4_
  72.7 2.4 %collective-permute-done.8.refs_5_ = bf16[32,512]{1,0:T(8,128)(2,1)S(1)} collective-permute-done((bf16[32,512]{1,0:T(8,128)(2,1)S(1)}, bf16[32,512]{1,0:T(8,128)(2,1)S(1)}, u32[]{:S(2)}, u32[]{:S(2)}) %collective-permute-start.8) | collective-permute-done | bytes 32800 | tf_op jit(solution)/shard_map/ppermute | solution.py:341
  75.1 0.7 collective-permute-done.9.refs_6_
  75.8 0.7 total.1
  76.5 4.3 %all-to-all-done.1.merged = bf16[32,4,16,512]{3,2,1,0:T(8,128)(2,1)S(1)} async-done(((bf16[32,4,16,512]{3,2,1,0:T(8,128)(2,1)}), bf16[32,4,16,512]{3,2,1,0:T(8,128)(2,1)S(1)}, u32[]{:S(2)}, u32[]{:S(2)}) %all-to-all-start.1) | async-done | bytes 2097184 | tf_op jit(solution)/shard_map/all_to_all | solution.py:337
  80.8 0.0 copy-done
  80.8 0.0 copy-done.1
  80.8 2.8 %back.1 = bf16[4,256,512]{2,1,0:T(8,128)(2,1)} custom-call(s32[4]{0:T(128)S(1)} %copy-done.1, bf16[4,256,512]{2,1,0:T(8,128)(2,1)S(1)} %copy-done, bf16[32,4,16,512]{3,2,1,0:T(8,128)(2,1)S(1)} %all-to-all-done.1.merged), custom_call_target="tpu_custom_call" | custom-call | flops 1073741824 | bytes 4194304 | tf_op jit(solution)/shard_map/back/pallas_call | solution.py:319
  (5 shorter events, 0.0 us)
Async XLA Ops:
  5.4 7.9 %copy-start.4 = (bf16[16,2,512]{2,1,0:T(2,128)(2,1)S(1)}, bf16[16,2,512]{2,1,0:T(2,128)(2,1)}, u32[]{:S(2)}) copy-start(bf16[16,2,512]{2,1,0:T(2,128)(2,1)} %param.9) | copy-start | bytes 98308
  5.4 38.3 %all-to-all-start = ((bf16[32,17,16,128]{3,2,1,0:T(8,128)(2,1)}), bf16[32,17,16,128]{3,2,1,0:T(8,128)(2,1)}, u32[]{:S(2)}, u32[]{:S(2)}) async-start(bf16[32,17,16,128]{3,2,1,0:T(8,128)(2,1)} %outer.1), calls=%async_computation | async-start | bytes 4456448 | tf_op jit(solution)/shard_map/all_to_all | solution.py:337
  13.3 8.7 %collective-permute-start = (bf16[32,512]{1,0:T(8,128)(2,1)S(1)}, bf16[32,512]{1,0:T(8,128)(2,1)S(1)}, u32[]{:S(2)}, u32[]{:S(2)}) collective-permute-start(bf16[32,512]{1,0:T(8,128)(2,1)S(1)} %reshape.11), channel_id=1, source_target_pairs={{0,128},{32,160},{64,192},{96,224},{128,0},{160,32},{192,64},{224,... | collective-permute-start | bytes 98312 | tf_op jit(solution)/shard_map/ppermute | solution.py:341
  22.0 5.8 %collective-permute-start.1 = (bf16[64,512]{1,0:T(8,128)(2,1)S(1)}, bf16[64,512]{1,0:T(8,128)(2,1)S(1)}, u32[]{:S(2)}, u32[]{:S(2)}) collective-permute-start(bf16[64,512]{1,0:T(8,128)(2,1)S(1)} %pad_maximum_fusion), channel_id=1, source_target_pairs={{0,64},{32,96},{64,128},{96,160},{128,192},{160,224},{192,0},{224,... | collective-permute-start | bytes 196616 | tf_op jit(solution)/shard_map/ppermute | solution.py:341
  27.9 5.8 %copy-start.2 = (bf16[128,512]{1,0:T(8,128)(2,1)}, bf16[128,512]{1,0:T(8,128)(2,1)S(1)}, u32[]{:S(2)}) copy-start(bf16[128,512]{1,0:T(8,128)(2,1)S(1)} %constant_dynamic-update-slice_fusion.near) | copy-start | bytes 393220
  27.9 5.8 %collective-permute-start.2 = (bf16[128,512]{1,0:T(8,128)(2,1)S(1)}, bf16[128,512]{1,0:T(8,128)(2,1)S(1)}, u32[]{:S(2)}, u32[]{:S(2)}) collective-permute-start(bf16[128,512]{1,0:T(8,128)(2,1)S(1)} %constant_dynamic-update-slice_fusion.near), channel_id=1, source_target_pairs={{0,32},{32,64},{64,96},{96,128},{128,160},{160,192},{192,224},{224... | collective-permute-start | bytes 393224 | tf_op jit(solution)/shard_map/ppermute | solution.py:341
  33.7 0.7 copy-start.3
  46.6 34.2 %all-to-all-start.1 = ((bf16[32,4,16,512]{3,2,1,0:T(8,128)(2,1)}), bf16[32,4,16,512]{3,2,1,0:T(8,128)(2,1)S(1)}, u32[]{:S(2)}, u32[]{:S(2)}) async-start(bf16[32,4,16,512]{3,2,1,0:T(8,128)(2,1)} %merge.1), calls=%async_computation.1 | async-start | bytes 4194304 | tf_op jit(solution)/shard_map/all_to_all | solution.py:337
  51.9 28.8 %copy-start = (bf16[4,256,512]{2,1,0:T(8,128)(2,1)S(1)}, bf16[4,256,512]{2,1,0:T(8,128)(2,1)}, u32[]{:S(2)}) copy-start(bf16[4,256,512]{2,1,0:T(8,128)(2,1)} %grad.3) | copy-start | bytes 3145732
  51.9 28.8 %copy-start.1 = (s32[4]{0:T(128)S(1)}, s32[4]{0:T(128)}, u32[]{:S(2)}) copy-start(s32[4]{0:T(128)} %counts.3) | copy-start | bytes 52
  56.2 13.4 %collective-permute-start.3 = (bf16[32,512]{1,0:T(8,128)(2,1)S(1)}, bf16[32,512]{1,0:T(8,128)(2,1)S(1)}, u32[]{:S(2)}, u32[]{:S(2)}) collective-permute-start(bf16[32,512]{1,0:T(8,128)(2,1)S(1)} %get-tuple-element.11), channel_id=1, source_target_pairs={{0,32},{32,64},{64,96},{96,128},{128,160},{160,192},{192,224},{224... | collective-permute-start | bytes 98312 | tf_op jit(solution)/shard_map/ppermute | solution.py:341
  57.9 14.1 %collective-permute-start.4 = (bf16[32,512]{1,0:T(8,128)(2,1)S(1)}, bf16[32,512]{1,0:T(8,128)(2,1)S(1)}, u32[]{:S(2)}, u32[]{:S(2)}) collective-permute-start(bf16[32,512]{1,0:T(8,128)(2,1)S(1)} %get-tuple-element.12), channel_id=1, source_target_pairs={{0,64},{32,96},{64,128},{96,160},{128,192},{160,224},{192,0},{224,... | collective-permute-start | bytes 98312 | tf_op jit(solution)/shard_map/ppermute | solution.py:341
  60.9 11.8 %collective-permute-start.5 = (bf16[32,512]{1,0:T(8,128)(2,1)S(1)}, bf16[32,512]{1,0:T(8,128)(2,1)S(1)}, u32[]{:S(2)}, u32[]{:S(2)}) collective-permute-start(bf16[32,512]{1,0:T(8,128)(2,1)S(1)} %get-tuple-element.13), channel_id=1, source_target_pairs={{0,96},{32,128},{64,160},{96,192},{128,224},{160,0},{192,32},{224,... | collective-permute-start | bytes 98312 | tf_op jit(solution)/shard_map/ppermute | solution.py:341
  64.6 8.0 %collective-permute-start.6 = (bf16[32,512]{1,0:T(8,128)(2,1)S(1)}, bf16[32,512]{1,0:T(8,128)(2,1)S(1)}, u32[]{:S(2)}, u32[]{:S(2)}) collective-permute-start(bf16[32,512]{1,0:T(8,128)(2,1)S(1)} %get-tuple-element.14), channel_id=1, source_target_pairs={{0,128},{32,160},{64,192},{96,224},{128,0},{160,32},{192,64},{224,... | collective-permute-start | bytes 98312 | tf_op jit(solution)/shard_map/ppermute | solution.py:341
  65.1 7.6 %collective-permute-start.7 = (bf16[32,512]{1,0:T(8,128)(2,1)S(1)}, bf16[32,512]{1,0:T(8,128)(2,1)S(1)}, u32[]{:S(2)}, u32[]{:S(2)}) collective-permute-start(bf16[32,512]{1,0:T(8,128)(2,1)S(1)} %get-tuple-element.15), channel_id=1, source_target_pairs={{0,160},{32,192},{64,224},{96,0},{128,32},{160,64},{192,96},{224,1... | collective-permute-start | bytes 98312 | tf_op jit(solution)/shard_map/ppermute | solution.py:341
  69.6 5.5 %collective-permute-start.8 = (bf16[32,512]{1,0:T(8,128)(2,1)S(1)}, bf16[32,512]{1,0:T(8,128)(2,1)S(1)}, u32[]{:S(2)}, u32[]{:S(2)}) collective-permute-start(bf16[32,512]{1,0:T(8,128)(2,1)S(1)} %get-tuple-element.16), channel_id=1, source_target_pairs={{0,192},{32,224},{64,0},{96,32},{128,64},{160,96},{192,128},{224,1... | collective-permute-start | bytes 98312 | tf_op jit(solution)/shard_map/ppermute | solution.py:341
  71.9 3.8 %collective-permute-start.9 = (bf16[32,512]{1,0:T(8,128)(2,1)S(1)}, bf16[32,512]{1,0:T(8,128)(2,1)S(1)}, u32[]{:S(2)}, u32[]{:S(2)}) collective-permute-start(bf16[32,512]{1,0:T(8,128)(2,1)S(1)} %get-tuple-element.17), channel_id=1, source_target_pairs={{0,224},{32,0},{64,32},{96,64},{128,96},{160,128},{192,160},{224,1... | collective-permute-start | bytes 98312 | tf_op jit(solution)/shard_map/ppermute | solution.py:341

commit v9 on v8

--- a/solution.py
+++ b/solution.py
@@ -301,16 +301,14 @@
     def send(k):
         return pltpu.make_async_copy(held.at[k], out.at[k], outs.at[k])
 
+    pick[...] = order()
     for k in range(K):
         masked = masked_of(grad[k], counts[k])
         near[k] = matmul(masked, merged[:, k].reshape(D, D), ((1,), (1,))).astype(BF16)
-        if k == 0:
-            pick[...] = order()
-        if k % 2 == 1:
-            done = matmul(near[k - 1 : k + 1].reshape(2 * M, D), pick[...], ((1,), (0,))).astype(BF16)
-            held[k - 1 : k + 1] = done.reshape(2, M, D)
-            send(k - 1).start()
-            send(k).start()
+        if k == 1 or k == 3:
+            for system in (k - 1, k):
+                held[system] = matmul(near[system], pick[...], ((1,), (0,))).astype(BF16)
+                send(system).start()
     for k in range(K):
         send(k).wait()
 

time: 84.8 us -> 84.8 us (level)
  no operation moved by 1% of the time
where the time goes in v9:
time: 84.8 us; the launch traced here: 83.5 us
  starting transfers between devices  39.3 us (46%)
  waiting for transfers between devices  25.7 us (30%)
  Pallas kernels  17 us (20%)
    ppermute x10, starting transfers between devices, along_z(): return lax.ppermute(array, 'z', [(i, (i + by) % NZ) for i in range(NZ)])  26.1 us
    ppermute x10, waiting for transfers between devices, along_z(): return lax.ppermute(array, 'z', [(i, (i + by) % NZ) for i in range(NZ)])  13.9 us
    all_to_all x2, starting transfers between devices, swap(): return lax.all_to_all(array, axes, 0, 0, tiled=True)  13.2 us
    all_to_all x2, waiting for transfers between devices, swap(): return lax.all_to_all(array, axes, 0, 0, tiled=True)  11.8 us
    pallas_call x1, Pallas kernels, outer(): pl.pallas_call(outer_kernel, in_specs=[SCALARS, WHOLE, ANY, ANY], out_spe...  4.75 us
    pallas_call x1, Pallas kernels, mix(): pl.pallas_call(mix_kernel, in_specs=[SCALARS, ANY], out_specs=[WHOLE] + [...  4.2 us
    pallas_call x1, Pallas kernels, merge(): pl.pallas_call(merge_kernel, in_specs=[ANY, ANY], out_specs=ANY, scratch_...  2.87 us
    pallas_call x1, Pallas kernels, back(): pl.pallas_call(back_kernel, in_specs=[SCALARS, WHOLE, WHOLE], out_specs=A...  2.71 us
  transfers between devices with their start and end apart: 12, of which 7 were waited for; matrix products, arithmetic and copies ran while one was open for 0% of the time, Pallas kernels for 8%

profile of v9, /device:TPU:9, one launch (start us, length us, event | category | flops | bytes accessed | tf_op | source)
XLA Modules:
  0.0 83.5 jit_solution(7429475192051257440)
XLA Ops:
  0.6 4.7 %outer.1 = bf16[32,17,16,128]{3,2,1,0:T(8,128)(2,1)} custom-call(s32[4]{0:T(128)} %counts.3, s32[4,16]{1,0:T(4,128)} %fixed.1, bf16[4,256,512]{2,1,0:T(8,128)(2,1)} %x.1, bf16[4,256,512]{2,1,0:T(8,128)(2,1)} %grad.3), custom_call_target="tpu_custom_call" | custom-call | flops 1073741824 | bytes 4194304 | tf_op jit(solution)/shard_map/outer/pallas_call | solution.py:109
  5.4 0.0 copy-start.4
  5.4 7.9 %all-to-all-start = ((bf16[32,17,16,128]{3,2,1,0:T(8,128)(2,1)}), bf16[32,17,16,128]{3,2,1,0:T(8,128)(2,1)}, u32[]{:S(2)}, u32[]{:S(2)}) async-start(bf16[32,17,16,128]{3,2,1,0:T(8,128)(2,1)} %outer.1), calls=%async_computation | async-start | bytes 4456448 | tf_op jit(solution)/shard_map/all_to_all | solution.py:335
  13.3 0.0 copy-done.4
  13.3 7.0 %collective-permute-start = (bf16[32,512]{1,0:T(8,128)(2,1)S(1)}, bf16[32,512]{1,0:T(8,128)(2,1)S(1)}, u32[]{:S(2)}, u32[]{:S(2)}) collective-permute-start(bf16[32,512]{1,0:T(8,128)(2,1)S(1)} %reshape.11), channel_id=1, source_target_pairs={{0,128},{32,160},{64,192},{96,224},{128,0},{160,32},{192,64},{224,... | collective-permute-start | bytes 98312 | tf_op jit(solution)/shard_map/ppermute | solution.py:339
  20.3 1.7 %collective-permute-done = bf16[32,512]{1,0:T(8,128)(2,1)S(1)} collective-permute-done((bf16[32,512]{1,0:T(8,128)(2,1)S(1)}, bf16[32,512]{1,0:T(8,128)(2,1)S(1)}, u32[]{:S(2)}, u32[]{:S(2)}) %collective-permute-start) | collective-permute-done | bytes 32800 | tf_op jit(solution)/shard_map/ppermute | solution.py:339
  22.0 1.0 %collective-permute-start.1 = (bf16[64,512]{1,0:T(8,128)(2,1)S(1)}, bf16[64,512]{1,0:T(8,128)(2,1)S(1)}, u32[]{:S(2)}, u32[]{:S(2)}) collective-permute-start(bf16[64,512]{1,0:T(8,128)(2,1)S(1)} %pad_maximum_fusion), channel_id=1, source_target_pairs={{0,64},{32,96},{64,128},{96,160},{128,192},{160,224},{192,0},{224,... | collective-permute-start | bytes 196616 | tf_op jit(solution)/shard_map/ppermute | solution.py:339
  23.1 4.8 %collective-permute-done.1 = bf16[64,512]{1,0:T(8,128)(2,1)S(1)} collective-permute-done((bf16[64,512]{1,0:T(8,128)(2,1)S(1)}, bf16[64,512]{1,0:T(8,128)(2,1)S(1)}, u32[]{:S(2)}, u32[]{:S(2)}) %collective-permute-start.1) | collective-permute-done | bytes 65568 | tf_op jit(solution)/shard_map/ppermute | solution.py:339
  27.9 0.0 copy-start.2
  27.9 1.5 %collective-permute-start.2 = (bf16[128,512]{1,0:T(8,128)(2,1)S(1)}, bf16[128,512]{1,0:T(8,128)(2,1)S(1)}, u32[]{:S(2)}, u32[]{:S(2)}) collective-permute-start(bf16[128,512]{1,0:T(8,128)(2,1)S(1)} %constant_dynamic-update-slice_fusion.near), channel_id=1, source_target_pairs={{0,32},{32,64},{64,96},{96,128},{128,160},{160,192},{192,224},{224... | collective-permute-start | bytes 393224 | tf_op jit(solution)/shard_map/ppermute | solution.py:339
  29.4 4.3 %collective-permute-done.2.far = bf16[128,512]{1,0:T(8,128)(2,1)S(1)} collective-permute-done((bf16[128,512]{1,0:T(8,128)(2,1)S(1)}, bf16[128,512]{1,0:T(8,128)(2,1)S(1)}, u32[]{:S(2)}, u32[]{:S(2)}) %collective-permute-start.2) | collective-permute-done | bytes 131104 | tf_op jit(solution)/shard_map/ppermute | solution.py:339
  33.7 0.0 copy-start.3
  33.7 0.0 copy-done.2
  33.7 0.6 copy-done.3
  34.4 1.8 %stack.1.rows = bf16[2,256,512]{2,1,0:T(8,128)(2,1)} custom-call(s32[1]{0:T(128)} %bitcast.z, bf16[128,512]{1,0:T(8,128)(2,1)} %copy-done.2, bf16[128,512]{1,0:T(8,128)(2,1)} %copy-done.3), custom_call_target="tpu_custom_call" | custom-call | bytes 786432 | tf_op jit(solution)/shard_map/stack/pallas_call | solution.py:158
  36.2 7.5 %all-to-all-done.message = bf16[32,17,16,128]{3,2,1,0:T(8,128)(2,1)} async-done(((bf16[32,17,16,128]{3,2,1,0:T(8,128)(2,1)}), bf16[32,17,16,128]{3,2,1,0:T(8,128)(2,1)}, u32[]{:S(2)}, u32[]{:S(2)}) %all-to-all-start) | async-done | bytes 2228256 | tf_op jit(solution)/shard_map/all_to_all | solution.py:335
  43.7 2.9 %merge.1 = bf16[32,4,16,512]{3,2,1,0:T(8,128)(2,1)} custom-call(bf16[32,17,16,128]{3,2,1,0:T(8,128)(2,1)} %all-to-all-done.message, bf16[2,256,512]{2,1,0:T(8,128)(2,1)} %stack.1.rows), custom_call_target="tpu_custom_call" | custom-call | flops 536870912 | bytes 3145728 | tf_op jit(solution)/shard_map/merge/pallas_call | solution.py:206
  46.6 5.3 %all-to-all-start.1 = ((bf16[32,4,16,512]{3,2,1,0:T(8,128)(2,1)}), bf16[32,4,16,512]{3,2,1,0:T(8,128)(2,1)S(1)}, u32[]{:S(2)}, u32[]{:S(2)}) async-start(bf16[32,4,16,512]{3,2,1,0:T(8,128)(2,1)} %merge.1), calls=%async_computation.1 | async-start | bytes 4194304 | tf_op jit(solution)/shard_map/all_to_all | solution.py:335
  51.9 0.0 copy-start
  51.9 0.0 copy-start.1
  52.0 4.2 %mix.1 = (f32[32,512]{1,0:T(8,128)S(1)}, bf16[32,512]{1,0:T(8,128)(2,1)S(1)}, bf16[32,512]{1,0:T(8,128)(2,1)S(1)}, bf16[32,512]{1,0:T(8,128)(2,1)S(1)}, bf16[32,...) custom-call(s32[1]{0:T(128)} %bitcast.z, ...), custom_call_target="tpu_custom_call" | custom-call | flops 1073741824 | bytes 3145728 | tf_op jit(solution)/shard_map/mix/pallas_call | solution.py:262
  56.2 1.7 %collective-permute-start.3 = (bf16[32,512]{1,0:T(8,128)(2,1)S(1)}, bf16[32,512]{1,0:T(8,128)(2,1)S(1)}, u32[]{:S(2)}, u32[]{:S(2)}) collective-permute-start(bf16[32,512]{1,0:T(8,128)(2,1)S(1)} %get-tuple-element.11), channel_id=1, source_target_pairs={{0,32},{32,64},{64,96},{96,128},{128,160},{160,192},{192,224},{224... | collective-permute-start | bytes 98312 | tf_op jit(solution)/shard_map/ppermute | solution.py:339
  57.9 3.0 %collective-permute-start.4 = (bf16[32,512]{1,0:T(8,128)(2,1)S(1)}, bf16[32,512]{1,0:T(8,128)(2,1)S(1)}, u32[]{:S(2)}, u32[]{:S(2)}) collective-permute-start(bf16[32,512]{1,0:T(8,128)(2,1)S(1)} %get-tuple-element.12), channel_id=1, source_target_pairs={{0,64},{32,96},{64,128},{96,160},{128,192},{160,224},{192,0},{224,... | collective-permute-start | bytes 98312 | tf_op jit(solution)/shard_map/ppermute | solution.py:339
  60.9 3.8 %collective-permute-start.5 = (bf16[32,512]{1,0:T(8,128)(2,1)S(1)}, bf16[32,512]{1,0:T(8,128)(2,1)S(1)}, u32[]{:S(2)}, u32[]{:S(2)}) collective-permute-start(bf16[32,512]{1,0:T(8,128)(2,1)S(1)} %get-tuple-element.13), channel_id=1, source_target_pairs={{0,96},{32,128},{64,160},{96,192},{128,224},{160,0},{192,32},{224,... | collective-permute-start | bytes 98312 | tf_op jit(solution)/shard_map/ppermute | solution.py:339
  64.6 0.4 collective-permute-start.6
  65.1 4.5 %collective-permute-start.7 = (bf16[32,512]{1,0:T(8,128)(2,1)S(1)}, bf16[32,512]{1,0:T(8,128)(2,1)S(1)}, u32[]{:S(2)}, u32[]{:S(2)}) collective-permute-start(bf16[32,512]{1,0:T(8,128)(2,1)S(1)} %get-tuple-element.15), channel_id=1, source_target_pairs={{0,160},{32,192},{64,224},{96,0},{128,32},{160,64},{192,96},{224,1... | collective-permute-start | bytes 98312 | tf_op jit(solution)/shard_map/ppermute | solution.py:339
  69.6 0.0 collective-permute-done.3.refs_0_
  69.6 2.4 %collective-permute-start.8 = (bf16[32,512]{1,0:T(8,128)(2,1)S(1)}, bf16[32,512]{1,0:T(8,128)(2,1)S(1)}, u32[]{:S(2)}, u32[]{:S(2)}) collective-permute-start(bf16[32,512]{1,0:T(8,128)(2,1)S(1)} %get-tuple-element.16), channel_id=1, source_target_pairs={{0,192},{32,224},{64,0},{96,32},{128,64},{160,96},{192,128},{224,1... | collective-permute-start | bytes 98312 | tf_op jit(solution)/shard_map/ppermute | solution.py:339
  71.9 0.0 collective-permute-done.4.refs_1_
  71.9 0.7 collective-permute-start.9
  72.7 0.0 collective-permute-done.5.refs_2_
  72.7 0.0 collective-permute-done.6.refs_3_
  72.7 0.0 collective-permute-done.7.refs_4_
  72.7 2.4 %collective-permute-done.8.refs_5_ = bf16[32,512]{1,0:T(8,128)(2,1)S(1)} collective-permute-done((bf16[32,512]{1,0:T(8,128)(2,1)S(1)}, bf16[32,512]{1,0:T(8,128)(2,1)S(1)}, u32[]{:S(2)}, u32[]{:S(2)}) %collective-permute-start.8) | collective-permute-done | bytes 32800 | tf_op jit(solution)/shard_map/ppermute | solution.py:339
  75.1 0.7 collective-permute-done.9.refs_6_
  75.8 0.7 total.1
  76.5 4.3 %all-to-all-done.1.merged = bf16[32,4,16,512]{3,2,1,0:T(8,128)(2,1)S(1)} async-done(((bf16[32,4,16,512]{3,2,1,0:T(8,128)(2,1)}), bf16[32,4,16,512]{3,2,1,0:T(8,128)(2,1)S(1)}, u32[]{:S(2)}, u32[]{:S(2)}) %all-to-all-start.1) | async-done | bytes 2097184 | tf_op jit(solution)/shard_map/all_to_all | solution.py:335
  80.8 0.0 copy-done
  80.8 0.0 copy-done.1
  80.8 2.7 %back.1 = bf16[4,256,512]{2,1,0:T(8,128)(2,1)} custom-call(s32[4]{0:T(128)S(1)} %copy-done.1, bf16[4,256,512]{2,1,0:T(8,128)(2,1)S(1)} %copy-done, bf16[32,4,16,512]{3,2,1,0:T(8,128)(2,1)S(1)} %all-to-all-done.1.merged), custom_call_target="tpu_custom_call" | custom-call | flops 1073741824 | bytes 4194304 | tf_op jit(solution)/shard_map/back/pallas_call | solution.py:317
  (5 shorter events, 0.0 us)
Async XLA Ops:
  5.4 7.9 %copy-start.4 = (bf16[16,2,512]{2,1,0:T(2,128)(2,1)S(1)}, bf16[16,2,512]{2,1,0:T(2,128)(2,1)}, u32[]{:S(2)}) copy-start(bf16[16,2,512]{2,1,0:T(2,128)(2,1)} %param.9) | copy-start | bytes 98308
  5.4 38.3 %all-to-all-start = ((bf16[32,17,16,128]{3,2,1,0:T(8,128)(2,1)}), bf16[32,17,16,128]{3,2,1,0:T(8,128)(2,1)}, u32[]{:S(2)}, u32[]{:S(2)}) async-start(bf16[32,17,16,128]{3,2,1,0:T(8,128)(2,1)} %outer.1), calls=%async_computation | async-start | bytes 4456448 | tf_op jit(solution)/shard_map/all_to_all | solution.py:335
  13.3 8.7 %collective-permute-start = (bf16[32,512]{1,0:T(8,128)(2,1)S(1)}, bf16[32,512]{1,0:T(8,128)(2,1)S(1)}, u32[]{:S(2)}, u32[]{:S(2)}) collective-permute-start(bf16[32,512]{1,0:T(8,128)(2,1)S(1)} %reshape.11), channel_id=1, source_target_pairs={{0,128},{32,160},{64,192},{96,224},{128,0},{160,32},{192,64},{224,... | collective-permute-start | bytes 98312 | tf_op jit(solution)/shard_map/ppermute | solution.py:339
  22.0 5.8 %collective-permute-start.1 = (bf16[64,512]{1,0:T(8,128)(2,1)S(1)}, bf16[64,512]{1,0:T(8,128)(2,1)S(1)}, u32[]{:S(2)}, u32[]{:S(2)}) collective-permute-start(bf16[64,512]{1,0:T(8,128)(2,1)S(1)} %pad_maximum_fusion), channel_id=1, source_target_pairs={{0,64},{32,96},{64,128},{96,160},{128,192},{160,224},{192,0},{224,... | collective-permute-start | bytes 196616 | tf_op jit(solution)/shard_map/ppermute | solution.py:339
  27.9 5.8 %copy-start.2 = (bf16[128,512]{1,0:T(8,128)(2,1)}, bf16[128,512]{1,0:T(8,128)(2,1)S(1)}, u32[]{:S(2)}) copy-start(bf16[128,512]{1,0:T(8,128)(2,1)S(1)} %constant_dynamic-update-slice_fusion.near) | copy-start | bytes 393220
  27.9 5.8 %collective-permute-start.2 = (bf16[128,512]{1,0:T(8,128)(2,1)S(1)}, bf16[128,512]{1,0:T(8,128)(2,1)S(1)}, u32[]{:S(2)}, u32[]{:S(2)}) collective-permute-start(bf16[128,512]{1,0:T(8,128)(2,1)S(1)} %constant_dynamic-update-slice_fusion.near), channel_id=1, source_target_pairs={{0,32},{32,64},{64,96},{96,128},{128,160},{160,192},{192,224},{224... | collective-permute-start | bytes 393224 | tf_op jit(solution)/shard_map/ppermute | solution.py:339
  33.7 0.7 copy-start.3
  46.6 34.2 %all-to-all-start.1 = ((bf16[32,4,16,512]{3,2,1,0:T(8,128)(2,1)}), bf16[32,4,16,512]{3,2,1,0:T(8,128)(2,1)S(1)}, u32[]{:S(2)}, u32[]{:S(2)}) async-start(bf16[32,4,16,512]{3,2,1,0:T(8,128)(2,1)} %merge.1), calls=%async_computation.1 | async-start | bytes 4194304 | tf_op jit(solution)/shard_map/all_to_all | solution.py:335
  51.9 28.8 %copy-start = (bf16[4,256,512]{2,1,0:T(8,128)(2,1)S(1)}, bf16[4,256,512]{2,1,0:T(8,128)(2,1)}, u32[]{:S(2)}) copy-start(bf16[4,256,512]{2,1,0:T(8,128)(2,1)} %grad.3) | copy-start | bytes 3145732
  51.9 28.8 %copy-start.1 = (s32[4]{0:T(128)S(1)}, s32[4]{0:T(128)}, u32[]{:S(2)}) copy-start(s32[4]{0:T(128)} %counts.3) | copy-start | bytes 52
  56.2 13.4 %collective-permute-start.3 = (bf16[32,512]{1,0:T(8,128)(2,1)S(1)}, bf16[32,512]{1,0:T(8,128)(2,1)S(1)}, u32[]{:S(2)}, u32[]{:S(2)}) collective-permute-start(bf16[32,512]{1,0:T(8,128)(2,1)S(1)} %get-tuple-element.11), channel_id=1, source_target_pairs={{0,32},{32,64},{64,96},{96,128},{128,160},{160,192},{192,224},{224... | collective-permute-start | bytes 98312 | tf_op jit(solution)/shard_map/ppermute | solution.py:339
  57.9 14.1 %collective-permute-start.4 = (bf16[32,512]{1,0:T(8,128)(2,1)S(1)}, bf16[32,512]{1,0:T(8,128)(2,1)S(1)}, u32[]{:S(2)}, u32[]{:S(2)}) collective-permute-start(bf16[32,512]{1,0:T(8,128)(2,1)S(1)} %get-tuple-element.12), channel_id=1, source_target_pairs={{0,64},{32,96},{64,128},{96,160},{128,192},{160,224},{192,0},{224,... | collective-permute-start | bytes 98312 | tf_op jit(solution)/shard_map/ppermute | solution.py:339
  60.9 11.8 %collective-permute-start.5 = (bf16[32,512]{1,0:T(8,128)(2,1)S(1)}, bf16[32,512]{1,0:T(8,128)(2,1)S(1)}, u32[]{:S(2)}, u32[]{:S(2)}) collective-permute-start(bf16[32,512]{1,0:T(8,128)(2,1)S(1)} %get-tuple-element.13), channel_id=1, source_target_pairs={{0,96},{32,128},{64,160},{96,192},{128,224},{160,0},{192,32},{224,... | collective-permute-start | bytes 98312 | tf_op jit(solution)/shard_map/ppermute | solution.py:339
  64.6 8.0 %collective-permute-start.6 = (bf16[32,512]{1,0:T(8,128)(2,1)S(1)}, bf16[32,512]{1,0:T(8,128)(2,1)S(1)}, u32[]{:S(2)}, u32[]{:S(2)}) collective-permute-start(bf16[32,512]{1,0:T(8,128)(2,1)S(1)} %get-tuple-element.14), channel_id=1, source_target_pairs={{0,128},{32,160},{64,192},{96,224},{128,0},{160,32},{192,64},{224,... | collective-permute-start | bytes 98312 | tf_op jit(solution)/shard_map/ppermute | solution.py:339
  65.1 7.6 %collective-permute-start.7 = (bf16[32,512]{1,0:T(8,128)(2,1)S(1)}, bf16[32,512]{1,0:T(8,128)(2,1)S(1)}, u32[]{:S(2)}, u32[]{:S(2)}) collective-permute-start(bf16[32,512]{1,0:T(8,128)(2,1)S(1)} %get-tuple-element.15), channel_id=1, source_target_pairs={{0,160},{32,192},{64,224},{96,0},{128,32},{160,64},{192,96},{224,1... | collective-permute-start | bytes 98312 | tf_op jit(solution)/shard_map/ppermute | solution.py:339
  69.6 5.5 %collective-permute-start.8 = (bf16[32,512]{1,0:T(8,128)(2,1)S(1)}, bf16[32,512]{1,0:T(8,128)(2,1)S(1)}, u32[]{:S(2)}, u32[]{:S(2)}) collective-permute-start(bf16[32,512]{1,0:T(8,128)(2,1)S(1)} %get-tuple-element.16), channel_id=1, source_target_pairs={{0,192},{32,224},{64,0},{96,32},{128,64},{160,96},{192,128},{224,1... | collective-permute-start | bytes 98312 | tf_op jit(solution)/shard_map/ppermute | solution.py:339
  71.9 3.8 %collective-permute-start.9 = (bf16[32,512]{1,0:T(8,128)(2,1)S(1)}, bf16[32,512]{1,0:T(8,128)(2,1)S(1)}, u32[]{:S(2)}, u32[]{:S(2)}) collective-permute-start(bf16[32,512]{1,0:T(8,128)(2,1)S(1)} %get-tuple-element.17), channel_id=1, source_target_pairs={{0,224},{32,0},{64,32},{96,64},{128,96},{160,128},{192,160},{224,1... | collective-permute-start | bytes 98312 | tf_op jit(solution)/shard_map/ppermute | solution.py:339

commit v10 on v9

--- a/solution.py
+++ b/solution.py
@@ -172,14 +172,15 @@
 
 def merge_kernel(message, rows, out, cards, weights, wide, held, ins, outs):
     fetch_cards = pltpu.make_async_copy(message.at[:, pl.ds(CARD, 1)], cards, ins.at[0])
-    fetch_rows = pltpu.make_async_copy(rows, weights, ins.at[1])
+    fetch_rows = [pltpu.make_async_copy(rows.at[h], weights.at[h], ins.at[1 + h]) for h in range(2)]
 
     def send(n):
         place = pl.ds(n * GROUP, GROUP)
         return pltpu.make_async_copy(held.at[place], out.at[place], outs.at[n])
 
     fetch_cards.start()
-    fetch_rows.start()
+    for copy in fetch_rows:
+        copy.start()
     system = row_of((NG * K, 1), 0)
     pick = one_hot(((system >> 2) << 4) + (system & (K - 1)) == row_of((1, NG * PER), 1))
     col = row_of((1, WIDTH), 1)
@@ -190,7 +191,8 @@
     fetch_cards.wait()
     values = matmul(pick, cards[...].reshape(NG * PER, LANES), ((1,), (0,))).astype(BF16)
     wide[...] = matmul(values, widen, ((1,), (0,)))
-    fetch_rows.wait()
+    for copy in fetch_rows:
+        copy.wait()
     for n in range(GROUPS):
         tall = jnp.where(same[None], wide[n * STEP : (n + 1) * STEP][:, None, :], 0.0)
         factor = tall.reshape(STEP * HALF, WIDTH).astype(BF16)
@@ -212,7 +214,7 @@
             pltpu.VMEM((2, WIDTH, D), BF16),
             pltpu.VMEM((NG * K, WIDTH), F32),
             pltpu.VMEM((NG, K, PER, D), BF16),
-            pltpu.SemaphoreType.DMA((2,)),
+            pltpu.SemaphoreType.DMA((3,)),
             pltpu.SemaphoreType.DMA((GROUPS,)),
         ],
         out_shape=jax.ShapeDtypeStruct((NG, K, PER, D), BF16),

time: 84.8 us -> 84.8 us (level)
  no operation moved by 1% of the time
where the time goes in v10:
time: 84.8 us; the launch traced here: 83.5 us
  starting transfers between devices  39.3 us (46%)
  waiting for transfers between devices  25.7 us (30%)
  Pallas kernels  17 us (20%)
    ppermute x10, starting transfers between devices, along_z(): return lax.ppermute(array, 'z', [(i, (i + by) % NZ) for i in range(NZ)])  26 us
    ppermute x10, waiting for transfers between devices, along_z(): return lax.ppermute(array, 'z', [(i, (i + by) % NZ) for i in range(NZ)])  13.9 us
    all_to_all x2, starting transfers between devices, swap(): return lax.all_to_all(array, axes, 0, 0, tiled=True)  13.2 us
    all_to_all x2, waiting for transfers between devices, swap(): return lax.all_to_all(array, axes, 0, 0, tiled=True)  11.8 us
    pallas_call x1, Pallas kernels, outer(): pl.pallas_call(outer_kernel, in_specs=[SCALARS, WHOLE, ANY, ANY], out_spe...  4.75 us
    pallas_call x1, Pallas kernels, mix(): pl.pallas_call(mix_kernel, in_specs=[SCALARS, ANY], out_specs=[WHOLE] + [...  4.21 us
    pallas_call x1, Pallas kernels, merge(): pl.pallas_call(merge_kernel, in_specs=[ANY, ANY], out_specs=ANY, scratch_...  2.88 us
    pallas_call x1, Pallas kernels, back(): pl.pallas_call(back_kernel, in_specs=[SCALARS, WHOLE, WHOLE], out_specs=A...  2.72 us
  transfers between devices with their start and end apart: 12, of which 7 were waited for; matrix products, arithmetic and copies ran while one was open for 0% of the time, Pallas kernels for 8%

profile of v10, /device:TPU:9, one launch (start us, length us, event | category | flops | bytes accessed | tf_op | source)
XLA Modules:
  0.0 83.5 jit_solution(2660930692319518332)
XLA Ops:
  0.6 4.7 %outer.1 = bf16[32,17,16,128]{3,2,1,0:T(8,128)(2,1)} custom-call(s32[4]{0:T(128)} %counts.3, s32[4,16]{1,0:T(4,128)} %fixed.1, bf16[4,256,512]{2,1,0:T(8,128)(2,1)} %x.1, bf16[4,256,512]{2,1,0:T(8,128)(2,1)} %grad.3), custom_call_target="tpu_custom_call" | custom-call | flops 1073741824 | bytes 4194304 | tf_op jit(solution)/shard_map/outer/pallas_call | solution.py:109
  5.4 0.0 copy-start.4
  5.4 7.9 %all-to-all-start = ((bf16[32,17,16,128]{3,2,1,0:T(8,128)(2,1)}), bf16[32,17,16,128]{3,2,1,0:T(8,128)(2,1)}, u32[]{:S(2)}, u32[]{:S(2)}) async-start(bf16[32,17,16,128]{3,2,1,0:T(8,128)(2,1)} %outer.1), calls=%async_computation | async-start | bytes 4456448 | tf_op jit(solution)/shard_map/all_to_all | solution.py:337
  13.3 0.0 copy-done.4
  13.3 7.0 %collective-permute-start = (bf16[32,512]{1,0:T(8,128)(2,1)S(1)}, bf16[32,512]{1,0:T(8,128)(2,1)S(1)}, u32[]{:S(2)}, u32[]{:S(2)}) collective-permute-start(bf16[32,512]{1,0:T(8,128)(2,1)S(1)} %reshape.11), channel_id=1, source_target_pairs={{0,128},{32,160},{64,192},{96,224},{128,0},{160,32},{192,64},{224,... | collective-permute-start | bytes 98312 | tf_op jit(solution)/shard_map/ppermute | solution.py:341
  20.3 1.7 %collective-permute-done = bf16[32,512]{1,0:T(8,128)(2,1)S(1)} collective-permute-done((bf16[32,512]{1,0:T(8,128)(2,1)S(1)}, bf16[32,512]{1,0:T(8,128)(2,1)S(1)}, u32[]{:S(2)}, u32[]{:S(2)}) %collective-permute-start) | collective-permute-done | bytes 32800 | tf_op jit(solution)/shard_map/ppermute | solution.py:341
  22.0 1.0 %collective-permute-start.1 = (bf16[64,512]{1,0:T(8,128)(2,1)S(1)}, bf16[64,512]{1,0:T(8,128)(2,1)S(1)}, u32[]{:S(2)}, u32[]{:S(2)}) collective-permute-start(bf16[64,512]{1,0:T(8,128)(2,1)S(1)} %pad_maximum_fusion), channel_id=1, source_target_pairs={{0,64},{32,96},{64,128},{96,160},{128,192},{160,224},{192,0},{224,... | collective-permute-start | bytes 196616 | tf_op jit(solution)/shard_map/ppermute | solution.py:341
  23.1 4.8 %collective-permute-done.1 = bf16[64,512]{1,0:T(8,128)(2,1)S(1)} collective-permute-done((bf16[64,512]{1,0:T(8,128)(2,1)S(1)}, bf16[64,512]{1,0:T(8,128)(2,1)S(1)}, u32[]{:S(2)}, u32[]{:S(2)}) %collective-permute-start.1) | collective-permute-done | bytes 65568 | tf_op jit(solution)/shard_map/ppermute | solution.py:341
  27.9 0.0 copy-start.2
  27.9 1.5 %collective-permute-start.2 = (bf16[128,512]{1,0:T(8,128)(2,1)S(1)}, bf16[128,512]{1,0:T(8,128)(2,1)S(1)}, u32[]{:S(2)}, u32[]{:S(2)}) collective-permute-start(bf16[128,512]{1,0:T(8,128)(2,1)S(1)} %constant_dynamic-update-slice_fusion.near), channel_id=1, source_target_pairs={{0,32},{32,64},{64,96},{96,128},{128,160},{160,192},{192,224},{224... | collective-permute-start | bytes 393224 | tf_op jit(solution)/shard_map/ppermute | solution.py:341
  29.4 4.3 %collective-permute-done.2.far = bf16[128,512]{1,0:T(8,128)(2,1)S(1)} collective-permute-done((bf16[128,512]{1,0:T(8,128)(2,1)S(1)}, bf16[128,512]{1,0:T(8,128)(2,1)S(1)}, u32[]{:S(2)}, u32[]{:S(2)}) %collective-permute-start.2) | collective-permute-done | bytes 131104 | tf_op jit(solution)/shard_map/ppermute | solution.py:341
  33.7 0.0 copy-start.3
  33.7 0.0 copy-done.2
  33.7 0.6 copy-done.3
  34.4 1.8 %stack.1.rows = bf16[2,256,512]{2,1,0:T(8,128)(2,1)} custom-call(s32[1]{0:T(128)} %bitcast.z, bf16[128,512]{1,0:T(8,128)(2,1)} %copy-done.2, bf16[128,512]{1,0:T(8,128)(2,1)} %copy-done.3), custom_call_target="tpu_custom_call" | custom-call | bytes 786432 | tf_op jit(solution)/shard_map/stack/pallas_call | solution.py:158
  36.2 7.5 %all-to-all-done.message = bf16[32,17,16,128]{3,2,1,0:T(8,128)(2,1)} async-done(((bf16[32,17,16,128]{3,2,1,0:T(8,128)(2,1)}), bf16[32,17,16,128]{3,2,1,0:T(8,128)(2,1)}, u32[]{:S(2)}, u32[]{:S(2)}) %all-to-all-start) | async-done | bytes 2228256 | tf_op jit(solution)/shard_map/all_to_all | solution.py:337
  43.7 2.9 %merge.1 = bf16[32,4,16,512]{3,2,1,0:T(8,128)(2,1)} custom-call(bf16[32,17,16,128]{3,2,1,0:T(8,128)(2,1)} %all-to-all-done.message, bf16[2,256,512]{2,1,0:T(8,128)(2,1)} %stack.1.rows), custom_call_target="tpu_custom_call" | custom-call | flops 536870912 | bytes 3145728 | tf_op jit(solution)/shard_map/merge/pallas_call | solution.py:208
  46.6 5.3 %all-to-all-start.1 = ((bf16[32,4,16,512]{3,2,1,0:T(8,128)(2,1)}), bf16[32,4,16,512]{3,2,1,0:T(8,128)(2,1)S(1)}, u32[]{:S(2)}, u32[]{:S(2)}) async-start(bf16[32,4,16,512]{3,2,1,0:T(8,128)(2,1)} %merge.1), calls=%async_computation.1 | async-start | bytes 4194304 | tf_op jit(solution)/shard_map/all_to_all | solution.py:337
  51.9 0.0 copy-start
  52.0 0.0 copy-start.1
  52.0 4.2 %mix.1 = (f32[32,512]{1,0:T(8,128)S(1)}, bf16[32,512]{1,0:T(8,128)(2,1)S(1)}, bf16[32,512]{1,0:T(8,128)(2,1)S(1)}, bf16[32,512]{1,0:T(8,128)(2,1)S(1)}, bf16[32,...) custom-call(s32[1]{0:T(128)} %bitcast.z, ...), custom_call_target="tpu_custom_call" | custom-call | flops 1073741824 | bytes 3145728 | tf_op jit(solution)/shard_map/mix/pallas_call | solution.py:264
  56.2 1.7 %collective-permute-start.3 = (bf16[32,512]{1,0:T(8,128)(2,1)S(1)}, bf16[32,512]{1,0:T(8,128)(2,1)S(1)}, u32[]{:S(2)}, u32[]{:S(2)}) collective-permute-start(bf16[32,512]{1,0:T(8,128)(2,1)S(1)} %get-tuple-element.11), channel_id=1, source_target_pairs={{0,32},{32,64},{64,96},{96,128},{128,160},{160,192},{192,224},{224... | collective-permute-start | bytes 98312 | tf_op jit(solution)/shard_map/ppermute | solution.py:341
  57.9 3.0 %collective-permute-start.4 = (bf16[32,512]{1,0:T(8,128)(2,1)S(1)}, bf16[32,512]{1,0:T(8,128)(2,1)S(1)}, u32[]{:S(2)}, u32[]{:S(2)}) collective-permute-start(bf16[32,512]{1,0:T(8,128)(2,1)S(1)} %get-tuple-element.12), channel_id=1, source_target_pairs={{0,64},{32,96},{64,128},{96,160},{128,192},{160,224},{192,0},{224,... | collective-permute-start | bytes 98312 | tf_op jit(solution)/shard_map/ppermute | solution.py:341
  60.9 3.8 %collective-permute-start.5 = (bf16[32,512]{1,0:T(8,128)(2,1)S(1)}, bf16[32,512]{1,0:T(8,128)(2,1)S(1)}, u32[]{:S(2)}, u32[]{:S(2)}) collective-permute-start(bf16[32,512]{1,0:T(8,128)(2,1)S(1)} %get-tuple-element.13), channel_id=1, source_target_pairs={{0,96},{32,128},{64,160},{96,192},{128,224},{160,0},{192,32},{224,... | collective-permute-start | bytes 98312 | tf_op jit(solution)/shard_map/ppermute | solution.py:341
  64.7 0.4 collective-permute-start.6
  65.1 4.5 %collective-permute-start.7 = (bf16[32,512]{1,0:T(8,128)(2,1)S(1)}, bf16[32,512]{1,0:T(8,128)(2,1)S(1)}, u32[]{:S(2)}, u32[]{:S(2)}) collective-permute-start(bf16[32,512]{1,0:T(8,128)(2,1)S(1)} %get-tuple-element.15), channel_id=1, source_target_pairs={{0,160},{32,192},{64,224},{96,0},{128,32},{160,64},{192,96},{224,1... | collective-permute-start | bytes 98312 | tf_op jit(solution)/shard_map/ppermute | solution.py:341
  69.6 0.0 collective-permute-done.3.refs_0_
  69.6 2.4 %collective-permute-start.8 = (bf16[32,512]{1,0:T(8,128)(2,1)S(1)}, bf16[32,512]{1,0:T(8,128)(2,1)S(1)}, u32[]{:S(2)}, u32[]{:S(2)}) collective-permute-start(bf16[32,512]{1,0:T(8,128)(2,1)S(1)} %get-tuple-element.16), channel_id=1, source_target_pairs={{0,192},{32,224},{64,0},{96,32},{128,64},{160,96},{192,128},{224,1... | collective-permute-start | bytes 98312 | tf_op jit(solution)/shard_map/ppermute | solution.py:341
  72.0 0.0 collective-permute-done.4.refs_1_
  72.0 0.7 collective-permute-start.9
  72.7 0.0 collective-permute-done.5.refs_2_
  72.7 0.0 collective-permute-done.6.refs_3_
  72.7 0.0 collective-permute-done.7.refs_4_
  72.7 2.4 %collective-permute-done.8.refs_5_ = bf16[32,512]{1,0:T(8,128)(2,1)S(1)} collective-permute-done((bf16[32,512]{1,0:T(8,128)(2,1)S(1)}, bf16[32,512]{1,0:T(8,128)(2,1)S(1)}, u32[]{:S(2)}, u32[]{:S(2)}) %collective-permute-start.8) | collective-permute-done | bytes 32800 | tf_op jit(solution)/shard_map/ppermute | solution.py:341
  75.1 0.7 collective-permute-done.9.refs_6_
  75.8 0.7 total.1
  76.5 4.3 %all-to-all-done.1.merged = bf16[32,4,16,512]{3,2,1,0:T(8,128)(2,1)S(1)} async-done(((bf16[32,4,16,512]{3,2,1,0:T(8,128)(2,1)}), bf16[32,4,16,512]{3,2,1,0:T(8,128)(2,1)S(1)}, u32[]{:S(2)}, u32[]{:S(2)}) %all-to-all-start.1) | async-done | bytes 2097184 | tf_op jit(solution)/shard_map/all_to_all | solution.py:337
  80.8 0.0 copy-done
  80.8 0.0 copy-done.1
  80.8 2.7 %back.1 = bf16[4,256,512]{2,1,0:T(8,128)(2,1)} custom-call(s32[4]{0:T(128)S(1)} %copy-done.1, bf16[4,256,512]{2,1,0:T(8,128)(2,1)S(1)} %copy-done, bf16[32,4,16,512]{3,2,1,0:T(8,128)(2,1)S(1)} %all-to-all-done.1.merged), custom_call_target="tpu_custom_call" | custom-call | flops 1073741824 | bytes 4194304 | tf_op jit(solution)/shard_map/back/pallas_call | solution.py:319
  (5 shorter events, 0.0 us)
Async XLA Ops:
  5.4 7.9 %copy-start.4 = (bf16[16,2,512]{2,1,0:T(2,128)(2,1)S(1)}, bf16[16,2,512]{2,1,0:T(2,128)(2,1)}, u32[]{:S(2)}) copy-start(bf16[16,2,512]{2,1,0:T(2,128)(2,1)} %param.9) | copy-start | bytes 98308
  5.4 38.3 %all-to-all-start = ((bf16[32,17,16,128]{3,2,1,0:T(8,128)(2,1)}), bf16[32,17,16,128]{3,2,1,0:T(8,128)(2,1)}, u32[]{:S(2)}, u32[]{:S(2)}) async-start(bf16[32,17,16,128]{3,2,1,0:T(8,128)(2,1)} %outer.1), calls=%async_computation | async-start | bytes 4456448 | tf_op jit(solution)/shard_map/all_to_all | solution.py:337
  13.3 8.7 %collective-permute-start = (bf16[32,512]{1,0:T(8,128)(2,1)S(1)}, bf16[32,512]{1,0:T(8,128)(2,1)S(1)}, u32[]{:S(2)}, u32[]{:S(2)}) collective-permute-start(bf16[32,512]{1,0:T(8,128)(2,1)S(1)} %reshape.11), channel_id=1, source_target_pairs={{0,128},{32,160},{64,192},{96,224},{128,0},{160,32},{192,64},{224,... | collective-permute-start | bytes 98312 | tf_op jit(solution)/shard_map/ppermute | solution.py:341
  22.0 5.8 %collective-permute-start.1 = (bf16[64,512]{1,0:T(8,128)(2,1)S(1)}, bf16[64,512]{1,0:T(8,128)(2,1)S(1)}, u32[]{:S(2)}, u32[]{:S(2)}) collective-permute-start(bf16[64,512]{1,0:T(8,128)(2,1)S(1)} %pad_maximum_fusion), channel_id=1, source_target_pairs={{0,64},{32,96},{64,128},{96,160},{128,192},{160,224},{192,0},{224,... | collective-permute-start | bytes 196616 | tf_op jit(solution)/shard_map/ppermute | solution.py:341
  27.9 5.8 %copy-start.2 = (bf16[128,512]{1,0:T(8,128)(2,1)}, bf16[128,512]{1,0:T(8,128)(2,1)S(1)}, u32[]{:S(2)}) copy-start(bf16[128,512]{1,0:T(8,128)(2,1)S(1)} %constant_dynamic-update-slice_fusion.near) | copy-start | bytes 393220
  27.9 5.8 %collective-permute-start.2 = (bf16[128,512]{1,0:T(8,128)(2,1)S(1)}, bf16[128,512]{1,0:T(8,128)(2,1)S(1)}, u32[]{:S(2)}, u32[]{:S(2)}) collective-permute-start(bf16[128,512]{1,0:T(8,128)(2,1)S(1)} %constant_dynamic-update-slice_fusion.near), channel_id=1, source_target_pairs={{0,32},{32,64},{64,96},{96,128},{128,160},{160,192},{192,224},{224... | collective-permute-start | bytes 393224 | tf_op jit(solution)/shard_map/ppermute | solution.py:341
  33.7 0.7 copy-start.3
  46.6 34.2 %all-to-all-start.1 = ((bf16[32,4,16,512]{3,2,1,0:T(8,128)(2,1)}), bf16[32,4,16,512]{3,2,1,0:T(8,128)(2,1)S(1)}, u32[]{:S(2)}, u32[]{:S(2)}) async-start(bf16[32,4,16,512]{3,2,1,0:T(8,128)(2,1)} %merge.1), calls=%async_computation.1 | async-start | bytes 4194304 | tf_op jit(solution)/shard_map/all_to_all | solution.py:337
  51.9 28.8 %copy-start = (bf16[4,256,512]{2,1,0:T(8,128)(2,1)S(1)}, bf16[4,256,512]{2,1,0:T(8,128)(2,1)}, u32[]{:S(2)}) copy-start(bf16[4,256,512]{2,1,0:T(8,128)(2,1)} %grad.3) | copy-start | bytes 3145732
  52.0 28.8 %copy-start.1 = (s32[4]{0:T(128)S(1)}, s32[4]{0:T(128)}, u32[]{:S(2)}) copy-start(s32[4]{0:T(128)} %counts.3) | copy-start | bytes 52
  56.2 13.4 %collective-permute-start.3 = (bf16[32,512]{1,0:T(8,128)(2,1)S(1)}, bf16[32,512]{1,0:T(8,128)(2,1)S(1)}, u32[]{:S(2)}, u32[]{:S(2)}) collective-permute-start(bf16[32,512]{1,0:T(8,128)(2,1)S(1)} %get-tuple-element.11), channel_id=1, source_target_pairs={{0,32},{32,64},{64,96},{96,128},{128,160},{160,192},{192,224},{224... | collective-permute-start | bytes 98312 | tf_op jit(solution)/shard_map/ppermute | solution.py:341
  57.9 14.1 %collective-permute-start.4 = (bf16[32,512]{1,0:T(8,128)(2,1)S(1)}, bf16[32,512]{1,0:T(8,128)(2,1)S(1)}, u32[]{:S(2)}, u32[]{:S(2)}) collective-permute-start(bf16[32,512]{1,0:T(8,128)(2,1)S(1)} %get-tuple-element.12), channel_id=1, source_target_pairs={{0,64},{32,96},{64,128},{96,160},{128,192},{160,224},{192,0},{224,... | collective-permute-start | bytes 98312 | tf_op jit(solution)/shard_map/ppermute | solution.py:341
  60.9 11.8 %collective-permute-start.5 = (bf16[32,512]{1,0:T(8,128)(2,1)S(1)}, bf16[32,512]{1,0:T(8,128)(2,1)S(1)}, u32[]{:S(2)}, u32[]{:S(2)}) collective-permute-start(bf16[32,512]{1,0:T(8,128)(2,1)S(1)} %get-tuple-element.13), channel_id=1, source_target_pairs={{0,96},{32,128},{64,160},{96,192},{128,224},{160,0},{192,32},{224,... | collective-permute-start | bytes 98312 | tf_op jit(solution)/shard_map/ppermute | solution.py:341
  64.7 8.0 %collective-permute-start.6 = (bf16[32,512]{1,0:T(8,128)(2,1)S(1)}, bf16[32,512]{1,0:T(8,128)(2,1)S(1)}, u32[]{:S(2)}, u32[]{:S(2)}) collective-permute-start(bf16[32,512]{1,0:T(8,128)(2,1)S(1)} %get-tuple-element.14), channel_id=1, source_target_pairs={{0,128},{32,160},{64,192},{96,224},{128,0},{160,32},{192,64},{224,... | collective-permute-start | bytes 98312 | tf_op jit(solution)/shard_map/ppermute | solution.py:341
  65.1 7.6 %collective-permute-start.7 = (bf16[32,512]{1,0:T(8,128)(2,1)S(1)}, bf16[32,512]{1,0:T(8,128)(2,1)S(1)}, u32[]{:S(2)}, u32[]{:S(2)}) collective-permute-start(bf16[32,512]{1,0:T(8,128)(2,1)S(1)} %get-tuple-element.15), channel_id=1, source_target_pairs={{0,160},{32,192},{64,224},{96,0},{128,32},{160,64},{192,96},{224,1... | collective-permute-start | bytes 98312 | tf_op jit(solution)/shard_map/ppermute | solution.py:341
  69.6 5.6 %collective-permute-start.8 = (bf16[32,512]{1,0:T(8,128)(2,1)S(1)}, bf16[32,512]{1,0:T(8,128)(2,1)S(1)}, u32[]{:S(2)}, u32[]{:S(2)}) collective-permute-start(bf16[32,512]{1,0:T(8,128)(2,1)S(1)} %get-tuple-element.16), channel_id=1, source_target_pairs={{0,192},{32,224},{64,0},{96,32},{128,64},{160,96},{192,128},{224,1... | collective-permute-start | bytes 98312 | tf_op jit(solution)/shard_map/ppermute | solution.py:341
  72.0 3.8 %collective-permute-start.9 = (bf16[32,512]{1,0:T(8,128)(2,1)S(1)}, bf16[32,512]{1,0:T(8,128)(2,1)S(1)}, u32[]{:S(2)}, u32[]{:S(2)}) collective-permute-start(bf16[32,512]{1,0:T(8,128)(2,1)S(1)} %get-tuple-element.17), channel_id=1, source_target_pairs={{0,224},{32,0},{64,32},{96,64},{128,96},{160,128},{192,160},{224,1... | collective-permute-start | bytes 98312 | tf_op jit(solution)/shard_map/ppermute | solution.py:341
